TPU v7x, 512 devices: a whole 4x4x16 slice. The times are simulated.
512 devices in a mesh: det: 32 (over y, x, core), shot: 16 (over z).
Axes of the slice: x: 4, y: 4, z: 16, core: 2. Of those that a mesh axis runs over, the one named last changes fastest.
Arguments:
- features: float32 [32768, 16384], P('det', 'shot'), may hold values from -200 to 200
- pairs: int32 [512, 2], P('det'), may hold values from 0 to 127, as said below
Outputs:
- tiles: float32 [256, 512, 256], P('shot', 'det')
Inputs may be any that keep to these rules, and one draw needn't show every extreme that they name: Row p of pairs belongs to owner o = p // 16: its first block lies in o * 4 to o * 4 + 3, and its second block differs from the first by at most 2; the pairs of one owner are distinct. Every owner but the last has the pair (o * 4 + 3, o * 4 + 5), and every owner but the first has the pair (o * 4, o * 4 - 2).
All inputs are finite; a program needn't handle non-finite values.
Results may differ from a plain program's by a relative error of at most 0.0003.
Values sent between devices are 32-bit elements; how exact they have to be, the bound alone decides.
No kernel may reach another device: no remote copies, remote signals or barrier semaphores. Data moves between devices by JAX's collectives and lax.ppermute only.
A program may use at most 128 MiB of HBM per device.

v0:
```python
import jax
import jax.numpy as jnp
from jax import lax
from jax.sharding import PartitionSpec as P

BLK = 256
REACH = 2


def extended_2(cells, sides, width):
    for axis, dim in sides:
        count = lax.axis_size(axis)
        ends = count - 1
        head = lax.slice_in_dim(cells, 0, width, axis=dim)
        tail = lax.slice_in_dim(cells, cells.shape[dim] - width, cells.shape[dim], axis=dim)
        cells = jnp.concatenate(
            [
                lax.ppermute(tail, axis, [(i, (i + 1) % count) for i in range(ends)]),
                cells,
                lax.ppermute(head, axis, [((i + 1) % count, i) for i in range(ends)]),
            ],
            axis=dim,
        )
    return cells


def tile_terms(left_panels, right_panels, scale):
    return (
        jnp.einsum(
            "pas,pbs->apb",
            left_panels,
            right_panels,
            precision=lax.Precision.HIGHEST,
            preferred_element_type=jnp.float32,
        )
        * scale
    )


def on_device(features, pairs):
    det_rows = features.shape[0]
    shot_cols = features.shape[1]
    blocks_here = det_rows // BLK
    width = REACH * BLK
    shots_all = shot_cols * lax.axis_size("shot")
    sums, squares = lax.psum(
        (jnp.sum(features, axis=1), jnp.sum(features * features, axis=1)), "shot"
    )
    mean = sums / shots_all
    inverse = lax.rsqrt(squares / shots_all - mean * mean + 1e-06)
    standard = (features - mean[:, None]) * inverse[:, None]
    extended = extended_2(standard, (("det", 0),), width)
    base = lax.axis_index("det") * blocks_here - REACH
    blocks = extended.reshape(-1, BLK, shot_cols)
    left_panels = jnp.take(blocks, pairs[:, 0] - base, axis=0)
    right_panels = jnp.take(blocks, pairs[:, 1] - base, axis=0)
    scale = 1.0 / jnp.sqrt(jnp.float32(shots_all))
    result = lax.psum_scatter(
        tile_terms(left_panels, right_panels, scale), "shot", scatter_dimension=0, tiled=True
    )
    return result


def solution(mesh):
    in_specs = (P("det", "shot"), P("det", None))
    out_specs = P("shot", "det", None)
    return jax.shard_map(
        on_device, mesh=mesh, in_specs=in_specs, out_specs=out_specs, check_vma=False
    )
```

profile of v0, /device:TPU:24, one launch (start us, length us, event | category | flops | bytes accessed | tf_op | source)
XLA Modules:
  0.0 225.8 jit_solution(7556071061990791822)
XLA Ops:
  6.5 0.0 reduce-scatter.2.cloned.1.call-start
  6.5 2.7 %fusion.11 = (f32[1024]{0:T(1024)S(1)}, f32[1024]{0:T(1024)S(1)}) fusion(f32[1024,1024]{1,0:T(8,128)} %param.4), kind=kLoop, calls=%fused_computation.21 | loop fusion | flops 3143680 | bytes 4202496 | tf_op jit(solution)/shard_map/reduce_sum | solution.py:47
  9.3 37.0 %all-reduce = (f32[1024]{0:T(1024)S(1)}, f32[1024]{0:T(1024)S(1)}) all-reduce(f32[1024]{0:T(1024)S(1)} %get-tuple-element.7, f32[1024]{0:T(1024)S(1)} %get-tuple-element.6), channel_id=1, replica_groups=mesh['det'=32,'shot'=16] {'shot'}, use_global_device_ids=true, to_apply=%region_3.0 | all-reduce | flops 2048 | bytes 16384 | tf_op jit(solution)/shard_map/psum | solution.py:46
  46.3 0.0 copy-start.1
  46.3 2.6 %subtract_multiply_fusion = f32[1024,1024]{1,0:T(8,128)S(1)} fusion(f32[1024,1024]{1,0:T(8,128)} %param.4, f32[1024]{0:T(1024)S(1)} %get-tuple-element.17, f32[1024]{0:T(1024)S(1)} %get-tuple-element.16), kind=kLoop, calls=%fused_computation.11 | loop fusion | flops 2097152 | bytes 8396800 | tf_op jit(solution)/shard_map/mul | solution.py:51
  48.9 0.0 copy-start
  48.9 1.9 copy-done
  50.9 1.8 fusion.12
  52.7 1.9 collective-permute-start
  54.6 5.8 %collective-permute-start.1 = (f32[512,1024]{1,0:T(8,128)S(1)}, f32[512,1024]{1,0:T(8,128)}, u32[]{:S(2)}, u32[]{:S(2)}) collective-permute-start(f32[512,1024]{1,0:T(8,128)S(1)} %get-tuple-element.15), channel_id=1, source_target_pairs={{16,0},{32,16},{48,32},{64,48},{80,64},{96,80},{112,96},{128,112},... | collective-permute-start | bytes 6291464 | tf_op jit(solution)/shard_map/ppermute | solution.py:20
  60.4 0.0 copy-done.1
  60.4 22.0 %collective-permute-done = f32[512,1024]{1,0:T(8,128)} collective-permute-done((f32[512,1024]{1,0:T(8,128)}, f32[512,1024]{1,0:T(8,128)}, u32[]{:S(2)}, u32[]{:S(2)}) %collective-permute-start) | collective-permute-done | bytes 2097184 | tf_op jit(solution)/shard_map/ppermute | solution.py:18
  82.5 1.4 collective-permute-done.1
  83.9 5.9 %pad_maximum_fusion = f32[2048,1024]{1,0:T(8,128)} fusion(f32[512,1024]{1,0:T(8,128)} %collective-permute-done.1, f32[1024,1024]{1,0:T(8,128)} %copy-done, f32[512,1024]{1,0:T(8,128)} %collective-permute-done), kind=kLoop, calls=%fused_computation.5 | loop fusion | flops 4194304 | bytes 16777216 | tf_op jit(solution)/shard_map/concatenate | solution.py:16
  89.9 11.4 %gather_fusion.1 = f32[16,256,1024]{2,1,0:T(8,128)} fusion(f32[8,256,1024]{2,1,0:T(8,128)} %bitcast.9, s32[1024]{0:T(1024)S(1)} %get-tuple-element.20), kind=kCustom, calls=%fused_computation.1.clone | custom fusion | bytes 33554496 | tf_op jit(solution)/shard_map/jit(_take)/gather | solution.py:55
  101.3 11.4 %gather_fusion = f32[16,256,1024]{2,1,0:T(8,128)} fusion(f32[8,256,1024]{2,1,0:T(8,128)} %bitcast.10, s32[1024]{0:T(1024)S(1)} %get-tuple-element.21), kind=kCustom, calls=%fused_computation.clone | custom fusion | bytes 33554496 | tf_op jit(solution)/shard_map/jit(_take)/gather | solution.py:56
  112.7 24.1 %multiply_bitcast_fusion = f32[256,16,256]{0,2,1:T(8,128)} fusion(f32[16,256,1024]{2,1,0:T(8,128)} %gather_fusion.1, pred[16]{0:T(512)(128)(4,1)S(1)} %get-tuple-element.18, f32[16,256,1024]{2,1,0:T(8,128)} %gather_fusion, pred[16]{0:T(512)(128)(4,1)S(1)} %get-tuple-element.10), kind=kOutput, calls=%fused_computation.9 | convolution fusion | flops 12894339072 | bytes 37748768 | tf_op jit(solution)/shard_map/pas,pbs->apb/dot_general | solution.py:29
  136.9 5.5 %copy.4 = f32[256,16,256]{2,1,0:T(8,128)} copy(f32[256,16,256]{0,2,1:T(8,128)} %multiply_bitcast_fusion) | data formatting | bytes 8388608 | tf_op jit(solution)/shard_map/mul | solution.py:29
  142.3 0.0 reduce-scatter.2.cloned.1.call-update
  142.4 76.6 %reduce-scatter.2.cloned.1.call-done = f32[16,16,256]{2,1,0:T(8,128)} async-done(((f32[256,16,256]{2,1,0:T(8,128)}), f32[16,16,256]{2,1,0:T(8,128)}) %reduce-scatter.2.cloned.1.call-update) | async-done | bytes 262160 | tf_op jit(solution)/shard_map/reduce_scatter | solution.py:58
  (3 shorter events, 0.0 us)
Async XLA Ops:
  6.5 212.4 %reduce-scatter.2.cloned.1.call-start = ((), (), s32[]{:S(2)}) async-start(), calls=%async_computation.1 | async-start | bytes 4456448 | tf_op jit(solution)/shard_map/reduce_scatter | solution.py:58
  46.3 14.1 %copy-start.1 = (s32[16,2]{0,1:T(2,128)S(1)}, s32[16,2]{0,1:T(2,128)}, u32[]{:S(2)}) copy-start(s32[16,2]{0,1:T(2,128)} %param.5) | copy-start | bytes 388
  48.9 1.9 copy-start
  52.7 29.8 %collective-permute-start = (f32[512,1024]{1,0:T(8,128)}, f32[512,1024]{1,0:T(8,128)}, u32[]{:S(2)}, u32[]{:S(2)}) collective-permute-start(f32[512,1024]{1,0:T(8,128)} %get-tuple-element.14), channel_id=1, source_target_pairs={{0,16},{16,32},{32,48},{48,64},{64,80},{80,96},{96,112},{112,128},... | collective-permute-start | bytes 6291464 | tf_op jit(solution)/shard_map/ppermute | solution.py:18
  54.6 29.3 %collective-permute-start.1 = (f32[512,1024]{1,0:T(8,128)S(1)}, f32[512,1024]{1,0:T(8,128)}, u32[]{:S(2)}, u32[]{:S(2)}) collective-permute-start(f32[512,1024]{1,0:T(8,128)S(1)} %get-tuple-element.15), channel_id=1, source_target_pairs={{16,0},{32,16},{48,32},{64,48},{80,64},{96,80},{112,96},{128,112},... | collective-permute-start | bytes 6291464 | tf_op jit(solution)/shard_map/ppermute | solution.py:20
Sparse Core Ops, SparseCore 0:
  142.5 76.3 reduce-scatter.1
where the time goes:
time: 226 us
  waiting for transfers between devices  100 us (44%)
  blocking collectives  37 us (16%)
  local copies, waits for them, and re-layouts  32.1 us (14%)
  matrix products  24.1 us (11%)
  between operations  13.5 us (6%)
  other arithmetic  11.3 us (5%)
  starting transfers between devices  7.66 us (3%)
    reduce_scatter x1, waiting for transfers between devices, on_device(): lax.psum_scatter(tile_terms(left_panels, right_panels, scale), 'shot', sc...  76.6 us
    psum x1, blocking collectives, on_device(): lax.psum((jnp.sum(features, axis=1), jnp.sum(features * features, axis=1)...  37 us
    dot_general x1, matrix products, tile_terms(): jnp.einsum('pas,pbs->apb', left_panels, right_panels, precision=lax.Preci...  24.1 us
    ppermute x1, waiting for transfers between devices, extended_2(): lax.ppermute(tail, axis, [(i, (i + 1) % count) for i in range(ends)])  22 us
    gather x1, local copies, waits for them, and re-layouts, on_device(): left_panels = jnp.take(blocks, pairs[:, 0] - base, axis=0)  11.4 us
    gather x1, local copies, waits for them, and re-layouts, on_device(): right_panels = jnp.take(blocks, pairs[:, 1] - base, axis=0)  11.4 us
    concatenate x1, other arithmetic, extended_2(): jnp.concatenate([lax.ppermute(tail, axis, [(i, (i + 1) % count) for i in...  5.95 us
    ppermute x1, starting transfers between devices, extended_2(): lax.ppermute(head, axis, [((i + 1) % count, i) for i in range(ends)])  5.75 us
  transfers between devices with their start and end apart: 3, of which 3 were waited for; matrix products, arithmetic and copies ran while one was open for 0% of the time, Pallas kernels for 0%

commit v1 on v0

v1 whole, which is shorter than its diff:
```python
import functools

import jax
import jax.numpy as jnp
from jax import lax
from jax.experimental import pallas as pl
from jax.experimental.pallas import tpu as pltpu
from jax.sharding import PartitionSpec as P

BLK = 256
OWN = 4
EARLY = 10
MAIN = 14
PAIRS = 16
SHARDS = 16
ROWS = BLK // SHARDS
REST = PAIRS - MAIN
CHUNKS = 4 * REST * ROWS
PART = REST * ROWS
F32 = jnp.float32
BF16 = jnp.bfloat16
SMEM = pltpu.SMEM


def split_block(x, hi_ref, lo_ref, at, stats_ref, row):
    count = x.shape[1]
    mean = jnp.sum(x, axis=1, keepdims=True) * (1.0 / count)
    centered = x - mean
    squares = jnp.sum(centered * centered, axis=1, keepdims=True)
    hi = centered.astype(BF16)
    hi_ref[pl.ds(at, BLK), :] = hi
    lo_ref[pl.ds(at, BLK), :] = (centered - hi.astype(F32)).astype(BF16)
    lane = lax.broadcasted_iota(jnp.int32, (BLK, 128), 1)
    both = jnp.where(lane < 8, jnp.broadcast_to(mean, (BLK, 128)), jnp.broadcast_to(squares, (BLK, 128)))
    flat = jnp.transpose(both)
    stats_ref[0, pl.ds(row, 1), :] = flat[0:1, :]
    stats_ref[1, pl.ds(row, 1), :] = flat[8:9, :]


def product(hi_a, lo_a, hi_b, lo_b):
    dims = (((1,), (1,)), ((), ()))
    dot = functools.partial(lax.dot_general, dimension_numbers=dims, preferred_element_type=F32)
    return dot(hi_a, hi_b) + (dot(hi_a, lo_b) + dot(lo_a, hi_b))


def early_kernel(
    pairs_ref, base_ref, x_ref,
    tiles_ref, hi_ref, lo_ref, stats_ref, lower_ref, upper_ref, first_ref, second_ref, slot_ref,
):
    step = pl.program_id(0)

    @pl.when(step == 0)
    def _():
        base = base_ref[0]

        def kind_of(p):
            second = pairs_ref[p, 1] - base
            inside = jnp.logical_and(second >= 0, second < OWN)
            near = jnp.logical_and(second >= -1, second <= OWN)
            return jnp.where(inside, 0, jnp.where(near, 1, 2))

        kinds = [kind_of(p) for p in range(PAIRS)]
        n_in = sum((k == 0).astype(jnp.int32) for k in kinds)
        n_near = sum((k == 1).astype(jnp.int32) for k in kinds)
        counts = [jnp.int32(0), n_in, n_in + n_near]
        for p in range(PAIRS):
            k = kinds[p]
            slot = jnp.where(k == 0, counts[0], jnp.where(k == 1, counts[1], counts[2]))
            counts = [c + (k == i).astype(jnp.int32) for i, c in enumerate(counts)]
            slot_ref[p] = slot
            first_ref[slot] = pairs_ref[p, 0] - base
            second_ref[slot] = pairs_ref[p, 1] - base

    @pl.when(step < OWN)
    def _():
        split_block(x_ref[...], hi_ref, lo_ref, pl.multiple_of(step * BLK, BLK), stats_ref, step)

    @pl.when(step == 1)
    def _():
        lower_ref[...] = x_ref[...]

    @pl.when(step == 2)
    def _():
        upper_ref[...] = x_ref[...]

    @pl.when(step >= OWN)
    def _():
        slot = step - OWN
        a = pl.ds(pl.multiple_of(first_ref[slot] * BLK, BLK), BLK)
        b = pl.ds(pl.multiple_of(second_ref[slot] * BLK, BLK), BLK)
        tile = product(hi_ref[a, :], lo_ref[a, :], hi_ref[b, :], lo_ref[b, :])
        tiles_ref[...] = tile.reshape(SHARDS, 1, ROWS, BLK)


def early(pairs, base, features):
    rows, shots = features.shape
    return pl.pallas_call(
        early_kernel,
        grid=(OWN + EARLY,),
        in_specs=[
            pl.BlockSpec(memory_space=SMEM),
            pl.BlockSpec(memory_space=SMEM),
            pl.BlockSpec((BLK, shots), lambda i: (jnp.minimum(i, OWN - 1), 0)),
        ],
        out_specs=[
            pl.BlockSpec((SHARDS, 1, ROWS, BLK), lambda i: (0, jnp.maximum(i - OWN, 0), 0, 0)),
            pl.BlockSpec((rows, shots), lambda i: (0, 0)),
            pl.BlockSpec((rows, shots), lambda i: (0, 0)),
            pl.BlockSpec((2, OWN, BLK), lambda i: (0, 0, 0)),
            pl.BlockSpec((BLK, shots), lambda i: (0, 0)),
            pl.BlockSpec((BLK, shots), lambda i: (0, 0)),
            pl.BlockSpec(memory_space=SMEM),
            pl.BlockSpec(memory_space=SMEM),
            pl.BlockSpec(memory_space=SMEM),
        ],
        out_shape=[
            pltpu.HBM((SHARDS, MAIN, ROWS, BLK), F32),
            jax.ShapeDtypeStruct((rows, shots), BF16),
            jax.ShapeDtypeStruct((rows, shots), BF16),
            jax.ShapeDtypeStruct((2, OWN, BLK), F32),
            jax.ShapeDtypeStruct((BLK, shots), F32),
            jax.ShapeDtypeStruct((BLK, shots), F32),
            jax.ShapeDtypeStruct((PAIRS,), jnp.int32),
            jax.ShapeDtypeStruct((PAIRS,), jnp.int32),
            jax.ShapeDtypeStruct((PAIRS,), jnp.int32),
        ],
        compiler_params=pltpu.CompilerParams(vmem_limit_bytes=40 << 20),
        cost_estimate=pl.CostEstimate(flops=6 * EARLY * BLK * BLK * shots, bytes_accessed=12 << 20, transcendentals=0),
        name="early_tiles",
    )(pairs, base, features)


def near_kernel(
    first_ref, second_ref, hi_a, lo_a, hi_b, lo_b, below_ref, above_ref, _, tiles_ref, hhi, hlo, unused
):
    step = pl.program_id(0)

    @pl.when(step == 0)
    def _():
        split_block(below_ref[...], hhi, hlo, 0, unused, 0)
        split_block(above_ref[...], hhi, hlo, BLK, unused, 1)

    second = second_ref[EARLY + step]
    inside = jnp.logical_and(second >= 0, second < OWN)

    @pl.when(inside)
    def _():
        tile = product(hi_a[...], lo_a[...], hi_b[...], lo_b[...])
        tiles_ref[...] = tile.reshape(SHARDS, 1, ROWS, BLK)

    @pl.when(jnp.logical_not(inside))
    def _():
        b = pl.ds(pl.multiple_of(jnp.where(second < 0, 0, BLK), BLK), BLK)
        tile = product(hi_a[...], lo_a[...], hhi[b, :], hlo[b, :])
        tiles_ref[...] = tile.reshape(SHARDS, 1, ROWS, BLK)


def near(first, second, hi, lo, below, above, tiles):
    shots = hi.shape[1]
    left = pl.BlockSpec((BLK, shots), lambda i, a, b: (a[EARLY + i], 0))
    right = pl.BlockSpec((BLK, shots), lambda i, a, b: (jnp.clip(b[EARLY + i], 0, OWN - 1), 0))
    halo = pl.BlockSpec((BLK, shots), lambda i, a, b: (0, 0))
    return pl.pallas_call(
        near_kernel,
        grid_spec=pltpu.PrefetchScalarGridSpec(
            num_scalar_prefetch=2,
            grid=(MAIN - EARLY,),
            in_specs=[left, left, right, right, halo, halo, pl.BlockSpec(memory_space=pl.ANY)],
            out_specs=pl.BlockSpec((SHARDS, 1, ROWS, BLK), lambda i, a, b: (0, EARLY + i, 0, 0)),
            scratch_shapes=[
                pltpu.VMEM((2 * BLK, shots), BF16),
                pltpu.VMEM((2 * BLK, shots), BF16),
                pltpu.VMEM((2, 8, BLK), F32),
            ],
        ),
        out_shape=pltpu.HBM(tiles.shape, F32),
        input_output_aliases={8: 0},
        compiler_params=pltpu.CompilerParams(vmem_limit_bytes=40 << 20),
        cost_estimate=pl.CostEstimate(flops=1 << 20, bytes_accessed=1 << 20, transcendentals=0),
        name="near_tiles",
    )(first, second, hi, lo, hi, lo, below, above, tiles)


def far_kernel(
    first_ref, second_ref, me_ref, hi_ref, lo_ref, far_below, below, above, far_above, own_ref,
    keep_ref, one_ref, two_ref, three_ref, stats_ref, hhi, hlo, full,
):
    outs = (keep_ref, one_ref, two_ref, three_ref)
    for place, ref in enumerate((far_below, below, above, far_above)):
        split_block(ref[...], hhi, hlo, place * BLK, stats_ref, place)
    me = me_ref[0]
    for t in range(REST):
        second = second_ref[MAIN + t]
        a = pl.ds(pl.multiple_of(first_ref[MAIN + t] * BLK, BLK), BLK)
        inside = jnp.logical_and(second >= 0, second < OWN)

        @pl.when(inside)
        def _():
            b = pl.ds(pl.multiple_of(jnp.clip(second, 0, OWN - 1) * BLK, BLK), BLK)
            full[...] = product(hi_ref[a, :], lo_ref[a, :], hi_ref[b, :], lo_ref[b, :])

        @pl.when(jnp.logical_not(inside))
        def _():
            place = jnp.where(second < 0, second + 2, second - 2)
            b = pl.ds(pl.multiple_of(jnp.clip(place, 0, 3) * BLK, BLK), BLK)
            full[...] = product(hi_ref[a, :], lo_ref[a, :], hhi[b, :], hlo[b, :])

        for ahead in range(SHARDS):
            shard = lax.rem(me - ahead + SHARDS, SHARDS)
            part = full[pl.ds(pl.multiple_of(shard * ROWS, ROWS), ROWS), :]
            at = (ahead // 4 * REST + t) * ROWS
            outs[ahead % 4][at : at + ROWS, :] = part
    for out in outs:
        for kind in range(2):
            at = CHUNKS + 8 * kind
            out[at : at + 2, :] = stats_ref[kind, 0:2, :]
            out[at + 2 : at + 6, :] = own_ref[kind]
            out[at + 6 : at + 8, :] = stats_ref[kind, 2:4, :]


def far(first, second, me, hi, lo, far_below, below, above, far_above, own):
    shots = hi.shape[1]
    vmem = pl.BlockSpec(memory_space=pltpu.VMEM)
    smem = pl.BlockSpec(memory_space=SMEM)
    return pl.pallas_call(
        far_kernel,
        in_specs=[smem] * 3 + [vmem] * 7,
        out_specs=[vmem] * 4,
        out_shape=[jax.ShapeDtypeStruct((CHUNKS + 16, BLK), F32)] * 4,
        scratch_shapes=[
            pltpu.VMEM((2, 4, BLK), F32),
            pltpu.VMEM((4 * BLK, shots), BF16),
            pltpu.VMEM((4 * BLK, shots), BF16),
            pltpu.VMEM((BLK, BLK), F32),
        ],
        compiler_params=pltpu.CompilerParams(vmem_limit_bytes=40 << 20),
        cost_estimate=pl.CostEstimate(flops=6 * 2 * BLK * BLK * shots, bytes_accessed=9 << 20, transcendentals=0),
        name="far_tiles",
    )(first, second, me, hi, lo, far_below, below, above, far_above, own)


def merge_kernel(keep_ref, one_ref, two_ref, three_ref, *outs):
    ins = (keep_ref, one_ref, two_ref, three_ref)
    for k, out in enumerate(outs):
        here, before = pl.ds(k * PART, PART), pl.ds((k + 3) % 4 * PART, PART)
        out[:PART, :] = (keep_ref[here, :] + one_ref[here, :]) + (two_ref[here, :] + three_ref[before, :])
        for i, ref in enumerate(ins):
            out[PART + 8 * i : PART + 8 * i + 8, :] = ref[CHUNKS : CHUNKS + 8, :]
        out[PART + 32 :, :] = sum(ref[CHUNKS + 8 :, :] for ref in ins)


def merge(*packs):
    vmem = pl.BlockSpec(memory_space=pltpu.VMEM)
    return pl.pallas_call(
        merge_kernel,
        in_specs=[vmem] * 4,
        out_specs=[vmem] * 4,
        out_shape=[jax.ShapeDtypeStruct((PART + 40, BLK), F32)] * 4,
        cost_estimate=pl.CostEstimate(flops=1 << 17, bytes_accessed=1 << 20, transcendentals=0),
        name="merge",
    )(*packs)


def factors_kernel(
    count, first_ref, second_ref, me_ref, one_ref, two_ref, three_ref, four_ref, shift_ref, scale_ref, turned, dev, inv
):
    packs = (one_ref, two_ref, three_ref, four_ref)
    shards = SHARDS
    total = shards * count
    means = jnp.concatenate([ref[PART : PART + 32, :].reshape(4, 8, BLK) for ref in packs], axis=0)
    mean = jnp.sum(means, axis=0) * (1.0 / shards)
    away = means - mean[None]
    squares = sum(ref[PART + 32 :, :] for ref in packs) + count * jnp.sum(away * away, axis=0)
    inverse = lax.rsqrt(squares * (1.0 / total) + 1e-06)
    inv[...] = inverse
    for block in range(8):
        dev[block] = away[:, block, :]
    for block in range(OWN):
        column = jnp.concatenate(
            [away[:, 2 + block, :], jnp.broadcast_to(inverse[2 + block : 3 + block, :], (128 - shards, BLK))], axis=0
        )
        turned[block] = jnp.transpose(column)
    mine = pl.ds(pl.multiple_of(me_ref[0] * ROWS, ROWS), ROWS)
    for slot in range(PAIRS):
        a = first_ref[slot]
        b = second_ref[slot] + 2
        left = turned[a, mine, :]
        shift_ref[slot] = count * jnp.dot(
            left[:, :shards], dev[b], precision=lax.Precision.HIGHEST, preferred_element_type=F32
        )
        scale_ref[slot] = left[:, shards : shards + 1] * inv[pl.ds(b, 1), :] * (1.0 / total**0.5)


def factors(count, first, second, me, *packs):
    vmem = pl.BlockSpec(memory_space=pltpu.VMEM)
    smem = pl.BlockSpec(memory_space=SMEM)
    return pl.pallas_call(
        functools.partial(factors_kernel, count),
        in_specs=[smem] * 3 + [vmem] * 4,
        out_specs=[vmem] * 2,
        out_shape=[jax.ShapeDtypeStruct((PAIRS, ROWS, BLK), F32)] * 2,
        scratch_shapes=[
            pltpu.VMEM((OWN, BLK, 128), F32),
            pltpu.VMEM((8, SHARDS, BLK), F32),
            pltpu.VMEM((8, BLK), F32),
        ],
        cost_estimate=pl.CostEstimate(flops=1 << 26, bytes_accessed=2 << 20, transcendentals=2048),
        name="factors",
    )(first, second, me, *packs)


def finish_kernel(slot_ref, main_ref, own_ref, one_ref, two_ref, three_ref, shift_ref, scale_ref, out_ref, all_ref):
    all_ref[:MAIN] = (main_ref[...] + shift_ref[:MAIN]) * scale_ref[:MAIN]
    rest = (own_ref[:PART, :] + one_ref[:PART, :]) + (two_ref[:PART, :] + three_ref[:PART, :])
    rest = rest.reshape(REST, ROWS, BLK)
    all_ref[MAIN:] = (rest + shift_ref[MAIN:]) * scale_ref[MAIN:]
    for p in range(PAIRS):
        out_ref[:, p, :] = all_ref[slot_ref[p]]


def finish(slot, main, own, one, two, three, shift, scale):
    vmem = pl.BlockSpec(memory_space=pltpu.VMEM)
    return pl.pallas_call(
        finish_kernel,
        in_specs=[pl.BlockSpec(memory_space=SMEM)] + [vmem] * 7,
        out_specs=vmem,
        out_shape=jax.ShapeDtypeStruct((ROWS, PAIRS, BLK), F32),
        scratch_shapes=[pltpu.VMEM((PAIRS, ROWS, BLK), F32)],
        cost_estimate=pl.CostEstimate(flops=1 << 18, bytes_accessed=1 << 20, transcendentals=0),
        name="finish",
    )(slot, main, own, one, two, three, shift, scale)


def on_device(features, pairs):
    shots = features.shape[1]
    owners, shards = lax.axis_size("det"), lax.axis_size("shot")
    base = (lax.axis_index("det") * OWN).astype(jnp.int32).reshape(1)
    me = lax.axis_index("shot").astype(jnp.int32).reshape(1)
    up = [(i, i + 1) for i in range(owners - 1)]
    down = [(i + 1, i) for i in range(owners - 1)]

    def block(x, k):
        return lax.slice_in_dim(x, k * BLK, (k + 1) * BLK, axis=0)

    def shifted(x, by):
        return lax.ppermute(x, "shot", [(i, (i + by) % shards) for i in range(shards)])

    features, top, bottom = lax.optimization_barrier((features, block(features, 3), block(features, 0)))
    below = lax.ppermute(top, "det", up)
    above = lax.ppermute(bottom, "det", down)
    tiles, hi, lo, own_stats, lower, upper, first, second, slot = early(
        pairs, base, pltpu.with_memory_space_constraint(features, pltpu.HBM)
    )
    far_below = lax.ppermute(upper, "det", up)
    far_above = lax.ppermute(lower, "det", down)
    tiles = near(first, second, hi, lo, below, above, tiles)
    main = lax.psum_scatter(
        tiles.reshape(SHARDS * MAIN * ROWS, BLK), "shot", scatter_dimension=0, tiled=True
    ).reshape(MAIN, ROWS, BLK)

    hi, tiles = lax.optimization_barrier((hi, tiles))
    keep, one, two, three = far(first, second, me, hi, lo, far_below, below, above, far_above, own_stats)
    own, one, two, three = merge(keep, shifted(one, -1), shifted(two, -2), shifted(three, 1))
    packs = own, shifted(one, -4), shifted(two, -8), shifted(three, 4)
    shift, scale = factors(float(shots), first, second, me, *packs)
    return finish(slot, main, *packs, shift, scale)


def solution(mesh):
    in_specs = (P("det", "shot"), P("det", None))
    out_specs = P("shot", "det", None)
    return jax.shard_map(on_device, mesh=mesh, in_specs=in_specs, out_specs=out_specs, check_vma=False)
```

time: 226 us -> 149 us (0.66)
  the two profiles are of different devices: /device:TPU:24 before, /device:TPU:28 now
where the time goes in v1:
time: 149 us
  waiting for transfers between devices  49.9 us (33%)
  starting transfers between devices  47.8 us (32%)
  Pallas kernels  29.7 us (20%)
  between operations  13.6 us (9%)
  local copies, waits for them, and re-layouts  7.77 us (5%)
    ppermute x6, starting transfers between devices, shifted(): lax.ppermute(x, 'shot', [(i, (i + by) % shards) for i in range(shards)])  36.7 us
    ppermute x6, waiting for transfers between devices, shifted(): lax.ppermute(x, 'shot', [(i, (i + by) % shards) for i in range(shards)])  21.2 us
    reduce_scatter x1, waiting for transfers between devices, on_device(): lax.psum_scatter(tiles.reshape(SHARDS * MAIN * ROWS, BLK), 'shot', scatte...  16 us
    pallas_call x1, Pallas kernels, early(): pl.pallas_call(early_kernel, grid=(OWN + EARLY,), in_specs=[pl.BlockSpec(...  12.2 us
    ppermute x1, waiting for transfers between devices, on_device(): far_below = lax.ppermute(upper, 'det', up)  10.9 us
    pallas_call x1, Pallas kernels, near(): pl.pallas_call(near_kernel, grid_spec=pltpu.PrefetchScalarGridSpec(num_sc...  6.38 us
    pallas_call x1, Pallas kernels, far(): pl.pallas_call(far_kernel, in_specs=[smem] * 3 + [vmem] * 7, out_specs=[v...  4.7 us
    unnamed x31, local copies, waits for them, and re-layouts  4.66 us
  transfers between devices with their start and end apart: 11, of which 7 were waited for; matrix products, arithmetic and copies ran while one was open for 0% of the time, Pallas kernels for 14%

profile of v1, /device:TPU:28, one launch (start us, length us, event | category | flops | bytes accessed | tf_op | source)
XLA Modules:
  0.0 148.8 jit_solution(14383430987639606945)
XLA Ops:
  6.5 0.0 copy-start.14
  6.5 0.0 reduce-scatter.2.cloned.1.call-start
  6.5 3.1 %fusion = (f32[256,1024]{1,0:T(8,128)}, f32[256,1024]{1,0:T(8,128)}) fusion(f32[1024,1024]{1,0:T(8,128)} %x_ref), kind=kLoop, calls=%fused_computation | loop fusion | bytes 4194304 | tf_op jit(solution)/shard_map/slice | solution.py:343
  9.7 1.9 %collective-permute-start = (f32[256,1024]{1,0:T(8,128)}, f32[256,1024]{1,0:T(8,128)S(1)}, u32[]{:S(2)}, u32[]{:S(2)}) collective-permute-start(f32[256,1024]{1,0:T(8,128)} %get-tuple-element.34), channel_id=1, source_target_pairs={{0,16},{16,32},{32,48},{48,64},{64,80},{80,96},{96,112},{112,128},... | collective-permute-start | bytes 3145736 | tf_op jit(solution)/shard_map/ppermute | solution.py:349
  11.6 3.6 %collective-permute-start.1 = (f32[256,1024]{1,0:T(8,128)}, f32[256,1024]{1,0:T(8,128)}, u32[]{:S(2)}, u32[]{:S(2)}) collective-permute-start(f32[256,1024]{1,0:T(8,128)} %get-tuple-element.35), channel_id=1, source_target_pairs={{16,0},{32,16},{48,32},{64,48},{80,64},{96,80},{112,96},{128,112},... | collective-permute-start | bytes 3145736 | tf_op jit(solution)/shard_map/ppermute | solution.py:350
  15.2 0.0 copy-done.14
  15.2 0.1 copy.4.pairs_ref
  15.3 12.2 %early_tiles.1 = (f32[16,14,16,256]{3,2,1,0:T(8,128)}, bf16[1024,1024]{1,0:T(8,128)(2,1)S(1)}, bf16[1024,1024]{1,0:T(8,128)(2,1)S(1)}, f32[2,4,256]{2,1,0:T(4,12...) custom-call(s32[16,2]{1,0:T(8,128)S(1)} %copy.4.pairs_ref, ...), custom_call_target="tpu_custom_call" | custom-call | flops 4026531840 | bytes 12582912 | tf_op jit(solution)/shard_map/early_tiles/pallas_call | solution.py:97
  27.6 0.0 copy-start.7
  27.6 1.0 copy-done.7
  28.5 0.0 copy-start
  28.5 0.0 copy-start.5
  28.5 0.0 copy-start.6
  28.5 0.0 copy-start.3
  28.5 0.0 copy-start.4
  28.6 0.0 collective-permute-done.below_ref.below
  28.6 0.0 collective-permute-done.1.above_ref.above
  28.6 6.4 %near_tiles.1 = f32[16,14,16,256]{3,2,1,0:T(8,128)} custom-call(s32[16]{0:T(128)S(1)} %get-tuple-element.30.first_ref, s32[16]{0:T(128)S(1)} %get-tuple-element.31.second_ref, bf16[1024,1024]{1,0:T(8,128)(2,1)S(1)} %get-tuple-element.37.hi_a.hi_b.hi_ref, bf16[1024,1024]{1,0:T(8,128)(2,1)S(1)} %get-tuple-element.33.lo_a.lo_b.lo_ref, ...), custom_call_target="tpu_custom_call", output_to_operand_aliasing={{}: (8, {})} | custom-call | flops 1048576 | bytes 1048576 | tf_op jit(solution)/shard_map/near_tiles/pallas_call | solution.py:163
  35.0 0.0 copy-done
  35.0 0.0 copy-done.5
  35.0 0.0 copy-done.6
  35.0 0.0 reduce-scatter.2.cloned.1.call-update
  35.0 2.2 %collective-permute-start.2 = (f32[256,1024]{1,0:T(8,128)}, f32[256,1024]{1,0:T(8,128)}, u32[]{:S(2)}, u32[]{:S(2)}) collective-permute-start(f32[256,1024]{1,0:T(8,128)} %copy-done.7), channel_id=1, source_target_pairs={{0,16},{16,32},{32,48},{48,64},{64,80},{80,96},{96,112},{112,128},... | collective-permute-start | bytes 3145736 | tf_op jit(solution)/shard_map/ppermute | solution.py:354
  37.2 3.4 %collective-permute-start.3 = (f32[256,1024]{1,0:T(8,128)}, f32[256,1024]{1,0:T(8,128)}, u32[]{:S(2)}, u32[]{:S(2)}) collective-permute-start(f32[256,1024]{1,0:T(8,128)} %copy-done.6), channel_id=1, source_target_pairs={{16,0},{32,16},{48,32},{64,48},{80,64},{96,80},{112,96},{128,112},... | collective-permute-start | bytes 3145736 | tf_op jit(solution)/shard_map/ppermute | solution.py:355
  40.6 10.9 %collective-permute-done.2.far_below = f32[256,1024]{1,0:T(8,128)} collective-permute-done((f32[256,1024]{1,0:T(8,128)}, f32[256,1024]{1,0:T(8,128)}, u32[]{:S(2)}, u32[]{:S(2)}) %collective-permute-start.2) | collective-permute-done | bytes 1048608 | tf_op jit(solution)/shard_map/ppermute | solution.py:354
  51.4 1.8 %collective-permute-done.3.far_above = f32[256,1024]{1,0:T(8,128)} collective-permute-done((f32[256,1024]{1,0:T(8,128)}, f32[256,1024]{1,0:T(8,128)}, u32[]{:S(2)}, u32[]{:S(2)}) %collective-permute-start.3) | collective-permute-done | bytes 1048608 | tf_op jit(solution)/shard_map/ppermute | solution.py:355
  53.2 0.0 copy-done.3
  53.2 0.0 copy-done.4
  53.2 0.0 copy-start.1
  53.2 1.6 %copy-done.1 = bf16[1024,1024]{1,0:T(8,128)(2,1)S(1)} copy-done((bf16[1024,1024]{1,0:T(8,128)(2,1)S(1)}, bf16[1024,1024]{1,0:T(8,128)(2,1)}, u32[]{:S(2)}) %copy-start.1) | copy-done | bytes 2097176
  54.8 4.7 %far_tiles.1 = (f32[144,256]{1,0:T(8,128)S(1)}, f32[144,256]{1,0:T(8,128)S(1)}, f32[144,256]{1,0:T(8,128)S(1)}, f32[144,256]{1,0:T(8,128)S(1)}) custom-call(s32[16]{0:T(128)S(1)} %get-tuple-element.30.first_ref, s32[16]{0:T(128)S(1)} %get-tuple-element.31.second_ref, s32[1]{0:T(128)} %bitcast.3.me_ref, ...), custom_call_target="tpu_custom_call" | custom-call | flops 805306368 | bytes 9437184 | tf_op jit(solution)/shard_map/far_tiles/pallas_call | solution.py:225
  59.5 0.0 copy-start.2
  59.5 0.7 copy-done.2
  60.2 11.4 %collective-permute-start.4 = (f32[144,256]{1,0:T(8,128)S(1)}, f32[144,256]{1,0:T(8,128)S(1)}, u32[]{:S(2)}, u32[]{:S(2)}) collective-permute-start(f32[144,256]{1,0:T(8,128)S(1)} %get-tuple-element.42), channel_id=1, source_target_pairs={{0,15},{1,0},{2,1},{3,2},{4,3},{5,4},{6,5},{7,6},{8,7},{9,8},{10,9... | collective-permute-start | bytes 442376 | tf_op jit(solution)/shard_map/ppermute | solution.py:346
  71.6 3.3 %collective-permute-start.5 = (f32[144,256]{1,0:T(8,128)S(1)}, f32[144,256]{1,0:T(8,128)S(1)}, u32[]{:S(2)}, u32[]{:S(2)}) collective-permute-start(f32[144,256]{1,0:T(8,128)S(1)} %get-tuple-element.43), channel_id=1, source_target_pairs={{0,14},{1,15},{2,0},{3,1},{4,2},{5,3},{6,4},{7,5},{8,6},{9,7},{10,... | collective-permute-start | bytes 442376 | tf_op jit(solution)/shard_map/ppermute | solution.py:346
  74.9 2.9 %collective-permute-start.6 = (f32[144,256]{1,0:T(8,128)S(1)}, f32[144,256]{1,0:T(8,128)S(1)}, u32[]{:S(2)}, u32[]{:S(2)}) collective-permute-start(f32[144,256]{1,0:T(8,128)S(1)} %get-tuple-element.44), channel_id=1, source_target_pairs={{0,1},{1,2},{2,3},{3,4},{4,5},{5,6},{6,7},{7,8},{8,9},{9,10},{10,1... | collective-permute-start | bytes 442376 | tf_op jit(solution)/shard_map/ppermute | solution.py:346
  77.9 1.2 collective-permute-done.4.one_ref
  79.0 0.0 copy-start.11
  79.0 8.8 %collective-permute-done.5.two_ref = f32[144,256]{1,0:T(8,128)S(1)} collective-permute-done((f32[144,256]{1,0:T(8,128)S(1)}, f32[144,256]{1,0:T(8,128)S(1)}, u32[]{:S(2)}, u32[]{:S(2)}) %collective-permute-start.5) | collective-permute-done | bytes 147488 | tf_op jit(solution)/shard_map/ppermute | solution.py:346
  87.9 0.0 copy-start.12
  87.9 0.0 collective-permute-done.6.three_ref
  87.9 0.0 copy-start.13
  87.9 0.0 copy-done.11
  87.9 0.6 copy-done.12
  88.5 0.1 copy-done.13
  88.6 1.9 %merge.1 = (f32[72,256]{1,0:T(8,128)}, f32[72,256]{1,0:T(8,128)}, f32[72,256]{1,0:T(8,128)}, f32[72,256]{1,0:T(8,128)}) custom-call(f32[144,256]{1,0:T(8,128)} %copy-done.2, f32[144,256]{1,0:T(8,128)} %copy-done.11, f32[144,256]{1,0:T(8,128)} %copy-done.12, f32[144,256]{1,0:T(8,128)} %copy-done.13), custom_call_target="tpu_custom_call" | custom-call | flops 131072 | bytes 1048576 | tf_op jit(solution)/shard_map/merge/pallas_call | solution.py:254
  90.4 6.2 %collective-permute-start.7 = (f32[72,256]{1,0:T(8,128)}, f32[72,256]{1,0:T(8,128)S(1)}, u32[]{:S(2)}, u32[]{:S(2)}) collective-permute-start(f32[72,256]{1,0:T(8,128)} %get-tuple-element.46), channel_id=1, source_target_pairs={{0,12},{1,13},{2,14},{3,15},{4,0},{5,1},{6,2},{7,3},{8,4},{9,5},{1... | collective-permute-start | bytes 221192 | tf_op jit(solution)/shard_map/ppermute | solution.py:346
  96.6 5.0 %collective-permute-start.8 = (f32[72,256]{1,0:T(8,128)}, f32[72,256]{1,0:T(8,128)S(1)}, u32[]{:S(2)}, u32[]{:S(2)}) collective-permute-start(f32[72,256]{1,0:T(8,128)} %get-tuple-element.47), channel_id=1, source_target_pairs={{0,8},{1,9},{2,10},{3,11},{4,12},{5,13},{6,14},{7,15},{8,0},{9,1},... | collective-permute-start | bytes 221192 | tf_op jit(solution)/shard_map/ppermute | solution.py:346
  101.7 7.8 %collective-permute-start.9 = (f32[72,256]{1,0:T(8,128)}, f32[72,256]{1,0:T(8,128)S(1)}, u32[]{:S(2)}, u32[]{:S(2)}) collective-permute-start(f32[72,256]{1,0:T(8,128)} %get-tuple-element.48), channel_id=1, source_target_pairs={{0,4},{1,5},{2,6},{3,7},{4,8},{5,9},{6,10},{7,11},{8,12},{9,13},{1... | collective-permute-start | bytes 221192 | tf_op jit(solution)/shard_map/ppermute | solution.py:346
  109.5 0.0 collective-permute-done.7.two_ref.one_ref
  109.5 0.0 copy-start.8
  109.5 3.5 %collective-permute-done.8.three_ref.two_ref = f32[72,256]{1,0:T(8,128)S(1)} collective-permute-done((f32[72,256]{1,0:T(8,128)}, f32[72,256]{1,0:T(8,128)S(1)}, u32[]{:S(2)}, u32[]{:S(2)}) %collective-permute-start.8) | collective-permute-done | bytes 73760 | tf_op jit(solution)/shard_map/ppermute | solution.py:346
  113.1 0.0 copy-start.9
  113.1 7.7 %collective-permute-done.9.four_ref.three_ref = f32[72,256]{1,0:T(8,128)S(1)} collective-permute-done((f32[72,256]{1,0:T(8,128)}, f32[72,256]{1,0:T(8,128)S(1)}, u32[]{:S(2)}, u32[]{:S(2)}) %collective-permute-start.9) | collective-permute-done | bytes 73760 | tf_op jit(solution)/shard_map/ppermute | solution.py:346
  120.7 0.0 copy-start.10
  120.7 0.0 copy-done.8
  120.7 0.0 copy-done.9
  120.7 0.6 copy-done.10
  121.4 2.4 %factors.1 = (f32[16,16,256]{2,1,0:T(8,128)}, f32[16,16,256]{2,1,0:T(8,128)}) custom-call(s32[16]{0:T(128)} %copy-done.3, s32[16]{0:T(128)} %copy-done.4, s32[1]{0:T(128)} %bitcast.3.me_ref, f32[72,256]{1,0:T(8,128)} %get-tuple-element.45.one_ref.own_ref, f32[72,256]{1,0:T(8,128)} %copy-done.8, f32[72,256]{1,0:T(8,128)} %copy-done.9, f32[72,256]{1,0:T(8,128)} %copy-done.10), custom_call_target="tpu_custom_call" | custom-call | flops 67108864 | bytes 2097152 | tf_op jit(solution)/shard_map/factors/pallas_call | solution.py:297
  123.8 16.0 %reduce-scatter.2.cloned.1.call-done = f32[224,256]{1,0:T(8,128)} async-done(((f32[3584,256]{1,0:T(8,128)}), f32[224,256]{1,0:T(8,128)}) %reduce-scatter.2.cloned.1.call-update) | async-done | bytes 229392 | tf_op jit(solution)/shard_map/reduce_scatter | solution.py:357
  139.8 2.1 %finish.1 = f32[16,16,256]{2,1,0:T(8,128)} custom-call(s32[16]{0:T(128)} %copy-done.5, f32[14,16,256]{2,1,0:T(8,128)} %bitcast.5, f32[72,256]{1,0:T(8,128)} %get-tuple-element.45.one_ref.own_ref, f32[72,256]{1,0:T(8,128)} %copy-done.8, f32[72,256]{1,0:T(8,128)} %copy-done.9, f32[72,256]{1,0:T(8,128)} %copy-done.10, ...), custom_call_target="tpu_custom_call" | custom-call | flops 262144 | bytes 1048576 | tf_op jit(solution)/shard_map/finish/pallas_call | solution.py:323
Async XLA Ops:
  6.5 8.7 %copy-start.14 = (s32[16,2]{0,1:T(2,128)S(1)}, s32[16,2]{0,1:T(2,128)}, u32[]{:S(2)}) copy-start(s32[16,2]{0,1:T(2,128)} %param.3) | copy-start | bytes 388
  6.5 133.3 %reduce-scatter.2.cloned.1.call-start = ((), (), s32[]{:S(2)}) async-start(), calls=%async_computation.1 | async-start | bytes 3899392 | tf_op jit(solution)/shard_map/reduce_scatter | solution.py:357
  9.7 18.9 %collective-permute-start = (f32[256,1024]{1,0:T(8,128)}, f32[256,1024]{1,0:T(8,128)S(1)}, u32[]{:S(2)}, u32[]{:S(2)}) collective-permute-start(f32[256,1024]{1,0:T(8,128)} %get-tuple-element.34), channel_id=1, source_target_pairs={{0,16},{16,32},{32,48},{48,64},{64,80},{80,96},{96,112},{112,128},... | collective-permute-start | bytes 3145736 | tf_op jit(solution)/shard_map/ppermute | solution.py:349
  11.6 17.0 %collective-permute-start.1 = (f32[256,1024]{1,0:T(8,128)}, f32[256,1024]{1,0:T(8,128)}, u32[]{:S(2)}, u32[]{:S(2)}) collective-permute-start(f32[256,1024]{1,0:T(8,128)} %get-tuple-element.35), channel_id=1, source_target_pairs={{16,0},{32,16},{48,32},{64,48},{80,64},{96,80},{112,96},{128,112},... | collective-permute-start | bytes 3145736 | tf_op jit(solution)/shard_map/ppermute | solution.py:350
  27.6 1.0 copy-start.7
  28.5 6.4 %copy-start = (bf16[1024,1024]{1,0:T(8,128)(2,1)}, bf16[1024,1024]{1,0:T(8,128)(2,1)S(1)}, u32[]{:S(2)}) copy-start(bf16[1024,1024]{1,0:T(8,128)(2,1)S(1)} %get-tuple-element.33.lo_a.lo_b.lo_ref) | copy-start | bytes 6291460
  28.5 6.4 %copy-start.5 = (s32[16]{0:T(128)}, s32[16]{0:T(128)S(1)}, u32[]{:S(2)}) copy-start(s32[16]{0:T(128)S(1)} %get-tuple-element.29.slot_ref) | copy-start | bytes 196
  28.5 6.4 %copy-start.6 = (f32[256,1024]{1,0:T(8,128)}, f32[256,1024]{1,0:T(8,128)S(1)}, u32[]{:S(2)}) copy-start(f32[256,1024]{1,0:T(8,128)S(1)} %get-tuple-element.39) | copy-start | bytes 3145732
  28.5 24.6 %copy-start.3 = (s32[16]{0:T(128)}, s32[16]{0:T(128)S(1)}, u32[]{:S(2)}) copy-start(s32[16]{0:T(128)S(1)} %get-tuple-element.30.first_ref) | copy-start | bytes 196
  28.5 24.6 %copy-start.4 = (s32[16]{0:T(128)}, s32[16]{0:T(128)S(1)}, u32[]{:S(2)}) copy-start(s32[16]{0:T(128)S(1)} %get-tuple-element.31.second_ref) | copy-start | bytes 196
  35.0 16.4 %collective-permute-start.2 = (f32[256,1024]{1,0:T(8,128)}, f32[256,1024]{1,0:T(8,128)}, u32[]{:S(2)}, u32[]{:S(2)}) collective-permute-start(f32[256,1024]{1,0:T(8,128)} %copy-done.7), channel_id=1, source_target_pairs={{0,16},{16,32},{32,48},{48,64},{64,80},{80,96},{96,112},{112,128},... | collective-permute-start | bytes 3145736 | tf_op jit(solution)/shard_map/ppermute | solution.py:354
  37.2 16.0 %collective-permute-start.3 = (f32[256,1024]{1,0:T(8,128)}, f32[256,1024]{1,0:T(8,128)}, u32[]{:S(2)}, u32[]{:S(2)}) collective-permute-start(f32[256,1024]{1,0:T(8,128)} %copy-done.6), channel_id=1, source_target_pairs={{16,0},{32,16},{48,32},{64,48},{80,64},{96,80},{112,96},{128,112},... | collective-permute-start | bytes 3145736 | tf_op jit(solution)/shard_map/ppermute | solution.py:355
  53.2 1.6 %copy-start.1 = (bf16[1024,1024]{1,0:T(8,128)(2,1)S(1)}, bf16[1024,1024]{1,0:T(8,128)(2,1)}, u32[]{:S(2)}) copy-start(bf16[1024,1024]{1,0:T(8,128)(2,1)} %copy-done) | copy-start | bytes 6291460
  59.5 0.7 copy-start.2
  60.2 18.9 %collective-permute-start.4 = (f32[144,256]{1,0:T(8,128)S(1)}, f32[144,256]{1,0:T(8,128)S(1)}, u32[]{:S(2)}, u32[]{:S(2)}) collective-permute-start(f32[144,256]{1,0:T(8,128)S(1)} %get-tuple-element.42), channel_id=1, source_target_pairs={{0,15},{1,0},{2,1},{3,2},{4,3},{5,4},{6,5},{7,6},{8,7},{9,8},{10,9... | collective-permute-start | bytes 442376 | tf_op jit(solution)/shard_map/ppermute | solution.py:346
  71.6 16.3 %collective-permute-start.5 = (f32[144,256]{1,0:T(8,128)S(1)}, f32[144,256]{1,0:T(8,128)S(1)}, u32[]{:S(2)}, u32[]{:S(2)}) collective-permute-start(f32[144,256]{1,0:T(8,128)S(1)} %get-tuple-element.43), channel_id=1, source_target_pairs={{0,14},{1,15},{2,0},{3,1},{4,2},{5,3},{6,4},{7,5},{8,6},{9,7},{10,... | collective-permute-start | bytes 442376 | tf_op jit(solution)/shard_map/ppermute | solution.py:346
  74.9 12.9 %collective-permute-start.6 = (f32[144,256]{1,0:T(8,128)S(1)}, f32[144,256]{1,0:T(8,128)S(1)}, u32[]{:S(2)}, u32[]{:S(2)}) collective-permute-start(f32[144,256]{1,0:T(8,128)S(1)} %get-tuple-element.44), channel_id=1, source_target_pairs={{0,1},{1,2},{2,3},{3,4},{4,5},{5,6},{6,7},{7,8},{8,9},{9,10},{10,1... | collective-permute-start | bytes 442376 | tf_op jit(solution)/shard_map/ppermute | solution.py:346
  79.0 8.8 %copy-start.11 = (f32[144,256]{1,0:T(8,128)}, f32[144,256]{1,0:T(8,128)S(1)}, u32[]{:S(2)}) copy-start(f32[144,256]{1,0:T(8,128)S(1)} %collective-permute-done.4.one_ref) | copy-start | bytes 442372
  87.9 0.6 copy-start.12
  87.9 0.7 copy-start.13
  90.4 19.1 %collective-permute-start.7 = (f32[72,256]{1,0:T(8,128)}, f32[72,256]{1,0:T(8,128)S(1)}, u32[]{:S(2)}, u32[]{:S(2)}) collective-permute-start(f32[72,256]{1,0:T(8,128)} %get-tuple-element.46), channel_id=1, source_target_pairs={{0,12},{1,13},{2,14},{3,15},{4,0},{5,1},{6,2},{7,3},{8,4},{9,5},{1... | collective-permute-start | bytes 221192 | tf_op jit(solution)/shard_map/ppermute | solution.py:346
  96.6 16.4 %collective-permute-start.8 = (f32[72,256]{1,0:T(8,128)}, f32[72,256]{1,0:T(8,128)S(1)}, u32[]{:S(2)}, u32[]{:S(2)}) collective-permute-start(f32[72,256]{1,0:T(8,128)} %get-tuple-element.47), channel_id=1, source_target_pairs={{0,8},{1,9},{2,10},{3,11},{4,12},{5,13},{6,14},{7,15},{8,0},{9,1},... | collective-permute-start | bytes 221192 | tf_op jit(solution)/shard_map/ppermute | solution.py:346
  101.7 19.1 %collective-permute-start.9 = (f32[72,256]{1,0:T(8,128)}, f32[72,256]{1,0:T(8,128)S(1)}, u32[]{:S(2)}, u32[]{:S(2)}) collective-permute-start(f32[72,256]{1,0:T(8,128)} %get-tuple-element.48), channel_id=1, source_target_pairs={{0,4},{1,5},{2,6},{3,7},{4,8},{5,9},{6,10},{7,11},{8,12},{9,13},{1... | collective-permute-start | bytes 221192 | tf_op jit(solution)/shard_map/ppermute | solution.py:346
  109.5 11.2 %copy-start.8 = (f32[72,256]{1,0:T(8,128)}, f32[72,256]{1,0:T(8,128)S(1)}, u32[]{:S(2)}) copy-start(f32[72,256]{1,0:T(8,128)S(1)} %collective-permute-done.7.two_ref.one_ref) | copy-start | bytes 221188
  113.1 7.7 %copy-start.9 = (f32[72,256]{1,0:T(8,128)}, f32[72,256]{1,0:T(8,128)S(1)}, u32[]{:S(2)}) copy-start(f32[72,256]{1,0:T(8,128)S(1)} %collective-permute-done.8.three_ref.two_ref) | copy-start | bytes 221188
  120.7 0.6 copy-start.10
Sparse Core Ops, SparseCore 0:
  35.1 104.6 reduce-scatter.1

commit v2 on v0

v2 whole, which is shorter than its diff:
```python
import functools

import jax
import jax.numpy as jnp
from jax import lax
from jax.experimental import pallas as pl
from jax.experimental.pallas import tpu as pltpu
from jax.sharding import PartitionSpec as P

BLK = 256
OWN = 4
EARLY = 10
MADE = 16
PAIRS = 16
HOME_A, HOME_B = 16, 17
SLOTS = 18
SHARDS = 16
ROWS = BLK // SHARDS
F32 = jnp.float32
BF16 = jnp.bfloat16
SMEM = pltpu.SMEM


def split_block(x, hi_ref, lo_ref, at, stats_ref, row):
    count = x.shape[1]
    mean = jnp.sum(x, axis=1, keepdims=True) * (1.0 / count)
    centered = x - mean
    squares = jnp.sum(centered * centered, axis=1, keepdims=True)
    hi = centered.astype(BF16)
    hi_ref[pl.ds(at, BLK), :] = hi
    lo_ref[pl.ds(at, BLK), :] = (centered - hi.astype(F32)).astype(BF16)
    lane = lax.broadcasted_iota(jnp.int32, (BLK, 128), 1)
    both = jnp.where(lane < 8, jnp.broadcast_to(mean, (BLK, 128)), jnp.broadcast_to(squares, (BLK, 128)))
    flat = jnp.transpose(both)
    stats_ref[0, pl.ds(row, 1), :] = flat[0:1, :]
    stats_ref[1, pl.ds(row, 1), :] = flat[8:9, :]


def product(hi_a, lo_a, hi_b, lo_b):
    dims = (((1,), (1,)), ((), ()))
    dot = functools.partial(lax.dot_general, dimension_numbers=dims, preferred_element_type=F32)
    return dot(hi_a, hi_b) + (dot(hi_a, lo_b) + dot(lo_a, hi_b))


def borders_kernel(core_ref, x_ref, a_ref, b_ref, sems):
    core = core_ref[0]
    to_a = pltpu.make_async_copy(x_ref.at[pl.ds(core * 3 * BLK, BLK), :], a_ref, sems.at[0])
    to_b = pltpu.make_async_copy(x_ref.at[pl.ds((1 - core) * 3 * BLK, BLK), :], b_ref, sems.at[1])
    to_a.start()
    to_b.start()
    to_a.wait()
    to_b.wait()


def borders(core, features):
    shots = features.shape[1]
    return pl.pallas_call(
        borders_kernel,
        in_specs=[pl.BlockSpec(memory_space=SMEM), pl.BlockSpec(memory_space=pl.ANY)],
        out_specs=[pl.BlockSpec(memory_space=pl.ANY)] * 2,
        out_shape=[jax.ShapeDtypeStruct((BLK, shots), F32)] * 2,
        scratch_shapes=[pltpu.SemaphoreType.DMA((2,))],
        cost_estimate=pl.CostEstimate(flops=0, bytes_accessed=4 << 20, transcendentals=0),
        name="borders",
    )(core, pltpu.with_memory_space_constraint(features, pltpu.HBM))


def assign(pairs_ref, base, core, first_ref, second_ref, slot_ref):
    def kind_of(p):
        second = pairs_ref[p, 1] - base
        inside = jnp.logical_and(second >= 0, second < OWN)
        near = jnp.logical_and(second >= -1, second <= OWN)
        with_a = (second < 0) == (core == 0)
        return jnp.where(inside, 0, jnp.where(near, jnp.where(with_a, 2, 1), jnp.where(with_a, 3, 4)))

    for slot in range(MADE, SLOTS):
        first_ref[slot] = 0
        second_ref[slot] = 0
    first_ref[14] = jnp.where(core == 0, OWN, -1)
    second_ref[14] = jnp.where(core == 0, 2, 1)
    first_ref[15] = jnp.where(core == 0, -1, OWN)
    second_ref[15] = jnp.where(core == 0, 1, 2)
    kinds = [kind_of(p) for p in range(PAIRS)]
    places = [jnp.int32(0)]
    for k in range(2):
        places.append(places[-1] + sum((kind == k).astype(jnp.int32) for kind in kinds))
    for p, kind in enumerate(kinds):
        place = jnp.where(kind == 0, places[0], jnp.where(kind == 1, places[1], places[2]))
        place = jnp.where(place >= 14, 15, place)
        slot = jnp.where(kind == 3, HOME_A, jnp.where(kind == 4, HOME_B, place))
        places = [place + (kind == k).astype(jnp.int32) for k, place in enumerate(places)]
        slot_ref[p] = slot
        first_ref[slot] = pairs_ref[p, 0] - base
        second_ref[slot] = pairs_ref[p, 1] - base


def early_kernel(
    pairs_ref, place_ref, x_ref, tiles_ref, hi_ref, lo_ref, stats_ref, first_ref, second_ref, slot_ref
):
    step = pl.program_id(0)

    @pl.when(step == 0)
    def _():
        assign(pairs_ref, place_ref[0], place_ref[1], first_ref, second_ref, slot_ref)

    @pl.when(step < OWN)
    def _():
        split_block(x_ref[...], hi_ref, lo_ref, pl.multiple_of(step * BLK, BLK), stats_ref, step)

    @pl.when(step >= OWN)
    def _():
        slot = step - OWN
        a = pl.ds(pl.multiple_of(first_ref[slot] * BLK, BLK), BLK)
        b = pl.ds(pl.multiple_of(second_ref[slot] * BLK, BLK), BLK)
        tile = product(hi_ref[a, :], lo_ref[a, :], hi_ref[b, :], lo_ref[b, :])
        tiles_ref[...] = tile.reshape(SHARDS, 1, ROWS, BLK)


def early(pairs, place, features):
    rows, shots = features.shape
    smem = pl.BlockSpec(memory_space=SMEM)
    return pl.pallas_call(
        early_kernel,
        grid=(OWN + EARLY,),
        in_specs=[smem, smem, pl.BlockSpec((BLK, shots), lambda i: (jnp.minimum(i, OWN - 1), 0))],
        out_specs=[
            pl.BlockSpec((SHARDS, 1, ROWS, BLK), lambda i: (0, jnp.maximum(i - OWN, 0), 0, 0)),
            pl.BlockSpec((rows, shots), lambda i: (0, 0)),
            pl.BlockSpec((rows, shots), lambda i: (0, 0)),
            pl.BlockSpec((2, OWN, BLK), lambda i: (0, 0, 0)),
            smem,
            smem,
            smem,
        ],
        out_shape=[
            pltpu.HBM((SHARDS, MADE, ROWS, BLK), F32),
            jax.ShapeDtypeStruct((rows, shots), BF16),
            jax.ShapeDtypeStruct((rows, shots), BF16),
            jax.ShapeDtypeStruct((2, OWN, BLK), F32),
            jax.ShapeDtypeStruct((SLOTS,), jnp.int32),
            jax.ShapeDtypeStruct((SLOTS,), jnp.int32),
            jax.ShapeDtypeStruct((PAIRS,), jnp.int32),
        ],
        compiler_params=pltpu.CompilerParams(vmem_limit_bytes=40 << 20),
        cost_estimate=pl.CostEstimate(flops=6 * EARLY * BLK * BLK * shots, bytes_accessed=12 << 20, transcendentals=0),
        name="early_tiles",
    )(pairs, place, pltpu.with_memory_space_constraint(features, pltpu.HBM))


def inside(block):
    return jnp.logical_and(block >= 0, block < OWN)


def mixed_tile(a, b, own_a, own_b, halos, tiles_ref):
    def put(left, right):
        tile = product(left[0][...], left[1][...], right[0][...], right[1][...])
        tiles_ref[...] = tile.reshape(SHARDS, 1, ROWS, BLK)

    pl.when(jnp.logical_and(inside(a), inside(b)))(lambda: put(own_a, own_b))
    for here, halo in halos:
        pl.when(jnp.logical_and(inside(a), jnp.logical_and(jnp.logical_not(inside(b)), here(b))))(lambda: put(own_a, halo))
        pl.when(jnp.logical_and(jnp.logical_not(inside(a)), here(a)))(lambda: put(halo, own_b))


def with_b_kernel(
    first_ref, second_ref, hi_a, lo_a, hi_b, lo_b, halo_ref, _, tiles_ref, hhi, hlo, unused
):
    step = pl.program_id(0)

    @pl.when(step == 0)
    def _():
        split_block(halo_ref[...], hhi, hlo, 0, unused, 0)

    slot = SLOTS_B[0] + step + jnp.where(step == 2, SLOTS_B[2] - SLOTS_B[1] - 1, 0)
    halos = [(lambda block: block == block, (hhi, hlo))]
    mixed_tile(first_ref[slot], second_ref[slot], (hi_a, lo_a), (hi_b, lo_b), halos, tiles_ref)


def with_a_kernel(
    first_ref, second_ref, place_ref, hi_a, lo_a, hi_b, lo_b, hhi, hlo, halo_ref, _, tiles_ref, ahi, alo, unused
):
    step = pl.program_id(0)

    @pl.when(step == 0)
    def _():
        split_block(halo_ref[...], ahi, alo, 0, unused, 0)

    slot = SLOTS_A[0] + step + jnp.where(step == 2, SLOTS_A[2] - SLOTS_A[1] - 1, 0)
    below_is_a = place_ref[1] == 0
    halos = [
        (lambda block: (block < 0) == below_is_a, (ahi, alo)),
        (lambda block: (block < 0) != below_is_a, (hhi, hlo)),
    ]
    mixed_tile(first_ref[slot], second_ref[slot], (hi_a, lo_a), (hi_b, lo_b), halos, tiles_ref)


SLOTS_B = (10, 11, 14)
SLOTS_A = (12, 13, 15)


def near(slots, first, second, place, hi, lo, split, halo, tiles):
    shots = hi.shape[1]
    skip = slots[2] - slots[1] - 1

    def slot_of(i):
        return slots[0] + i + jnp.where(i == 2, skip, 0)

    left = pl.BlockSpec((BLK, shots), lambda i, *s: (jnp.clip(s[0][slot_of(i)], 0, OWN - 1), 0))
    right = pl.BlockSpec((BLK, shots), lambda i, *s: (jnp.clip(s[1][slot_of(i)], 0, OWN - 1), 0))
    whole = pl.BlockSpec((BLK, shots), lambda i, *s: (0, 0))
    tile = pl.BlockSpec((SHARDS, 1, ROWS, BLK), lambda i, *s: (0, slot_of(i), 0, 0))
    parts = [jax.ShapeDtypeStruct((BLK, shots), BF16)] * 2
    vmem_parts = [pltpu.VMEM((BLK, shots), BF16)] * 2
    alone = split is None
    scalars = (first, second) if alone else (first, second, place)
    arrays = (hi, lo, hi, lo) + (() if alone else tuple(split)) + (halo, tiles)
    return pl.pallas_call(
        with_b_kernel if alone else with_a_kernel,
        grid_spec=pltpu.PrefetchScalarGridSpec(
            num_scalar_prefetch=len(scalars),
            grid=(3,),
            in_specs=[left, left, right, right]
            + ([] if alone else [whole, whole])
            + [whole, pl.BlockSpec(memory_space=pl.ANY)],
            out_specs=[tile] + ([whole, whole] if alone else []),
            scratch_shapes=([] if alone else vmem_parts) + [pltpu.VMEM((2, 8, BLK), F32)],
        ),
        out_shape=[pltpu.HBM(tiles.shape, F32)] + (parts if alone else []),
        input_output_aliases={len(scalars) + len(arrays) - 1: 0},
        compiler_params=pltpu.CompilerParams(vmem_limit_bytes=24 << 20),
        cost_estimate=pl.CostEstimate(flops=6 * 3 * BLK * BLK * shots, bytes_accessed=5 << 20, transcendentals=0),
        name="tiles_with_b" if alone else "tiles_with_a",
    )(*scalars, *arrays)


def factors_kernel(
    count, first_ref, second_ref, me_ref, own_ref, below_ref, above_ref, shift_ref, scale_ref, turned, dev, inv
):
    shards = own_ref.shape[0]
    total = shards * count
    stats = jnp.concatenate([below_ref[...], own_ref[...], above_ref[...]], axis=2)
    means, squares = stats[:, 0], stats[:, 1]
    mean = jnp.sum(means, axis=0) * (1.0 / shards)
    away = means - mean[None]
    squares = jnp.sum(squares, axis=0) + count * jnp.sum(away * away, axis=0)
    inverse = lax.rsqrt(squares * (1.0 / total) + 1e-06)
    inv[...] = inverse
    for block in range(8):
        dev[block] = away[:, block, :]
    for block in range(OWN):
        column = jnp.concatenate(
            [away[:, 2 + block, :], jnp.broadcast_to(inverse[2 + block : 3 + block, :], (128 - shards, BLK))], axis=0
        )
        turned[block] = jnp.transpose(column)
    mine = pl.ds(pl.multiple_of(me_ref[0] * ROWS, ROWS), ROWS)
    for slot in range(SLOTS):
        a = jnp.clip(first_ref[slot], 0, OWN - 1)
        b = second_ref[slot] + 2
        left = turned[a, mine, :]
        shift_ref[slot] = count * jnp.dot(
            left[:, :shards], dev[b], precision=lax.Precision.HIGHEST, preferred_element_type=F32
        )
        scale_ref[slot] = left[:, shards : shards + 1] * inv[pl.ds(b, 1), :] * (1.0 / total**0.5)


def factors(count, first, second, me, *stats):
    vmem = pl.BlockSpec(memory_space=pltpu.VMEM)
    smem = pl.BlockSpec(memory_space=SMEM)
    return pl.pallas_call(
        functools.partial(factors_kernel, count),
        in_specs=[smem] * 3 + [vmem] * 3,
        out_specs=[vmem] * 2,
        out_shape=[jax.ShapeDtypeStruct((SLOTS, ROWS, BLK), F32)] * 2,
        scratch_shapes=[
            pltpu.VMEM((OWN, BLK, 128), F32),
            pltpu.VMEM((8, SHARDS, BLK), F32),
            pltpu.VMEM((8, BLK), F32),
        ],
        compiler_params=pltpu.CompilerParams(vmem_limit_bytes=8 << 20),
        cost_estimate=pl.CostEstimate(flops=1 << 26, bytes_accessed=2 << 20, transcendentals=2048),
        name="factors",
    )(first, second, me, *stats)


def finish_kernel(slot_ref, main_ref, home_a_ref, home_b_ref, shift_ref, scale_ref, out_ref, all_ref):
    all_ref[:MADE] = (main_ref[...] + shift_ref[:MADE]) * scale_ref[:MADE]
    all_ref[HOME_A] = (home_a_ref[...] + shift_ref[HOME_A]) * scale_ref[HOME_A]
    all_ref[HOME_B] = (home_b_ref[...] + shift_ref[HOME_B]) * scale_ref[HOME_B]
    for p in range(PAIRS):
        out_ref[:, p, :] = all_ref[slot_ref[p]]


def finish(slot, main, home_a, home_b, shift, scale):
    vmem = pl.BlockSpec(memory_space=pltpu.VMEM)
    return pl.pallas_call(
        finish_kernel,
        in_specs=[pl.BlockSpec(memory_space=SMEM)] + [vmem] * 5,
        out_specs=vmem,
        out_shape=jax.ShapeDtypeStruct((ROWS, PAIRS, BLK), F32),
        scratch_shapes=[pltpu.VMEM((SLOTS, ROWS, BLK), F32)],
        compiler_params=pltpu.CompilerParams(vmem_limit_bytes=8 << 20),
        cost_estimate=pl.CostEstimate(flops=1 << 18, bytes_accessed=1 << 20, transcendentals=0),
        name="finish",
    )(slot, main, home_a, home_b, shift, scale)


def on_device(features, pairs):
    shots = features.shape[1]
    owners = lax.axis_size("det")
    owner = lax.axis_index("det").astype(jnp.int32)
    core = lax.rem(owner, 2)
    place = jnp.stack([owner * OWN, core])
    me = lax.axis_index("shot").astype(jnp.int32).reshape(1)

    def swap(x, start):
        ends = [(i, i + 1) for i in range(start, owners - 1, 2)]
        return lax.ppermute(x, "det", ends + [(b, a) for a, b in ends])

    to_a, to_b = borders(core.reshape(1), features)
    from_a = swap(to_a, 1)
    from_b = swap(to_b, 0)
    tiles, hi, lo, stats, first, second, slot = early(pairs, place, features)
    tiles, *split = near(SLOTS_B, first, second, place, hi, lo, None, from_b, tiles)
    (tiles,) = near(SLOTS_A, first, second, place, hi, lo, split, from_a, tiles)
    main = lax.psum_scatter(
        tiles.reshape(SHARDS * MADE * ROWS, BLK), "shot", scatter_dimension=0, tiled=True
    ).reshape(MADE, ROWS, BLK)

    stats, tiles = lax.optimization_barrier((stats, tiles))
    stats = lax.all_gather(stats.reshape(2 * OWN, BLK), "shot").reshape(-1, 2, OWN, BLK)
    up = [(i, i + 1) for i in range(owners - 1)]
    below = lax.ppermute(stats[:, :, 2:], "det", up)
    above = lax.ppermute(stats[:, :, :2], "det", [(b, a) for a, b in up])
    shift, scale = factors(float(shots), first, second, me, stats, below, above)
    home_a, home_b = swap(main[15], 1), swap(main[14], 0)
    return finish(slot, main, home_a, home_b, shift, scale)


def solution(mesh):
    in_specs = (P("det", "shot"), P("det", None))
    out_specs = P("shot", "det", None)
    return jax.shard_map(on_device, mesh=mesh, in_specs=in_specs, out_specs=out_specs, check_vma=False)
```

time: 226 us -> 201 us (0.89)
  Pallas kernels: 0 us -> 87 us
  waiting for transfers between devices: 100 us -> 43.6 us
  local copies, waits for them, and re-layouts: 32.1 us -> 1.87 us
  matrix products: 24.1 us -> 0 us
  other arithmetic: 11.3 us -> 0.07 us
  starting transfers between devices: 7.66 us -> 17.3 us
    pallas_call x0 -> x6, Pallas kernels: none -> 87 us  [the longest x1 64.6 us: borders(): pl.pallas_call(borders_kernel, in_specs=[pl.BlockSpec(memory_space=SMEM),...]
    psum x1 -> x0, blocking collectives: 37 us -> none  [on_device(): lax.psum((jnp.sum(features, axis=1), jnp.sum(features * features, axis=1)...]
    all_gather x0 -> x1, blocking collectives: none -> 36.2 us  [on_device(): lax.all_gather(stats.reshape(2 * OWN, BLK), 'shot').reshape(-1, 2, OWN, BLK)]
    reduce_scatter x1, waiting for transfers between devices: 76.6 us -> 42 us  [on_device(): lax.psum_scatter(tiles.reshape(SHARDS * MADE * ROWS, BLK), 'shot', scatte...]
    dot_general x1 -> x0, matrix products: 24.1 us -> none  [tile_terms(): jnp.einsum('pas,pbs->apb', left_panels, right_panels, precision=lax.Preci...]
    gather x2 -> x0, local copies, waits for them, and re-layouts: 22.9 us -> none  [the longest x1 11.4 us: on_device(): left_panels = jnp.take(blocks, pairs[:, 0] - base, axis=0)]
    ppermute x2 -> x6, waiting for transfers between devices: 23.5 us -> 1.58 us  [the longest x4 1.58 us: swap(): return lax.ppermute(x, 'det', ends + [(b, a) for a, b in ends])]
    ppermute x2 -> x6, starting transfers between devices: 7.66 us -> 17.3 us  [the longest x4 13 us: swap(): return lax.ppermute(x, 'det', ends + [(b, a) for a, b in ends])]
  transfers between devices with their start and end apart: 3 -> 7, of which waited for: 3 -> 2; matrix products, arithmetic and copies ran while one was open for 0% -> 0% of each run, Pallas kernels for 0% -> 9%
where the time goes in v2:
time: 201 us; the launch traced here: 200 us
  Pallas kernels  87 us (43%)
  waiting for transfers between devices  43.6 us (22%)
  blocking collectives  36.2 us (18%)
  starting transfers between devices  17.3 us (9%)
  between operations  13.5 us (7%)
    pallas_call x1, Pallas kernels, borders(): pl.pallas_call(borders_kernel, in_specs=[pl.BlockSpec(memory_space=SMEM),...  64.6 us
    reduce_scatter x1, waiting for transfers between devices, on_device(): lax.psum_scatter(tiles.reshape(SHARDS * MADE * ROWS, BLK), 'shot', scatte...  42 us
    all_gather x1, blocking collectives, on_device(): lax.all_gather(stats.reshape(2 * OWN, BLK), 'shot').reshape(-1, 2, OWN, BLK)  36.2 us
    ppermute x4, starting transfers between devices, swap(): return lax.ppermute(x, 'det', ends + [(b, a) for a, b in ends])  13 us
    pallas_call x1, Pallas kernels, early(): pl.pallas_call(early_kernel, grid=(OWN + EARLY,), in_specs=[smem, smem, p...  12.1 us
    pallas_call x2, Pallas kernels, near(): pl.pallas_call(with_b_kernel if alone else with_a_kernel, grid_spec=pltpu...  7.54 us
  transfers between devices with their start and end apart: 7, of which 2 were waited for; matrix products, arithmetic and copies ran while one was open for 0% of the time, Pallas kernels for 9%

profile of v2, /device:TPU:24, one launch (start us, length us, event | category | flops | bytes accessed | tf_op | source)
XLA Modules:
  0.0 199.6 jit_solution(3486286347210852129)
XLA Ops:
  6.5 0.0 copy-start.1
  6.5 0.0 reduce-scatter.2.cloned.1.call-start
  6.5 64.6 %borders.1 = (f32[256,1024]{1,0:T(8,128)}, f32[256,1024]{1,0:T(8,128)}) custom-call(s32[1]{0:T(128)} %bitcast.1.core_ref, f32[1024,1024]{1,0:T(8,128)} %x_ref.3), custom_call_target="tpu_custom_call" | custom-call | bytes 4194304 | tf_op jit(solution)/shard_map/borders/pallas_call | solution.py:57
  71.2 1.9 collective-permute-start
  73.1 4.9 %collective-permute-start.1 = (f32[256,1024]{1,0:T(8,128)}, f32[256,1024]{1,0:T(8,128)S(1)}, u32[]{:S(2)}, u32[]{:S(2)}) collective-permute-start(f32[256,1024]{1,0:T(8,128)} %get-tuple-element.29), channel_id=1, source_target_pairs={{16,32},{48,64},{80,96},{112,128},{144,160},{176,192},{208,224},{2... | collective-permute-start | bytes 3145736 | tf_op jit(solution)/shard_map/ppermute | solution.py:317
  78.1 0.0 copy-done.1
  78.1 0.1 copy.6.pairs_ref
  78.2 0.1 pad_add_fusion.place_ref
  78.2 12.1 %early_tiles.1 = (f32[16,16,16,256]{3,2,1,0:T(8,128)}, bf16[1024,1024]{1,0:T(8,128)(2,1)S(1)}, bf16[1024,1024]{1,0:T(8,128)(2,1)S(1)}, f32[2,4,256]{2,1,0:T(4,12...) custom-call(s32[16,2]{1,0:T(8,128)S(1)} %copy.6.pairs_ref, s32[2]{0:T(128)S(1)} %pad_add_fusion.place_ref, ...), custom_call_target="tpu_custom_call" | custom-call | flops 4026531840 | bytes 12582912 | tf_op jit(solution)/shard_map/early_tiles/pallas_call | solution.py:122
  90.3 0.0 collective-permute-done.halo_ref
  90.3 3.7 %tiles_with_b.1 = (f32[16,16,16,256]{3,2,1,0:T(8,128)}, bf16[256,1024]{1,0:T(8,128)(2,1)S(1)}, bf16[256,1024]{1,0:T(8,128)(2,1)S(1)}) custom-call(s32[18]{0:T(128)S(1)} %get-tuple-element.21.first_ref, s32[18]{0:T(128)S(1)} %get-tuple-element.22.second_ref, bf16[1024,1024]{1,0:T(8,128)(2,1)S(1)} %get-tuple-element.23.hi_a.hi_b, ...), custom_call_target="tpu_custom_call", output_to_operand_aliasing={{0}: (7, {})} | custom-call | flops 1207959552 | bytes 5242880 | tf_op jit(solution)/shard_map/tiles_with_b/pallas_call | solution.py:217
  94.1 0.0 collective-permute-done.1.halo_ref
  94.1 3.8 %tiles_with_a.1 = f32[16,16,16,256]{3,2,1,0:T(8,128)} custom-call(s32[18]{0:T(128)S(1)} %get-tuple-element.21.first_ref, s32[18]{0:T(128)S(1)} %get-tuple-element.22.second_ref, s32[2]{0:T(128)S(1)} %pad_add_fusion.place_ref, bf16[1024,1024]{1,0:T(8,128)(2,1)S(1)} %get-tuple-element.23.hi_a.hi_b, ...), custom_call_target="tpu_custom_call", output_to_operand_aliasing={{}: (10, {})} | custom-call | flops 1207959552 | bytes 5242880 | tf_op jit(solution)/shard_map/tiles_with_a/pallas_call | solution.py:217
  97.9 0.0 reduce-scatter.2.cloned.1.call-update
  97.9 36.2 %all_gather.3 = f32[16,8,256]{2,1,0:T(8,128)S(1)} all-gather(f32[1,8,256]{2,1,0:T(8,128)S(1)} %all_gather_reshape.3), channel_id=1, replica_groups=mesh['det'=32,'shot'=16] {'shot'}, dimensions={0}, use_global_device_ids=true | all-gather | bytes 139264 | tf_op jit(solution)/shard_map/all_gather | solution.py:330
  134.1 0.1 fusion.1
  134.2 1.9 collective-permute-start.5
  136.1 2.4 %collective-permute-start.4 = (f32[16,2,2,256]{3,2,1,0:T(2,128)S(1)}, f32[16,2,2,256]{3,2,1,0:T(2,128)S(1)}, u32[]{:S(2)}, u32[]{:S(2)}) collective-permute-start(f32[16,2,2,256]{3,2,1,0:T(2,128)S(1)} %get-tuple-element.38), channel_id=1, source_target_pairs={{0,16},{16,32},{32,48},{48,64},{64,80},{80,96},{96,112},{112,128},... | collective-permute-start | bytes 196616 | tf_op jit(solution)/shard_map/ppermute | solution.py:332
  138.5 42.0 %reduce-scatter.2.cloned.1.call-done = f32[256,256]{1,0:T(8,128)} async-done(((f32[4096,256]{1,0:T(8,128)}), f32[256,256]{1,0:T(8,128)}) %reduce-scatter.2.cloned.1.call-update) | async-done | bytes 262160 | tf_op jit(solution)/shard_map/reduce_scatter | solution.py:325
  180.6 0.7 fusion
  181.3 1.9 collective-permute-start.3
  183.2 4.2 %collective-permute-start.2 = (f32[16,256]{1,0:T(8,128)S(1)}, f32[16,256]{1,0:T(8,128)S(1)}, u32[]{:S(2)}, u32[]{:S(2)}) collective-permute-start(f32[16,256]{1,0:T(8,128)S(1)} %get-tuple-element.36), channel_id=1, source_target_pairs={{16,32},{48,64},{80,96},{112,128},{144,160},{176,192},{208,224},{2... | collective-permute-start | bytes 49160 | tf_op jit(solution)/shard_map/ppermute | solution.py:317
  187.4 0.0 collective-permute-done.5.above_ref
  187.4 0.0 collective-permute-done.4.below_ref
  187.4 1.4 factors.1
  188.8 0.0 collective-permute-done.3.home_b_ref
  188.8 1.6 collective-permute-done.2.home_a_ref
  190.4 0.0 copy-start
  190.4 0.9 copy-done
  191.3 1.4 finish.1
  (2 shorter events, 0.0 us)
Async XLA Ops:
  6.5 71.5 %copy-start.1 = (s32[16,2]{0,1:T(2,128)S(1)}, s32[16,2]{0,1:T(2,128)}, u32[]{:S(2)}) copy-start(s32[16,2]{0,1:T(2,128)} %param.3) | copy-start | bytes 388
  6.5 174.0 %reduce-scatter.2.cloned.1.call-start = ((), (), s32[]{:S(2)}) async-start(), calls=%async_computation.1 | async-start | bytes 4456448 | tf_op jit(solution)/shard_map/reduce_scatter | solution.py:325
  71.2 19.2 %collective-permute-start = (f32[256,1024]{1,0:T(8,128)}, f32[256,1024]{1,0:T(8,128)S(1)}, u32[]{:S(2)}, u32[]{:S(2)}) collective-permute-start(f32[256,1024]{1,0:T(8,128)} %get-tuple-element.25), channel_id=1, source_target_pairs={{0,16},{32,48},{64,80},{96,112},{128,144},{160,176},{192,208},{224... | collective-permute-start | bytes 3145736 | tf_op jit(solution)/shard_map/ppermute | solution.py:317
  73.1 20.9 %collective-permute-start.1 = (f32[256,1024]{1,0:T(8,128)}, f32[256,1024]{1,0:T(8,128)S(1)}, u32[]{:S(2)}, u32[]{:S(2)}) collective-permute-start(f32[256,1024]{1,0:T(8,128)} %get-tuple-element.29), channel_id=1, source_target_pairs={{16,32},{48,64},{80,96},{112,128},{144,160},{176,192},{208,224},{2... | collective-permute-start | bytes 3145736 | tf_op jit(solution)/shard_map/ppermute | solution.py:317
  134.2 53.2 %collective-permute-start.5 = (f32[16,2,2,256]{3,2,1,0:T(2,128)S(1)}, f32[16,2,2,256]{3,2,1,0:T(2,128)S(1)}, u32[]{:S(2)}, u32[]{:S(2)}) collective-permute-start(f32[16,2,2,256]{3,2,1,0:T(2,128)S(1)} %get-tuple-element.37), channel_id=1, source_target_pairs={{16,0},{32,16},{48,32},{64,48},{80,64},{96,80},{112,96},{128,112},... | collective-permute-start | bytes 196616 | tf_op jit(solution)/shard_map/ppermute | solution.py:333
  136.1 51.3 %collective-permute-start.4 = (f32[16,2,2,256]{3,2,1,0:T(2,128)S(1)}, f32[16,2,2,256]{3,2,1,0:T(2,128)S(1)}, u32[]{:S(2)}, u32[]{:S(2)}) collective-permute-start(f32[16,2,2,256]{3,2,1,0:T(2,128)S(1)} %get-tuple-element.38), channel_id=1, source_target_pairs={{0,16},{16,32},{32,48},{48,64},{64,80},{80,96},{96,112},{112,128},... | collective-permute-start | bytes 196616 | tf_op jit(solution)/shard_map/ppermute | solution.py:332
  181.3 7.5 %collective-permute-start.3 = (f32[16,256]{1,0:T(8,128)S(1)}, f32[16,256]{1,0:T(8,128)S(1)}, u32[]{:S(2)}, u32[]{:S(2)}) collective-permute-start(f32[16,256]{1,0:T(8,128)S(1)} %get-tuple-element.35), channel_id=1, source_target_pairs={{0,16},{32,48},{64,80},{96,112},{128,144},{160,176},{192,208},{224... | collective-permute-start | bytes 49160 | tf_op jit(solution)/shard_map/ppermute | solution.py:317
  183.2 7.2 %collective-permute-start.2 = (f32[16,256]{1,0:T(8,128)S(1)}, f32[16,256]{1,0:T(8,128)S(1)}, u32[]{:S(2)}, u32[]{:S(2)}) collective-permute-start(f32[16,256]{1,0:T(8,128)S(1)} %get-tuple-element.36), channel_id=1, source_target_pairs={{16,32},{48,64},{80,96},{112,128},{144,160},{176,192},{208,224},{2... | collective-permute-start | bytes 49160 | tf_op jit(solution)/shard_map/ppermute | solution.py:317
  190.4 1.0 copy-start
Sparse Core Ops, SparseCore 0:
  98.0 82.4 reduce-scatter.1

commit v3 on v2

v3 whole, which is shorter than its diff:
```python
import functools

import jax
import jax.numpy as jnp
from jax import lax
from jax.experimental import pallas as pl
from jax.experimental.pallas import tpu as pltpu
from jax.sharding import PartitionSpec as P

BLK = 256
OWN = 4
EARLY = 10
MADE = 16
PAIRS = 16
HOME = 16
SLOTS = 17
SHARDS = 16
ROWS = BLK // SHARDS
F32 = jnp.float32
BF16 = jnp.bfloat16
SMEM = pltpu.SMEM
VMEM = pltpu.VMEM


def split_block(x, hi_ref, lo_ref, at, stats_ref, row):
    count = x.shape[1]
    mean = jnp.sum(x, axis=1, keepdims=True) * (1.0 / count)
    centered = x - mean
    squares = jnp.sum(centered * centered, axis=1, keepdims=True)
    hi = centered.astype(BF16)
    hi_ref[pl.ds(at, BLK), :] = hi
    lo_ref[pl.ds(at, BLK), :] = (centered - hi.astype(F32)).astype(BF16)
    lane = lax.broadcasted_iota(jnp.int32, (BLK, 128), 1)
    both = jnp.where(lane < 8, jnp.broadcast_to(mean, (BLK, 128)), jnp.broadcast_to(squares, (BLK, 128)))
    flat = jnp.transpose(both)
    stats_ref[0, pl.ds(row, 1), :] = flat[0:1, :]
    stats_ref[1, pl.ds(row, 1), :] = flat[8:9, :]


def product(hi_a, lo_a, hi_b, lo_b):
    dims = (((1,), (1,)), ((), ()))
    dot = functools.partial(lax.dot_general, dimension_numbers=dims, preferred_element_type=F32)
    return dot(hi_a, hi_b) + (dot(hi_a, lo_b) + dot(lo_a, hi_b))


def borders_kernel(core_ref, x_ref, a_ref, b_ref, sems):
    core = core_ref[0]
    to_a = pltpu.make_async_copy(x_ref.at[pl.ds(core * (3 * BLK), BLK), :], a_ref, sems.at[0])
    to_b = pltpu.make_async_copy(x_ref.at[pl.ds((1 - core) * (2 * BLK), 2 * BLK), :], b_ref, sems.at[1])
    to_a.start()
    to_b.start()
    to_a.wait()
    to_b.wait()


def borders(core, features):
    shots = features.shape[1]
    return pl.pallas_call(
        borders_kernel,
        in_specs=[pl.BlockSpec(memory_space=SMEM), pl.BlockSpec(memory_space=pl.ANY)],
        out_specs=[pl.BlockSpec(memory_space=VMEM)] * 2,
        out_shape=[jax.ShapeDtypeStruct((BLK, shots), F32), jax.ShapeDtypeStruct((2 * BLK, shots), F32)],
        scratch_shapes=[pltpu.SemaphoreType.DMA((2,))],
        compiler_params=pltpu.CompilerParams(vmem_limit_bytes=8 << 20),
        cost_estimate=pl.CostEstimate(flops=0, bytes_accessed=4 << 20, transcendentals=0),
        name="borders",
    )(core, pltpu.with_memory_space_constraint(features, pltpu.HBM))


def assign(pairs_ref, base, core, first_ref, second_ref, slot_ref):
    def kind_of(p):
        second = pairs_ref[p, 1] - base
        own = jnp.logical_and(second >= 0, second < OWN)
        near = jnp.logical_and(second >= -1, second <= OWN)
        with_a = (second < 0) == (core == 0)
        return jnp.where(own, 0, jnp.where(with_a, jnp.where(near, 2, 3), 1))

    first_ref[HOME] = 0
    second_ref[HOME] = 0
    first_ref[15] = jnp.where(core == 0, -1, OWN)
    second_ref[15] = jnp.where(core == 0, 1, 2)
    kinds = [kind_of(p) for p in range(PAIRS)]
    places = [jnp.int32(0)]
    for k in range(2):
        places.append(places[-1] + sum((kind == k).astype(jnp.int32) for kind in kinds))
    for p, kind in enumerate(kinds):
        place = jnp.where(kind == 0, places[0], jnp.where(kind == 1, places[1], places[2]))
        slot = jnp.where(kind == 3, HOME, place)
        places = [place + (kind == k).astype(jnp.int32) for k, place in enumerate(places)]
        slot_ref[p] = slot
        first_ref[slot] = pairs_ref[p, 0] - base
        second_ref[slot] = pairs_ref[p, 1] - base


def fill(start, count, make, tiles_ref, buffers, sems):
    def copy(step):
        way = lax.rem(step, 2)
        return pltpu.make_async_copy(buffers.at[way], tiles_ref.at[:, start + step], sems.at[way])

    def body(step, carry):
        pl.when(step >= 2)(lambda: copy(step - 2).wait())

        def put(tile):
            buffers[lax.rem(step, 2)] = tile.reshape(SHARDS, ROWS, BLK)

        make(start + step, put)
        copy(step).start()
        return carry

    lax.fori_loop(0, count, body, 0)
    copy(jnp.int32(count - 2)).wait()
    copy(jnp.int32(count - 1)).wait()


def rows_of(ref, place):
    return ref[pl.ds(pl.multiple_of(place * BLK, BLK), BLK), :]


def early_kernel(
    pairs_ref, place_ref, x_ref, tiles_ref, hi_ref, lo_ref, stats_ref, first_ref, second_ref, slot_ref,
    x_vmem, buffers, in_sems, out_sems,
):
    loads = [
        pltpu.make_async_copy(x_ref.at[pl.ds(k * BLK, BLK), :], x_vmem.at[k], in_sems.at[k]) for k in range(OWN)
    ]
    for load in loads:
        load.start()
    assign(pairs_ref, place_ref[0], place_ref[1], first_ref, second_ref, slot_ref)
    for k, load in enumerate(loads):
        load.wait()
        split_block(x_vmem[k], hi_ref, lo_ref, k * BLK, stats_ref, k)

    def make(slot, put):
        a, b = first_ref[slot], second_ref[slot]
        put(product(rows_of(hi_ref, a), rows_of(lo_ref, a), rows_of(hi_ref, b), rows_of(lo_ref, b)))

    fill(0, EARLY, make, tiles_ref, buffers, out_sems)


def early(pairs, place, features):
    rows, shots = features.shape
    smem, vmem, anywhere = (pl.BlockSpec(memory_space=space) for space in (SMEM, VMEM, pl.ANY))
    return pl.pallas_call(
        early_kernel,
        in_specs=[smem, smem, anywhere],
        out_specs=[anywhere, vmem, vmem, vmem, smem, smem, smem],
        out_shape=[
            pltpu.HBM((SHARDS, MADE, ROWS, BLK), F32),
            jax.ShapeDtypeStruct((rows, shots), BF16),
            jax.ShapeDtypeStruct((rows, shots), BF16),
            jax.ShapeDtypeStruct((2, OWN, BLK), F32),
            jax.ShapeDtypeStruct((SLOTS,), jnp.int32),
            jax.ShapeDtypeStruct((SLOTS,), jnp.int32),
            jax.ShapeDtypeStruct((PAIRS,), jnp.int32),
        ],
        scratch_shapes=[
            VMEM((OWN, BLK, shots), F32),
            VMEM((2, SHARDS, ROWS, BLK), F32),
            pltpu.SemaphoreType.DMA((OWN,)),
            pltpu.SemaphoreType.DMA((2,)),
        ],
        compiler_params=pltpu.CompilerParams(vmem_limit_bytes=24 << 20),
        cost_estimate=pl.CostEstimate(flops=6 * EARLY * BLK * BLK * shots, bytes_accessed=12 << 20, transcendentals=0),
        name="early_tiles",
    )(pairs, place, pltpu.with_memory_space_constraint(features, pltpu.HBM))


def mixed(first_ref, second_ref, own, halos):
    def inside(block):
        return jnp.logical_and(block >= 0, block < OWN)

    def parts(refs, place):
        return [rows_of(ref, place) for ref in refs]

    def make(slot, put):
        a, b = first_ref[slot], second_ref[slot]
        a_in, b_in = inside(a), inside(b)
        pl.when(jnp.logical_and(a_in, b_in))(lambda: put(product(*parts(own, a), *parts(own, b))))
        for here, place, halo in halos:

            @pl.when(jnp.logical_and(jnp.logical_not(b_in), here(b)))
            def _():
                put(product(*parts(own, a), *parts(halo, place(b))))

            @pl.when(jnp.logical_and(jnp.logical_not(a_in), here(a)))
            def _():
                put(product(*parts(halo, place(a)), *parts(own, b)))

    return make


def place_in_b(block):
    return jnp.where(block < 0, block + 2, block - OWN)


def with_b_kernel(
    first_ref, second_ref, hi_ref, lo_ref, halo_ref, _, tiles_ref, bhi_ref, blo_ref, unused, buffers, sems
):
    for k in range(2):
        split_block(halo_ref[k * BLK : (k + 1) * BLK, :], bhi_ref, blo_ref, k * BLK, unused, k)
    halos = [(lambda block: block == block, place_in_b, (bhi_ref, blo_ref))]
    make = mixed(first_ref, second_ref, (hi_ref, lo_ref), halos)
    fill(EARLY, 3, make, tiles_ref, buffers, sems)


def with_a_kernel(
    first_ref, second_ref, place_ref, hi_ref, lo_ref, bhi_ref, blo_ref, halo_ref, _, tiles_ref,
    ahi_ref, alo_ref, unused, buffers, sems,
):
    split_block(halo_ref[...], ahi_ref, alo_ref, 0, unused, 0)
    below_is_a = place_ref[1] == 0
    halos = [
        (lambda block: (block < 0) == below_is_a, lambda block: 0, (ahi_ref, alo_ref)),
        (lambda block: (block < 0) != below_is_a, place_in_b, (bhi_ref, blo_ref)),
    ]
    make = mixed(first_ref, second_ref, (hi_ref, lo_ref), halos)
    fill(EARLY + 3, 3, make, tiles_ref, buffers, sems)


def near(kernel, scalars, arrays, tiles, split_out, shots, name):
    smem, vmem, anywhere = (pl.BlockSpec(memory_space=space) for space in (SMEM, VMEM, pl.ANY))
    ahead = len(scalars) + len(arrays)
    return pl.pallas_call(
        kernel,
        in_specs=[smem] * len(scalars) + [vmem] * len(arrays) + [anywhere],
        out_specs=[anywhere] + ([vmem] * 2 if split_out else []),
        out_shape=[pltpu.HBM(tiles.shape, F32)]
        + ([jax.ShapeDtypeStruct((split_out * BLK, shots), BF16)] * 2 if split_out else []),
        scratch_shapes=([] if split_out else [VMEM((BLK, shots), BF16)] * 2)
        + [VMEM((2, 8, BLK), F32), VMEM((2, SHARDS, ROWS, BLK), F32), pltpu.SemaphoreType.DMA((2,))],
        input_output_aliases={ahead: 0},
        compiler_params=pltpu.CompilerParams(vmem_limit_bytes=16 << 20),
        cost_estimate=pl.CostEstimate(flops=6 * 3 * BLK * BLK * shots, bytes_accessed=5 << 20, transcendentals=0),
        name=name,
    )(*scalars, *arrays, tiles)


def factors_kernel(
    count, first_ref, second_ref, me_ref, own_ref, below_ref, above_ref, shift_ref, scale_ref, turned, dev, inv
):
    shards = own_ref.shape[0]
    total = shards * count
    stats = jnp.concatenate([below_ref[...], own_ref[...], above_ref[...]], axis=2)
    means, squares = stats[:, 0], stats[:, 1]
    mean = jnp.sum(means, axis=0) * (1.0 / shards)
    away = means - mean[None]
    squares = jnp.sum(squares, axis=0) + count * jnp.sum(away * away, axis=0)
    inverse = lax.rsqrt(squares * (1.0 / total) + 1e-06)
    inv[...] = inverse
    for block in range(8):
        dev[block] = away[:, block, :]
    for block in range(OWN):
        column = jnp.concatenate(
            [away[:, 2 + block, :], jnp.broadcast_to(inverse[2 + block : 3 + block, :], (128 - shards, BLK))], axis=0
        )
        turned[block] = jnp.transpose(column)
    mine = pl.ds(pl.multiple_of(me_ref[0] * ROWS, ROWS), ROWS)
    for slot in range(SLOTS):
        a = jnp.clip(first_ref[slot], 0, OWN - 1)
        b = second_ref[slot] + 2
        left = turned[a, mine, :]
        shift_ref[slot] = count * jnp.dot(
            left[:, :shards], dev[b], precision=lax.Precision.HIGHEST, preferred_element_type=F32
        )
        scale_ref[slot] = left[:, shards : shards + 1] * inv[pl.ds(b, 1), :] * (1.0 / total**0.5)


def factors(count, first, second, me, *stats):
    vmem = pl.BlockSpec(memory_space=VMEM)
    smem = pl.BlockSpec(memory_space=SMEM)
    return pl.pallas_call(
        functools.partial(factors_kernel, count),
        in_specs=[smem] * 3 + [vmem] * 3,
        out_specs=[vmem] * 2,
        out_shape=[jax.ShapeDtypeStruct((SLOTS, ROWS, BLK), F32)] * 2,
        scratch_shapes=[
            VMEM((OWN, BLK, 128), F32),
            VMEM((8, SHARDS, BLK), F32),
            VMEM((8, BLK), F32),
        ],
        compiler_params=pltpu.CompilerParams(vmem_limit_bytes=8 << 20),
        cost_estimate=pl.CostEstimate(flops=1 << 26, bytes_accessed=2 << 20, transcendentals=2048),
        name="factors",
    )(first, second, me, *stats)


def finish_kernel(slot_ref, main_ref, home_ref, shift_ref, scale_ref, out_ref, all_ref):
    all_ref[:MADE] = (main_ref[...] + shift_ref[:MADE]) * scale_ref[:MADE]
    all_ref[HOME] = (home_ref[...] + shift_ref[HOME]) * scale_ref[HOME]
    for p in range(PAIRS):
        out_ref[:, p, :] = all_ref[slot_ref[p]]


def finish(slot, main, home, shift, scale):
    vmem = pl.BlockSpec(memory_space=VMEM)
    return pl.pallas_call(
        finish_kernel,
        in_specs=[pl.BlockSpec(memory_space=SMEM)] + [vmem] * 4,
        out_specs=vmem,
        out_shape=jax.ShapeDtypeStruct((ROWS, PAIRS, BLK), F32),
        scratch_shapes=[VMEM((SLOTS, ROWS, BLK), F32)],
        compiler_params=pltpu.CompilerParams(vmem_limit_bytes=8 << 20),
        cost_estimate=pl.CostEstimate(flops=1 << 18, bytes_accessed=1 << 20, transcendentals=0),
        name="finish",
    )(slot, main, home, shift, scale)


def on_device(features, pairs):
    shots = features.shape[1]
    owners = lax.axis_size("det")
    owner = lax.axis_index("det").astype(jnp.int32)
    core = lax.rem(owner, 2)
    place = jnp.stack([owner * OWN, core])
    me = lax.axis_index("shot").astype(jnp.int32).reshape(1)

    def swap(x, start):
        ends = [(i, i + 1) for i in range(start, owners - 1, 2)]
        return lax.ppermute(x, "det", ends + [(b, a) for a, b in ends])

    to_a, to_b = borders(core.reshape(1), features)
    from_a = swap(to_a, 1)
    from_b = swap(to_b, 0)
    tiles, hi, lo, stats, first, second, slot = early(pairs, place, features)
    tiles, *split = near(with_b_kernel, (first, second), (hi, lo, from_b), tiles, 2, shots, "tiles_with_b")
    (tiles,) = near(with_a_kernel, (first, second, place), (hi, lo, *split, from_a), tiles, 0, shots, "tiles_with_a")
    main = lax.psum_scatter(
        tiles.reshape(SHARDS * MADE * ROWS, BLK), "shot", scatter_dimension=0, tiled=True
    ).reshape(MADE, ROWS, BLK)

    stats, tiles = lax.optimization_barrier((stats, tiles))
    stats = lax.all_gather(stats.reshape(2 * OWN, BLK), "shot").reshape(-1, 2, OWN, BLK)
    up = [(i, i + 1) for i in range(owners - 1)]
    below = lax.ppermute(stats[:, :, 2:], "det", up)
    above = lax.ppermute(stats[:, :, :2], "det", [(b, a) for a, b in up])
    shift, scale = factors(float(shots), first, second, me, stats, below, above)
    return finish(slot, main, swap(main[15], 1), shift, scale)


def solution(mesh):
    in_specs = (P("det", "shot"), P("det", None))
    out_specs = P("shot", "det", None)
    return jax.shard_map(on_device, mesh=mesh, in_specs=in_specs, out_specs=out_specs, check_vma=False)
```

time: 201 us -> 137 us (0.68)
  Pallas kernels: 87 us -> 25.7 us
  starting transfers between devices: 17.3 us -> 13.1 us
  waiting for transfers between devices: 43.6 us -> 45.9 us
    pallas_call x1, Pallas kernels: 64.6 us -> 3.58 us  [borders(): pl.pallas_call(borders_kernel, in_specs=[pl.BlockSpec(memory_space=SMEM),...]
    ppermute x4 -> x3, starting transfers between devices: 13 us -> 8.78 us  [swap(): return lax.ppermute(x, 'det', ends + [(b, a) for a, b in ends])]
    ppermute x4 -> x3, waiting for transfers between devices: 1.58 us -> 3.92 us  [swap(): return lax.ppermute(x, 'det', ends + [(b, a) for a, b in ends])]
  transfers between devices with their start and end apart: 7 -> 6, of which waited for: 2 -> 2; matrix products, arithmetic and copies ran while one was open for 0% -> 1% of each run, Pallas kernels for 9% -> 12%
where the time goes in v3:
time: 137 us; the launch traced here: 136 us
  waiting for transfers between devices  45.9 us (34%)
  blocking collectives  36.2 us (26%)
  Pallas kernels  25.7 us (19%)
  between operations  13.5 us (10%)
  starting transfers between devices  13.1 us (10%)
  local copies, waits for them, and re-layouts  1.86 us (1%)
    reduce_scatter x1, waiting for transfers between devices, on_device(): lax.psum_scatter(tiles.reshape(SHARDS * MADE * ROWS, BLK), 'shot', scatte...  42 us
    all_gather x1, blocking collectives, on_device(): lax.all_gather(stats.reshape(2 * OWN, BLK), 'shot').reshape(-1, 2, OWN, BLK)  36.2 us
    pallas_call x1, Pallas kernels, early(): pl.pallas_call(early_kernel, in_specs=[smem, smem, anywhere], out_specs=[...  11.7 us
    ppermute x3, starting transfers between devices, swap(): return lax.ppermute(x, 'det', ends + [(b, a) for a, b in ends])  8.78 us
    pallas_call x2, Pallas kernels, near(): pl.pallas_call(kernel, in_specs=[smem] * len(scalars) + [vmem] * len(arra...  7.72 us
    ppermute x3, waiting for transfers between devices, swap(): return lax.ppermute(x, 'det', ends + [(b, a) for a, b in ends])  3.92 us
    pallas_call x1, Pallas kernels, borders(): pl.pallas_call(borders_kernel, in_specs=[pl.BlockSpec(memory_space=SMEM),...  3.58 us
  transfers between devices with their start and end apart: 6, of which 2 were waited for; matrix products, arithmetic and copies ran while one was open for 1% of the time, Pallas kernels for 12%

profile of v3, /device:TPU:24, one launch (start us, length us, event | category | flops | bytes accessed | tf_op | source)
XLA Modules:
  0.0 136.4 jit_solution(16300275220688601719)
XLA Ops:
  6.5 0.0 copy-start.1
  6.5 0.0 reduce-scatter.2.cloned.1.call-start
  6.5 3.6 %borders.1 = (f32[256,1024]{1,0:T(8,128)}, f32[512,1024]{1,0:T(8,128)}) custom-call(s32[1]{0:T(128)} %bitcast.1.core_ref, f32[1024,1024]{1,0:T(8,128)} %x_ref.3), custom_call_target="tpu_custom_call" | custom-call | bytes 4194304 | tf_op jit(solution)/shard_map/borders/pallas_call | solution.py:58
  10.1 1.9 %collective-permute-start = (f32[512,1024]{1,0:T(8,128)}, f32[512,1024]{1,0:T(8,128)S(1)}, u32[]{:S(2)}, u32[]{:S(2)}) collective-permute-start(f32[512,1024]{1,0:T(8,128)} %get-tuple-element.25), channel_id=1, source_target_pairs={{0,16},{32,48},{64,80},{96,112},{128,144},{160,176},{192,208},{224... | collective-permute-start | bytes 6291464 | tf_op jit(solution)/shard_map/ppermute | solution.py:318
  12.1 4.9 %collective-permute-start.1 = (f32[256,1024]{1,0:T(8,128)}, f32[256,1024]{1,0:T(8,128)S(1)}, u32[]{:S(2)}, u32[]{:S(2)}) collective-permute-start(f32[256,1024]{1,0:T(8,128)} %get-tuple-element.29), channel_id=1, source_target_pairs={{16,32},{48,64},{80,96},{112,128},{144,160},{176,192},{208,224},{2... | collective-permute-start | bytes 3145736 | tf_op jit(solution)/shard_map/ppermute | solution.py:318
  17.0 0.0 copy-done.1
  17.0 0.1 copy.6.pairs_ref
  17.1 0.1 pad_add_fusion.place_ref
  17.2 11.7 %early_tiles.1 = (f32[16,16,16,256]{3,2,1,0:T(8,128)}, bf16[1024,1024]{1,0:T(8,128)(2,1)S(1)}, bf16[1024,1024]{1,0:T(8,128)(2,1)S(1)}, f32[2,4,256]{2,1,0:T(4,12...) custom-call(s32[16,2]{1,0:T(8,128)S(1)} %copy.6.pairs_ref, s32[2]{0:T(128)S(1)} %pad_add_fusion.place_ref, ...), custom_call_target="tpu_custom_call" | custom-call | flops 4026531840 | bytes 12582912 | tf_op jit(solution)/shard_map/early_tiles/pallas_call | solution.py:143
  28.9 0.0 collective-permute-done.halo_ref
  28.9 4.0 %tiles_with_b.1 = (f32[16,16,16,256]{3,2,1,0:T(8,128)}, bf16[512,1024]{1,0:T(8,128)(2,1)S(1)}, bf16[512,1024]{1,0:T(8,128)(2,1)S(1)}) custom-call(s32[17]{0:T(128)S(1)} %get-tuple-element.21.first_ref, s32[17]{0:T(128)S(1)} %get-tuple-element.22.second_ref, bf16[1024,1024]{1,0:T(8,128)(2,1)S(1)} %get-tuple-element.23.hi_ref, ...), custom_call_target="tpu_custom_call", output_to_operand_aliasing={{0}: (5, {})} | custom-call | flops 1207959552 | bytes 5242880 | tf_op jit(solution)/shard_map/tiles_with_b/pallas_call | solution.py:223
  32.9 0.0 collective-permute-done.1.halo_ref
  32.9 3.7 %tiles_with_a.1 = f32[16,16,16,256]{3,2,1,0:T(8,128)} custom-call(s32[17]{0:T(128)S(1)} %get-tuple-element.21.first_ref, s32[17]{0:T(128)S(1)} %get-tuple-element.22.second_ref, s32[2]{0:T(128)S(1)} %pad_add_fusion.place_ref, bf16[1024,1024]{1,0:T(8,128)(2,1)S(1)} %get-tuple-element.23.hi_ref, ...), custom_call_target="tpu_custom_call", output_to_operand_aliasing={{}: (8, {})} | custom-call | flops 1207959552 | bytes 5242880 | tf_op jit(solution)/shard_map/tiles_with_a/pallas_call | solution.py:223
  36.6 0.0 reduce-scatter.2.cloned.1.call-update
  36.7 36.2 %all_gather.3 = f32[16,8,256]{2,1,0:T(8,128)S(1)} all-gather(f32[1,8,256]{2,1,0:T(8,128)S(1)} %all_gather_reshape.3), channel_id=1, replica_groups=mesh['det'=32,'shot'=16] {'shot'}, dimensions={0}, use_global_device_ids=true | all-gather | bytes 139264 | tf_op jit(solution)/shard_map/all_gather | solution.py:331
  72.9 0.1 fusion
  73.0 1.9 %collective-permute-start.4 = (f32[16,2,2,256]{3,2,1,0:T(2,128)S(1)}, f32[16,2,2,256]{3,2,1,0:T(2,128)S(1)}, u32[]{:S(2)}, u32[]{:S(2)}) collective-permute-start(f32[16,2,2,256]{3,2,1,0:T(2,128)S(1)} %get-tuple-element.35), channel_id=1, source_target_pairs={{16,0},{32,16},{48,32},{64,48},{80,64},{96,80},{112,96},{128,112},... | collective-permute-start | bytes 196616 | tf_op jit(solution)/shard_map/ppermute | solution.py:334
  74.9 2.4 %collective-permute-start.3 = (f32[16,2,2,256]{3,2,1,0:T(2,128)S(1)}, f32[16,2,2,256]{3,2,1,0:T(2,128)S(1)}, u32[]{:S(2)}, u32[]{:S(2)}) collective-permute-start(f32[16,2,2,256]{3,2,1,0:T(2,128)S(1)} %get-tuple-element.36), channel_id=1, source_target_pairs={{0,16},{16,32},{32,48},{48,64},{64,80},{80,96},{96,112},{112,128},... | collective-permute-start | bytes 196616 | tf_op jit(solution)/shard_map/ppermute | solution.py:333
  77.3 42.0 %reduce-scatter.2.cloned.1.call-done = f32[256,256]{1,0:T(8,128)} async-done(((f32[4096,256]{1,0:T(8,128)}), f32[256,256]{1,0:T(8,128)}) %reduce-scatter.2.cloned.1.call-update) | async-done | bytes 262160 | tf_op jit(solution)/shard_map/reduce_scatter | solution.py:326
  119.3 0.7 slice.13
  120.0 1.9 %collective-permute-start.2 = (f32[16,256]{1,0:T(8,128)S(1)}, f32[16,256]{1,0:T(8,128)S(1)}, u32[]{:S(2)}, u32[]{:S(2)}) collective-permute-start(f32[16,256]{1,0:T(8,128)S(1)} %slice.13), channel_id=1, source_target_pairs={{16,32},{48,64},{80,96},{112,128},{144,160},{176,192},{208,224},{2... | collective-permute-start | bytes 49160 | tf_op jit(solution)/shard_map/ppermute | solution.py:318
  121.9 0.0 collective-permute-done.4.above_ref
  121.9 0.0 collective-permute-done.3.below_ref
  121.9 1.3 factors.1
  123.2 3.9 %collective-permute-done.2.home_ref = f32[16,256]{1,0:T(8,128)S(1)} collective-permute-done((f32[16,256]{1,0:T(8,128)S(1)}, f32[16,256]{1,0:T(8,128)S(1)}, u32[]{:S(2)}, u32[]{:S(2)}) %collective-permute-start.2) | collective-permute-done | bytes 16416 | tf_op jit(solution)/shard_map/ppermute | solution.py:318
  127.2 0.0 copy-start
  127.2 0.9 copy-done
  128.1 1.4 %finish.1 = f32[16,16,256]{2,1,0:T(8,128)} custom-call(s32[16]{0:T(128)S(1)} %get-tuple-element.20.slot_ref, f32[16,16,256]{2,1,0:T(8,128)S(1)} %bitcast.5, f32[16,256]{1,0:T(8,128)S(1)} %collective-permute-done.2.home_ref, f32[17,16,256]{2,1,0:T(8,128)S(1)} %get-tuple-element.33.shift_ref, f32[17,16,256]{2,1,0:T(8,128)S(1)} %get-tuple-element.34.scale_ref), custom_call_target="tpu_custom_call" | custom-call | flops 262144 | bytes 1048576 | tf_op jit(solution)/shard_map/finish/pallas_call | solution.py:296
  (2 shorter events, 0.0 us)
Async XLA Ops:
  6.5 10.5 %copy-start.1 = (s32[16,2]{0,1:T(2,128)S(1)}, s32[16,2]{0,1:T(2,128)}, u32[]{:S(2)}) copy-start(s32[16,2]{0,1:T(2,128)} %param.3) | copy-start | bytes 388
  6.5 112.7 %reduce-scatter.2.cloned.1.call-start = ((), (), s32[]{:S(2)}) async-start(), calls=%async_computation.1 | async-start | bytes 4456448 | tf_op jit(solution)/shard_map/reduce_scatter | solution.py:326
  10.1 18.7 %collective-permute-start = (f32[512,1024]{1,0:T(8,128)}, f32[512,1024]{1,0:T(8,128)S(1)}, u32[]{:S(2)}, u32[]{:S(2)}) collective-permute-start(f32[512,1024]{1,0:T(8,128)} %get-tuple-element.25), channel_id=1, source_target_pairs={{0,16},{32,48},{64,80},{96,112},{128,144},{160,176},{192,208},{224... | collective-permute-start | bytes 6291464 | tf_op jit(solution)/shard_map/ppermute | solution.py:318
  12.1 20.8 %collective-permute-start.1 = (f32[256,1024]{1,0:T(8,128)}, f32[256,1024]{1,0:T(8,128)S(1)}, u32[]{:S(2)}, u32[]{:S(2)}) collective-permute-start(f32[256,1024]{1,0:T(8,128)} %get-tuple-element.29), channel_id=1, source_target_pairs={{16,32},{48,64},{80,96},{112,128},{144,160},{176,192},{208,224},{2... | collective-permute-start | bytes 3145736 | tf_op jit(solution)/shard_map/ppermute | solution.py:318
  73.0 48.9 %collective-permute-start.4 = (f32[16,2,2,256]{3,2,1,0:T(2,128)S(1)}, f32[16,2,2,256]{3,2,1,0:T(2,128)S(1)}, u32[]{:S(2)}, u32[]{:S(2)}) collective-permute-start(f32[16,2,2,256]{3,2,1,0:T(2,128)S(1)} %get-tuple-element.35), channel_id=1, source_target_pairs={{16,0},{32,16},{48,32},{64,48},{80,64},{96,80},{112,96},{128,112},... | collective-permute-start | bytes 196616 | tf_op jit(solution)/shard_map/ppermute | solution.py:334
  74.9 47.0 %collective-permute-start.3 = (f32[16,2,2,256]{3,2,1,0:T(2,128)S(1)}, f32[16,2,2,256]{3,2,1,0:T(2,128)S(1)}, u32[]{:S(2)}, u32[]{:S(2)}) collective-permute-start(f32[16,2,2,256]{3,2,1,0:T(2,128)S(1)} %get-tuple-element.36), channel_id=1, source_target_pairs={{0,16},{16,32},{32,48},{48,64},{64,80},{80,96},{96,112},{112,128},... | collective-permute-start | bytes 196616 | tf_op jit(solution)/shard_map/ppermute | solution.py:333
  120.0 7.2 %collective-permute-start.2 = (f32[16,256]{1,0:T(8,128)S(1)}, f32[16,256]{1,0:T(8,128)S(1)}, u32[]{:S(2)}, u32[]{:S(2)}) collective-permute-start(f32[16,256]{1,0:T(8,128)S(1)} %slice.13), channel_id=1, source_target_pairs={{16,32},{48,64},{80,96},{112,128},{144,160},{176,192},{208,224},{2... | collective-permute-start | bytes 49160 | tf_op jit(solution)/shard_map/ppermute | solution.py:318
  127.2 1.0 copy-start
Sparse Core Ops, SparseCore 0:
  36.8 82.4 reduce-scatter.1

commit v4 on v3

v4 whole, which is shorter than its diff:
```python
import functools

import jax
import jax.numpy as jnp
from jax import lax
from jax.experimental import pallas as pl
from jax.experimental.pallas import tpu as pltpu
from jax.sharding import PartitionSpec as P

BLK = 256
OWN = 4
EARLY = 10
MADE = 16
PAIRS = 16
HOME = 16
SLOTS = 17
PLACES = 7
AT_ONCE = 10
COST = 1 << 34
SHARDS = 16
ROWS = BLK // SHARDS
F32 = jnp.float32
BF16 = jnp.bfloat16
SMEM = pltpu.SMEM
VMEM = pltpu.VMEM


def split_block(x, parts_ref, place, stats_ref, row):
    count = x.shape[1]
    mean = jnp.sum(x, axis=1, keepdims=True) * (1.0 / count)
    centered = x - mean
    hi = centered.astype(BF16)
    at = 2 * BLK * place
    parts_ref[at : at + BLK, :] = hi
    parts_ref[at + BLK : at + 2 * BLK, :] = (centered - hi.astype(F32)).astype(BF16)
    if stats_ref is None:
        return
    squares = jnp.sum(centered * centered, axis=1, keepdims=True)
    lane = lax.broadcasted_iota(jnp.int32, (BLK, 128), 1)
    both = jnp.where(lane < 8, jnp.broadcast_to(mean, (BLK, 128)), jnp.broadcast_to(squares, (BLK, 128)))
    flat = jnp.transpose(both)
    stats_ref[0, pl.ds(row, 1), :] = flat[0:1, :]
    stats_ref[1, pl.ds(row, 1), :] = flat[8:9, :]


def product(parts_ref, a, b):
    dot = functools.partial(
        lax.dot_general, dimension_numbers=(((1,), (1,)), ((), ())), preferred_element_type=F32
    )
    at = pl.multiple_of(a * (2 * BLK), 2 * BLK)
    by = pl.multiple_of(b * (2 * BLK), 2 * BLK)
    both = dot(parts_ref[pl.ds(at, 2 * BLK), :], parts_ref[pl.ds(by, BLK), :])
    rest = dot(parts_ref[pl.ds(at, BLK), :], parts_ref[pl.ds(by + BLK, BLK), :])
    return both[:BLK] + (both[BLK:] + rest)


def border_kernel(start_ref, x_ref, out_ref, sem):
    copy = pltpu.make_async_copy(x_ref.at[pl.ds(start_ref[0] * BLK, out_ref.shape[0]), :], out_ref, sem)
    copy.start()
    copy.wait()


def border(start, blocks, features, name):
    shots = features.shape[1]
    return pl.pallas_call(
        border_kernel,
        in_specs=[pl.BlockSpec(memory_space=SMEM), pl.BlockSpec(memory_space=pl.ANY)],
        out_specs=pl.BlockSpec(memory_space=VMEM),
        out_shape=jax.ShapeDtypeStruct((blocks * BLK, shots), F32),
        scratch_shapes=[pltpu.SemaphoreType.DMA],
        compiler_params=pltpu.CompilerParams(vmem_limit_bytes=8 << 20),
        cost_estimate=pl.CostEstimate(flops=0, bytes_accessed=blocks << 21, transcendentals=0),
        name=name,
    )(start.reshape(1), pltpu.with_memory_space_constraint(features, pltpu.HBM))


def assign(pairs_ref, base, core, first_ref, second_ref, slot_ref, left_ref, right_ref):
    def kind_of(p):
        second = pairs_ref[p, 1] - base
        own = jnp.logical_and(second >= 0, second < OWN)
        near = jnp.logical_and(second >= -1, second <= OWN)
        with_a = (second < 0) == (core == 0)
        return jnp.where(own, 0, jnp.where(with_a, jnp.where(near, 2, 3), 1))

    first_ref[HOME] = 0
    second_ref[HOME] = 0
    first_ref[15] = jnp.where(core == 0, -1, OWN)
    second_ref[15] = jnp.where(core == 0, 1, 2)
    kinds = [kind_of(p) for p in range(PAIRS)]
    n_in, n_with_b = (sum((kind == k).astype(jnp.int32) for kind in kinds) for k in range(2))
    places = [jnp.int32(0), jnp.int32(EARLY), n_in + n_with_b]
    for p, kind in enumerate(kinds):
        own = places[0] + jnp.where(places[0] >= EARLY, n_with_b, 0)
        place = jnp.where(kind == 0, own, jnp.where(kind == 1, places[1], places[2]))
        slot = jnp.where(kind == 3, HOME, place)
        places = [place + (kind == k).astype(jnp.int32) for k, place in enumerate(places)]
        slot_ref[p] = slot
        first_ref[slot] = pairs_ref[p, 0] - base
        second_ref[slot] = pairs_ref[p, 1] - base

    def place_of(block):
        with_a = (block < 0) == (core == 0)
        beside = jnp.where(with_a, 6, jnp.where(block < 0, block + 6, block))
        return jnp.where(jnp.logical_and(block >= 0, block < OWN), block, beside)

    for slot in range(MADE):
        left_ref[slot] = place_of(first_ref[slot])
        right_ref[slot] = place_of(second_ref[slot])


def fill(start, count, at_once, parts_ref, left_ref, right_ref, tiles_ref, buffers, sems):
    rounds = count // at_once

    def copy(step, k):
        way = lax.rem(step, 2) * at_once + k if rounds > 1 else k
        return pltpu.make_async_copy(buffers.at[way], tiles_ref.at[:, start + step * at_once + k], sems.at[way])

    def body(step, carry):
        slots = [start + step * at_once + k for k in range(at_once)]
        tiles = [product(parts_ref, left_ref[slot], right_ref[slot]) for slot in slots]
        for k, tile in enumerate(tiles):
            pl.when(step >= 2)(lambda: copy(step - 2, k).wait())
            buffers[lax.rem(step, 2) * at_once + k if rounds > 1 else k] = tile.reshape(SHARDS, ROWS, BLK)
            copy(step, k).start()
        return carry

    lax.fori_loop(0, rounds, body, 0)
    for step in range(max(rounds - 2, 0), rounds):
        for k in range(at_once):
            copy(jnp.int32(step), k).wait()


def early_kernel(
    pairs_ref, place_ref, x_ref, tiles_ref, parts_ref, stats_ref, first_ref, second_ref, slot_ref, left_ref, right_ref,
    x_vmem, buffers, in_sems, out_sems,
):
    loads = [
        pltpu.make_async_copy(x_ref.at[pl.ds(k * BLK, BLK), :], x_vmem.at[k], in_sems.at[k]) for k in range(OWN)
    ]
    for load in loads:
        load.start()
    assign(pairs_ref, place_ref[0], place_ref[1], first_ref, second_ref, slot_ref, left_ref, right_ref)
    for k, load in enumerate(loads):
        load.wait()
        split_block(x_vmem[k], parts_ref, k, stats_ref, k)
    fill(0, EARLY, AT_ONCE, parts_ref, left_ref, right_ref, tiles_ref, buffers, out_sems)


def early(pairs, place, features):
    shots = features.shape[1]
    smem, vmem, anywhere = (pl.BlockSpec(memory_space=space) for space in (SMEM, VMEM, pl.ANY))
    numbers = jax.ShapeDtypeStruct((SLOTS,), jnp.int32)
    return pl.pallas_call(
        early_kernel,
        in_specs=[smem, smem, anywhere],
        out_specs=[anywhere, vmem, vmem] + [smem] * 5,
        out_shape=[
            pltpu.HBM((SHARDS, MADE, ROWS, BLK), F32),
            jax.ShapeDtypeStruct((PLACES * 2 * BLK, shots), BF16),
            jax.ShapeDtypeStruct((2, OWN, BLK), F32),
            numbers,
            numbers,
            jax.ShapeDtypeStruct((PAIRS,), jnp.int32),
            numbers,
            numbers,
        ],
        scratch_shapes=[
            VMEM((OWN, BLK, shots), F32),
            VMEM((AT_ONCE, SHARDS, ROWS, BLK), F32),
            pltpu.SemaphoreType.DMA((OWN,)),
            pltpu.SemaphoreType.DMA((AT_ONCE,)),
        ],
        compiler_params=pltpu.CompilerParams(vmem_limit_bytes=24 << 20),
        cost_estimate=pl.CostEstimate(flops=6 * EARLY * BLK * BLK * shots, bytes_accessed=12 << 20, transcendentals=0),
        name="early_tiles",
    )(pairs, place, pltpu.with_memory_space_constraint(features, pltpu.HBM))


def near_kernel(start, place, left_ref, right_ref, halo_ref, _, __, tiles_ref, parts_ref, buffers, sems):
    for k in range(halo_ref.shape[0] // BLK):
        split_block(halo_ref[k * BLK : (k + 1) * BLK, :], parts_ref, place + k, None, None)
    fill(start, 3, 3, parts_ref, left_ref, right_ref, tiles_ref, buffers, sems)


def near(start, place, left, right, halo, parts, tiles, name, cost):
    smem, vmem, anywhere = (pl.BlockSpec(memory_space=space) for space in (SMEM, VMEM, pl.ANY))
    return pl.pallas_call(
        functools.partial(near_kernel, start, place),
        in_specs=[smem, smem, vmem, vmem, anywhere],
        out_specs=[anywhere, vmem],
        out_shape=[pltpu.HBM(tiles.shape, F32), jax.ShapeDtypeStruct(parts.shape, BF16)],
        scratch_shapes=[VMEM((3, SHARDS, ROWS, BLK), F32), pltpu.SemaphoreType.DMA((3,))],
        input_output_aliases={3: 1, 4: 0},
        compiler_params=pltpu.CompilerParams(vmem_limit_bytes=16 << 20),
        cost_estimate=pl.CostEstimate(flops=cost, bytes_accessed=1 << 20, transcendentals=0),
        name=name,
    )(left, right, halo, parts, tiles)


def factors_kernel(
    count, first_ref, second_ref, me_ref, own_ref, below_ref, above_ref, shift_ref, scale_ref, turned, dev, inv
):
    shards = own_ref.shape[0]
    total = shards * count
    stats = jnp.concatenate([below_ref[...], own_ref[...], above_ref[...]], axis=2)
    means, squares = stats[:, 0], stats[:, 1]
    mean = jnp.sum(means, axis=0) * (1.0 / shards)
    away = means - mean[None]
    squares = jnp.sum(squares, axis=0) + count * jnp.sum(away * away, axis=0)
    inverse = lax.rsqrt(squares * (1.0 / total) + 1e-06)
    inv[...] = inverse
    for block in range(8):
        dev[block] = away[:, block, :]
    for block in range(OWN):
        column = jnp.concatenate(
            [away[:, 2 + block, :], jnp.broadcast_to(inverse[2 + block : 3 + block, :], (128 - shards, BLK))], axis=0
        )
        turned[block] = jnp.transpose(column)
    mine = pl.ds(pl.multiple_of(me_ref[0] * ROWS, ROWS), ROWS)
    for slot in range(SLOTS):
        a = jnp.clip(first_ref[slot], 0, OWN - 1)
        b = second_ref[slot] + 2
        left = turned[a, mine, :]
        shift_ref[slot] = count * jnp.dot(
            left[:, :shards], dev[b], precision=lax.Precision.HIGHEST, preferred_element_type=F32
        )
        scale_ref[slot] = left[:, shards : shards + 1] * inv[pl.ds(b, 1), :] * (1.0 / total**0.5)


def factors(count, first, second, me, *stats):
    vmem = pl.BlockSpec(memory_space=VMEM)
    smem = pl.BlockSpec(memory_space=SMEM)
    return pl.pallas_call(
        functools.partial(factors_kernel, count),
        in_specs=[smem] * 3 + [vmem] * 3,
        out_specs=[vmem] * 2,
        out_shape=[jax.ShapeDtypeStruct((SLOTS, ROWS, BLK), F32)] * 2,
        scratch_shapes=[
            VMEM((OWN, BLK, 128), F32),
            VMEM((8, SHARDS, BLK), F32),
            VMEM((8, BLK), F32),
        ],
        compiler_params=pltpu.CompilerParams(vmem_limit_bytes=8 << 20),
        cost_estimate=pl.CostEstimate(flops=1 << 26, bytes_accessed=2 << 20, transcendentals=2048),
        name="factors",
    )(first, second, me, *stats)


def finish_kernel(slot_ref, main_ref, home_ref, shift_ref, scale_ref, out_ref, all_ref):
    all_ref[:MADE] = (main_ref[...] + shift_ref[:MADE]) * scale_ref[:MADE]
    all_ref[HOME] = (home_ref[...] + shift_ref[HOME]) * scale_ref[HOME]
    for p in range(PAIRS):
        out_ref[:, p, :] = all_ref[slot_ref[p]]


def finish(slot, main, home, shift, scale):
    vmem = pl.BlockSpec(memory_space=VMEM)
    return pl.pallas_call(
        finish_kernel,
        in_specs=[pl.BlockSpec(memory_space=SMEM)] + [vmem] * 4,
        out_specs=vmem,
        out_shape=jax.ShapeDtypeStruct((ROWS, PAIRS, BLK), F32),
        scratch_shapes=[VMEM((SLOTS, ROWS, BLK), F32)],
        compiler_params=pltpu.CompilerParams(vmem_limit_bytes=8 << 20),
        cost_estimate=pl.CostEstimate(flops=1 << 18, bytes_accessed=1 << 20, transcendentals=0),
        name="finish",
    )(slot, main, home, shift, scale)


def on_device(features, pairs):
    shots = features.shape[1]
    owners = lax.axis_size("det")
    owner = lax.axis_index("det").astype(jnp.int32)
    core = lax.rem(owner, 2)
    place = jnp.stack([owner * OWN, core])
    me = lax.axis_index("shot").astype(jnp.int32).reshape(1)

    def swap(x, start):
        ends = [(i, i + 1) for i in range(start, owners - 1, 2)]
        return lax.ppermute(x, "det", ends + [(b, a) for a, b in ends])

    to_a = border(3 * core, 1, features, "border_for_a")
    later, to_a = lax.optimization_barrier((2 - 2 * core, to_a))
    from_a = swap(to_a, 1)
    from_b = swap(border(later, 2, features, "border_for_b"), 0)
    tiles, parts, stats, first, second, slot, left, right = early(pairs, place, features)
    tiles, parts = near(EARLY + 3, 6, left, right, from_a, parts, tiles, "tiles_with_a", COST)
    tiles, _ = near(EARLY, 4, left, right, from_b, parts, tiles, "tiles_with_b", COST)
    main = lax.psum_scatter(
        tiles.reshape(SHARDS * MADE * ROWS, BLK), "shot", scatter_dimension=0, tiled=True
    ).reshape(MADE, ROWS, BLK)

    stats, tiles = lax.optimization_barrier((stats, tiles))
    stats = lax.all_gather(stats.reshape(2 * OWN, BLK), "shot").reshape(-1, 2, OWN, BLK)
    up = [(i, i + 1) for i in range(owners - 1)]
    below = lax.ppermute(stats[:, :, 2:], "det", up)
    above = lax.ppermute(stats[:, :, :2], "det", [(b, a) for a, b in up])
    shift, scale = factors(float(shots), first, second, me, stats, below, above)
    return finish(slot, main, swap(main[15], 1), shift, scale)


def solution(mesh):
    in_specs = (P("det", "shot"), P("det", None))
    out_specs = P("shot", "det", None)
    return jax.shard_map(on_device, mesh=mesh, in_specs=in_specs, out_specs=out_specs, check_vma=False)
```

time: 137 us -> 136 us (level)
  starting transfers between devices: 13.1 us -> 15.8 us
  Pallas kernels: 25.7 us -> 23.4 us
    ppermute x1, starting transfers between devices: 1.92 us -> 5.75 us  [on_device(): above = lax.ppermute(stats[:, :, :2], 'det', [(b, a) for a, b in up])]
    pallas_call x1, Pallas kernels: 11.7 us -> 9.47 us  [early(): pl.pallas_call(early_kernel, in_specs=[smem, smem, anywhere], out_specs=[...]
    reduce_scatter x1, waiting for transfers between devices: 42 us -> 39.8 us  [on_device(): lax.psum_scatter(tiles.reshape(SHARDS * MADE * ROWS, BLK), 'shot', scatte...]
    pallas_call x3 -> x4, Pallas kernels: 11.3 us -> 11.2 us  [the longest x2 8.39 us: near(): pl.pallas_call(functools.partial(near_kernel, start, place), in_specs=[sm...]
  transfers between devices with their start and end apart: 6 -> 6, of which waited for: 2 -> 3; matrix products, arithmetic and copies ran while one was open for 1% -> 1% of each run, Pallas kernels for 12% -> 12%
where the time goes in v4:
time: 136 us; the launch traced here: 135 us
  waiting for transfers between devices  44.6 us (33%)
  blocking collectives  36.3 us (27%)
  Pallas kernels  23.4 us (17%)
  starting transfers between devices  15.8 us (12%)
  between operations  13.5 us (10%)
  local copies, waits for them, and re-layouts  1.86 us (1%)
    reduce_scatter x1, waiting for transfers between devices, on_device(): lax.psum_scatter(tiles.reshape(SHARDS * MADE * ROWS, BLK), 'shot', scatte...  39.8 us
    all_gather x1, blocking collectives, on_device(): lax.all_gather(stats.reshape(2 * OWN, BLK), 'shot').reshape(-1, 2, OWN, BLK)  36.3 us
    pallas_call x1, Pallas kernels, early(): pl.pallas_call(early_kernel, in_specs=[smem, smem, anywhere], out_specs=[...  9.47 us
    pallas_call x2, Pallas kernels, near(): pl.pallas_call(functools.partial(near_kernel, start, place), in_specs=[sm...  8.39 us
    ppermute x3, starting transfers between devices, swap(): return lax.ppermute(x, 'det', ends + [(b, a) for a, b in ends])  8.12 us
    ppermute x1, starting transfers between devices, on_device(): above = lax.ppermute(stats[:, :, :2], 'det', [(b, a) for a, b in up])  5.75 us
    ppermute x3, waiting for transfers between devices, swap(): return lax.ppermute(x, 'det', ends + [(b, a) for a, b in ends])  4.77 us
    pallas_call x2, Pallas kernels, border(): pl.pallas_call(border_kernel, in_specs=[pl.BlockSpec(memory_space=SMEM),...  2.84 us
  transfers between devices with their start and end apart: 6, of which 3 were waited for; matrix products, arithmetic and copies ran while one was open for 1% of the time, Pallas kernels for 12%

profile of v4, /device:TPU:24, one launch (start us, length us, event | category | flops | bytes accessed | tf_op | source)
XLA Modules:
  0.0 135.5 jit_solution(12386009571039260872)
XLA Ops:
  6.5 0.0 reduce-scatter.2.cloned.1.call-start
  6.5 1.2 border_for_a.1
  7.8 0.0 copy-start.1
  7.8 4.3 %collective-permute-start.1 = (f32[256,1024]{1,0:T(8,128)S(1)}, f32[256,1024]{1,0:T(8,128)}, u32[]{:S(2)}, u32[]{:S(2)}) collective-permute-start(f32[256,1024]{1,0:T(8,128)S(1)} %border_for_a.1), channel_id=1, source_target_pairs={{16,32},{48,64},{80,96},{112,128},{144,160},{176,192},{208,224},{2... | collective-permute-start | bytes 3145736 | tf_op jit(solution)/shard_map/ppermute | solution.py:280
  12.1 1.6 %border_for_b.1 = f32[512,1024]{1,0:T(8,128)S(1)} custom-call(s32[1]{0:T(128)} %bitcast.3.start_ref, f32[1024,1024]{1,0:T(8,128)} %x_ref.5), custom_call_target="tpu_custom_call" | custom-call | bytes 4194304 | tf_op jit(solution)/shard_map/border_for_b/pallas_call | solution.py:65
  13.7 1.9 %collective-permute-start = (f32[512,1024]{1,0:T(8,128)S(1)}, f32[512,1024]{1,0:T(8,128)}, u32[]{:S(2)}, u32[]{:S(2)}) collective-permute-start(f32[512,1024]{1,0:T(8,128)S(1)} %border_for_b.1), channel_id=1, source_target_pairs={{0,16},{32,48},{64,80},{96,112},{128,144},{160,176},{192,208},{224... | collective-permute-start | bytes 6291464 | tf_op jit(solution)/shard_map/ppermute | solution.py:280
  15.6 0.0 copy-done.1
  15.6 0.1 copy.8.pairs_ref
  15.7 0.1 pad_add_fusion.place_ref
  15.8 9.5 %early_tiles.1 = (f32[16,16,16,256]{3,2,1,0:T(8,128)}, bf16[3584,1024]{1,0:T(8,128)(2,1)S(1)}, f32[2,4,256]{2,1,0:T(4,128)S(1)}, s32[17]{0:T(128)S(1)}, s32[17]{...) custom-call(s32[16,2]{1,0:T(8,128)S(1)} %copy.8.pairs_ref, s32[2]{0:T(128)S(1)} %pad_add_fusion.place_ref, ...), custom_call_target="tpu_custom_call" | custom-call | flops 4026531840 | bytes 12582912 | tf_op jit(solution)/shard_map/early_tiles/pallas_call | solution.py:153
  25.3 0.8 collective-permute-done.1.halo_ref
  26.1 3.9 %tiles_with_a.1 = (f32[16,16,16,256]{3,2,1,0:T(8,128)}, bf16[3584,1024]{1,0:T(8,128)(2,1)S(1)}) custom-call(s32[17]{0:T(128)S(1)} %get-tuple-element.22.left_ref, s32[17]{0:T(128)S(1)} %get-tuple-element.23.right_ref, f32[256,1024]{1,0:T(8,128)} %collective-permute-done.1.halo_ref, ...), custom_call_target="tpu_custom_call", output_to_operand_aliasing={{1}: (3, {}), {0}: (4, {})} | custom-call | flops 17179869184 | bytes 1048576 | tf_op jit(solution)/shard_map/tiles_with_a/pallas_call | solution.py:187
  30.0 0.0 collective-permute-done.halo_ref
  30.0 4.5 %tiles_with_b.1 = (f32[16,16,16,256]{3,2,1,0:T(8,128)}, bf16[3584,1024]{1,0:T(8,128)(2,1)S(1)}) custom-call(s32[17]{0:T(128)S(1)} %get-tuple-element.22.left_ref, s32[17]{0:T(128)S(1)} %get-tuple-element.23.right_ref, f32[512,1024]{1,0:T(8,128)} %collective-permute-done.halo_ref, ...), custom_call_target="tpu_custom_call", output_to_operand_aliasing={{1}: (3, {}), {0}: (4, {})} | custom-call | flops 17179869184 | bytes 1048576 | tf_op jit(solution)/shard_map/tiles_with_b/pallas_call | solution.py:187
  34.5 0.0 reduce-scatter.2.cloned.1.call-update
  34.6 36.3 %all_gather.3 = f32[16,8,256]{2,1,0:T(8,128)S(1)} all-gather(f32[1,8,256]{2,1,0:T(8,128)S(1)} %all_gather_reshape.3), channel_id=1, replica_groups=mesh['det'=32,'shot'=16] {'shot'}, dimensions={0}, use_global_device_ids=true | all-gather | bytes 139264 | tf_op jit(solution)/shard_map/all_gather | solution.py:294
  70.9 0.1 fusion
  70.9 1.9 %collective-permute-start.3 = (f32[16,2,2,256]{3,2,1,0:T(2,128)S(1)}, f32[16,2,2,256]{3,2,1,0:T(2,128)S(1)}, u32[]{:S(2)}, u32[]{:S(2)}) collective-permute-start(f32[16,2,2,256]{3,2,1,0:T(2,128)S(1)} %get-tuple-element.38), channel_id=1, source_target_pairs={{0,16},{16,32},{32,48},{48,64},{64,80},{80,96},{96,112},{112,128},... | collective-permute-start | bytes 196616 | tf_op jit(solution)/shard_map/ppermute | solution.py:296
  72.9 5.8 %collective-permute-start.4 = (f32[16,2,2,256]{3,2,1,0:T(2,128)S(1)}, f32[16,2,2,256]{3,2,1,0:T(2,128)S(1)}, u32[]{:S(2)}, u32[]{:S(2)}) collective-permute-start(f32[16,2,2,256]{3,2,1,0:T(2,128)S(1)} %get-tuple-element.37), channel_id=1, source_target_pairs={{16,0},{32,16},{48,32},{64,48},{80,64},{96,80},{112,96},{128,112},... | collective-permute-start | bytes 196616 | tf_op jit(solution)/shard_map/ppermute | solution.py:297
  78.6 39.8 %reduce-scatter.2.cloned.1.call-done = f32[256,256]{1,0:T(8,128)} async-done(((f32[4096,256]{1,0:T(8,128)}), f32[256,256]{1,0:T(8,128)}) %reduce-scatter.2.cloned.1.call-update) | async-done | bytes 262160 | tf_op jit(solution)/shard_map/reduce_scatter | solution.py:289
  118.4 0.7 slice.13
  119.1 1.9 %collective-permute-start.2 = (f32[16,256]{1,0:T(8,128)S(1)}, f32[16,256]{1,0:T(8,128)S(1)}, u32[]{:S(2)}, u32[]{:S(2)}) collective-permute-start(f32[16,256]{1,0:T(8,128)S(1)} %slice.13), channel_id=1, source_target_pairs={{16,32},{48,64},{80,96},{112,128},{144,160},{176,192},{208,224},{2... | collective-permute-start | bytes 49160 | tf_op jit(solution)/shard_map/ppermute | solution.py:280
  121.0 0.0 collective-permute-done.3.below_ref
  121.1 0.0 collective-permute-done.4.above_ref
  121.1 1.3 factors.1
  122.4 3.9 %collective-permute-done.2.home_ref = f32[16,256]{1,0:T(8,128)S(1)} collective-permute-done((f32[16,256]{1,0:T(8,128)S(1)}, f32[16,256]{1,0:T(8,128)S(1)}, u32[]{:S(2)}, u32[]{:S(2)}) %collective-permute-start.2) | collective-permute-done | bytes 16416 | tf_op jit(solution)/shard_map/ppermute | solution.py:280
  126.3 0.0 copy-start
  126.3 0.9 copy-done
  127.2 1.4 %finish.1 = f32[16,16,256]{2,1,0:T(8,128)} custom-call(s32[16]{0:T(128)S(1)} %get-tuple-element.21.slot_ref, f32[16,16,256]{2,1,0:T(8,128)S(1)} %bitcast.7, f32[16,256]{1,0:T(8,128)S(1)} %collective-permute-done.2.home_ref, f32[17,16,256]{2,1,0:T(8,128)S(1)} %get-tuple-element.35.shift_ref, f32[17,16,256]{2,1,0:T(8,128)S(1)} %get-tuple-element.36.scale_ref), custom_call_target="tpu_custom_call" | custom-call | flops 262144 | bytes 1048576 | tf_op jit(solution)/shard_map/finish/pallas_call | solution.py:258
  (2 shorter events, 0.0 us)
Async XLA Ops:
  6.5 111.9 %reduce-scatter.2.cloned.1.call-start = ((), (), s32[]{:S(2)}) async-start(), calls=%async_computation.1 | async-start | bytes 4456448 | tf_op jit(solution)/shard_map/reduce_scatter | solution.py:289
  7.8 7.9 %copy-start.1 = (s32[16,2]{0,1:T(2,128)S(1)}, s32[16,2]{0,1:T(2,128)}, u32[]{:S(2)}) copy-start(s32[16,2]{0,1:T(2,128)} %param.3) | copy-start | bytes 388
  7.8 18.3 %collective-permute-start.1 = (f32[256,1024]{1,0:T(8,128)S(1)}, f32[256,1024]{1,0:T(8,128)}, u32[]{:S(2)}, u32[]{:S(2)}) collective-permute-start(f32[256,1024]{1,0:T(8,128)S(1)} %border_for_a.1), channel_id=1, source_target_pairs={{16,32},{48,64},{80,96},{112,128},{144,160},{176,192},{208,224},{2... | collective-permute-start | bytes 3145736 | tf_op jit(solution)/shard_map/ppermute | solution.py:280
  13.7 16.3 %collective-permute-start = (f32[512,1024]{1,0:T(8,128)S(1)}, f32[512,1024]{1,0:T(8,128)}, u32[]{:S(2)}, u32[]{:S(2)}) collective-permute-start(f32[512,1024]{1,0:T(8,128)S(1)} %border_for_b.1), channel_id=1, source_target_pairs={{0,16},{32,48},{64,80},{96,112},{128,144},{160,176},{192,208},{224... | collective-permute-start | bytes 6291464 | tf_op jit(solution)/shard_map/ppermute | solution.py:280
  70.9 50.1 %collective-permute-start.3 = (f32[16,2,2,256]{3,2,1,0:T(2,128)S(1)}, f32[16,2,2,256]{3,2,1,0:T(2,128)S(1)}, u32[]{:S(2)}, u32[]{:S(2)}) collective-permute-start(f32[16,2,2,256]{3,2,1,0:T(2,128)S(1)} %get-tuple-element.38), channel_id=1, source_target_pairs={{0,16},{16,32},{32,48},{48,64},{64,80},{80,96},{96,112},{112,128},... | collective-permute-start | bytes 196616 | tf_op jit(solution)/shard_map/ppermute | solution.py:296
  72.9 48.2 %collective-permute-start.4 = (f32[16,2,2,256]{3,2,1,0:T(2,128)S(1)}, f32[16,2,2,256]{3,2,1,0:T(2,128)S(1)}, u32[]{:S(2)}, u32[]{:S(2)}) collective-permute-start(f32[16,2,2,256]{3,2,1,0:T(2,128)S(1)} %get-tuple-element.37), channel_id=1, source_target_pairs={{16,0},{32,16},{48,32},{64,48},{80,64},{96,80},{112,96},{128,112},... | collective-permute-start | bytes 196616 | tf_op jit(solution)/shard_map/ppermute | solution.py:297
  119.1 7.2 %collective-permute-start.2 = (f32[16,256]{1,0:T(8,128)S(1)}, f32[16,256]{1,0:T(8,128)S(1)}, u32[]{:S(2)}, u32[]{:S(2)}) collective-permute-start(f32[16,256]{1,0:T(8,128)S(1)} %slice.13), channel_id=1, source_target_pairs={{16,32},{48,64},{80,96},{112,128},{144,160},{176,192},{208,224},{2... | collective-permute-start | bytes 49160 | tf_op jit(solution)/shard_map/ppermute | solution.py:280
  126.3 1.0 copy-start
Sparse Core Ops, SparseCore 0:
  34.7 83.6 reduce-scatter.1

commit v5 on v4

--- a/solution.py
+++ b/solution.py
@@ -15,8 +15,9 @@
 HOME = 16
 SLOTS = 17
 PLACES = 7
-AT_ONCE = 10
-COST = 1 << 34
+EARLY_GROUPS = (4, 3, 3)
+NEAR_GROUPS = (3, 3)
+SPLIT_COST = 1 << 34
 SHARDS = 16
 ROWS = BLK // SHARDS
 F32 = jnp.float32
@@ -54,20 +55,34 @@
     return both[:BLK] + (both[BLK:] + rest)
 
 
-def border_kernel(start_ref, x_ref, out_ref, sem):
-    copy = pltpu.make_async_copy(x_ref.at[pl.ds(start_ref[0] * BLK, out_ref.shape[0]), :], out_ref, sem)
-    copy.start()
-    copy.wait()
+def border_kernel(start_ref, x_ref, out_ref, held, in_sems, out_sems):
+    rows = held.shape[1]
+    loads, stores = [], []
+    for k in range(held.shape[0]):
+        here = pl.ds(pl.multiple_of(start_ref[0] * BLK + k * rows, rows), rows)
+        loads.append(pltpu.make_async_copy(x_ref.at[here, :], held.at[k], in_sems.at[k]))
+        stores.append(pltpu.make_async_copy(held.at[k], out_ref.at[pl.ds(k * rows, rows), :], out_sems.at[k]))
+        loads[k].start()
+    for load, store in zip(loads, stores):
+        load.wait()
+        store.start()
+    for store in stores:
+        store.wait()
 
 
 def border(start, blocks, features, name):
     shots = features.shape[1]
+    pieces = 4
     return pl.pallas_call(
         border_kernel,
         in_specs=[pl.BlockSpec(memory_space=SMEM), pl.BlockSpec(memory_space=pl.ANY)],
-        out_specs=pl.BlockSpec(memory_space=VMEM),
-        out_shape=jax.ShapeDtypeStruct((blocks * BLK, shots), F32),
-        scratch_shapes=[pltpu.SemaphoreType.DMA],
+        out_specs=pl.BlockSpec(memory_space=pl.ANY),
+        out_shape=pltpu.HBM((blocks * BLK, shots), F32),
+        scratch_shapes=[
+            VMEM((pieces, blocks * BLK // pieces, shots), F32),
+            pltpu.SemaphoreType.DMA((pieces,)),
+            pltpu.SemaphoreType.DMA((pieces,)),
+        ],
         compiler_params=pltpu.CompilerParams(vmem_limit_bytes=8 << 20),
         cost_estimate=pl.CostEstimate(flops=0, bytes_accessed=blocks << 21, transcendentals=0),
         name=name,
@@ -108,26 +123,20 @@
         right_ref[slot] = place_of(second_ref[slot])
 
 
-def fill(start, count, at_once, parts_ref, left_ref, right_ref, tiles_ref, buffers, sems):
-    rounds = count // at_once
-
-    def copy(step, k):
-        way = lax.rem(step, 2) * at_once + k if rounds > 1 else k
-        return pltpu.make_async_copy(buffers.at[way], tiles_ref.at[:, start + step * at_once + k], sems.at[way])
-
-    def body(step, carry):
-        slots = [start + step * at_once + k for k in range(at_once)]
-        tiles = [product(parts_ref, left_ref[slot], right_ref[slot]) for slot in slots]
-        for k, tile in enumerate(tiles):
-            pl.when(step >= 2)(lambda: copy(step - 2, k).wait())
-            buffers[lax.rem(step, 2) * at_once + k if rounds > 1 else k] = tile.reshape(SHARDS, ROWS, BLK)
-            copy(step, k).start()
-        return carry
-
-    lax.fori_loop(0, rounds, body, 0)
-    for step in range(max(rounds - 2, 0), rounds):
-        for k in range(at_once):
-            copy(jnp.int32(step), k).wait()
+def fill(start, counts, parts_ref, left_ref, right_ref, tiles_ref, buffers, sems):
+    def copy(k):
+        return pltpu.make_async_copy(buffers.at[k], tiles_ref.at[:, start + k], sems.at[k])
+
+    done = 0
+    for count in counts:
+        group = range(done, done + count)
+        tiles = [product(parts_ref, left_ref[start + k], right_ref[start + k]) for k in group]
+        for k, tile in zip(group, tiles):
+            buffers[k] = tile.reshape(SHARDS, ROWS, BLK)
+            copy(k).start()
+        done += count
+    for k in range(done):
+        copy(k).wait()
 
 
 def early_kernel(
@@ -143,7 +152,7 @@
     for k, load in enumerate(loads):
         load.wait()
         split_block(x_vmem[k], parts_ref, k, stats_ref, k)
-    fill(0, EARLY, AT_ONCE, parts_ref, left_ref, right_ref, tiles_ref, buffers, out_sems)
+    fill(0, EARLY_GROUPS, parts_ref, left_ref, right_ref, tiles_ref, buffers, out_sems)
 
 
 def early(pairs, place, features):
@@ -166,9 +175,9 @@
         ],
         scratch_shapes=[
             VMEM((OWN, BLK, shots), F32),
-            VMEM((AT_ONCE, SHARDS, ROWS, BLK), F32),
+            VMEM((EARLY, SHARDS, ROWS, BLK), F32),
             pltpu.SemaphoreType.DMA((OWN,)),
-            pltpu.SemaphoreType.DMA((AT_ONCE,)),
+            pltpu.SemaphoreType.DMA((EARLY,)),
         ],
         compiler_params=pltpu.CompilerParams(vmem_limit_bytes=24 << 20),
         cost_estimate=pl.CostEstimate(flops=6 * EARLY * BLK * BLK * shots, bytes_accessed=12 << 20, transcendentals=0),
@@ -176,24 +185,45 @@
     )(pairs, place, pltpu.with_memory_space_constraint(features, pltpu.HBM))
 
 
-def near_kernel(start, place, left_ref, right_ref, halo_ref, _, __, tiles_ref, parts_ref, buffers, sems):
-    for k in range(halo_ref.shape[0] // BLK):
-        split_block(halo_ref[k * BLK : (k + 1) * BLK, :], parts_ref, place + k, None, None)
-    fill(start, 3, 3, parts_ref, left_ref, right_ref, tiles_ref, buffers, sems)
-
-
-def near(start, place, left, right, halo, parts, tiles, name, cost):
+def split_kernel(place, halo_ref, _, parts_ref):
+    split_block(halo_ref[...], parts_ref, place, None, None)
+
+
+def split(place, halo, parts):
+    vmem = pl.BlockSpec(memory_space=VMEM)
+    return pl.pallas_call(
+        functools.partial(split_kernel, place),
+        in_specs=[vmem, vmem],
+        out_specs=vmem,
+        out_shape=jax.ShapeDtypeStruct(parts.shape, BF16),
+        input_output_aliases={1: 0},
+        compiler_params=pltpu.CompilerParams(vmem_limit_bytes=8 << 20),
+        cost_estimate=pl.CostEstimate(flops=SPLIT_COST, bytes_accessed=1 << 20, transcendentals=0),
+        name="split_a",
+    )(halo, parts)
+
+
+def near_kernel(left_ref, right_ref, halo_ref, _, __, tiles_ref, parts_ref, buffers, sems):
+    for k in range(2):
+        split_block(halo_ref[k * BLK : (k + 1) * BLK, :], parts_ref, OWN + k, None, None)
+    fill(EARLY, NEAR_GROUPS, parts_ref, left_ref, right_ref, tiles_ref, buffers, sems)
+
+
+def near(left, right, halo, parts, tiles):
     smem, vmem, anywhere = (pl.BlockSpec(memory_space=space) for space in (SMEM, VMEM, pl.ANY))
-    return pl.pallas_call(
-        functools.partial(near_kernel, start, place),
+    count = MADE - EARLY
+    return pl.pallas_call(
+        near_kernel,
         in_specs=[smem, smem, vmem, vmem, anywhere],
         out_specs=[anywhere, vmem],
         out_shape=[pltpu.HBM(tiles.shape, F32), jax.ShapeDtypeStruct(parts.shape, BF16)],
-        scratch_shapes=[VMEM((3, SHARDS, ROWS, BLK), F32), pltpu.SemaphoreType.DMA((3,))],
+        scratch_shapes=[VMEM((count, SHARDS, ROWS, BLK), F32), pltpu.SemaphoreType.DMA((count,))],
         input_output_aliases={3: 1, 4: 0},
         compiler_params=pltpu.CompilerParams(vmem_limit_bytes=16 << 20),
-        cost_estimate=pl.CostEstimate(flops=cost, bytes_accessed=1 << 20, transcendentals=0),
-        name=name,
+        cost_estimate=pl.CostEstimate(
+            flops=6 * count * BLK * BLK * halo.shape[1], bytes_accessed=5 << 20, transcendentals=0
+        ),
+        name="near_tiles",
     )(left, right, halo, parts, tiles)
 
 
@@ -284,8 +314,8 @@
     from_a = swap(to_a, 1)
     from_b = swap(border(later, 2, features, "border_for_b"), 0)
     tiles, parts, stats, first, second, slot, left, right = early(pairs, place, features)
-    tiles, parts = near(EARLY + 3, 6, left, right, from_a, parts, tiles, "tiles_with_a", COST)
-    tiles, _ = near(EARLY, 4, left, right, from_b, parts, tiles, "tiles_with_b", COST)
+    parts = split(6, from_a, parts)
+    tiles, _ = near(left, right, from_b, parts, tiles)
     main = lax.psum_scatter(
         tiles.reshape(SHARDS * MADE * ROWS, BLK), "shot", scatter_dimension=0, tiled=True
     ).reshape(MADE, ROWS, BLK)

time: 136 us -> 133 us (0.978)
  starting transfers between devices: 15.8 us -> 12.4 us
  waiting for transfers between devices: 44.6 us -> 47 us
  Pallas kernels: 23.4 us -> 21.6 us
    ppermute x1, starting transfers between devices: 5.75 us -> 1.92 us  [on_device(): above = lax.ppermute(stats[:, :, :2], 'det', [(b, a) for a, b in up])]
    pallas_call x2, Pallas kernels: 8.39 us -> 4.99 us  [the longest x1 4.74 us: near(): pl.pallas_call(near_kernel, in_specs=[smem, smem, vmem, vmem, anywhere],...]
    reduce_scatter x1, waiting for transfers between devices: 39.8 us -> 42.9 us  [on_device(): lax.psum_scatter(tiles.reshape(SHARDS * MADE * ROWS, BLK), 'shot', scatte...]
    pallas_call x2, Pallas kernels: 2.84 us -> 4.46 us  [border(): pl.pallas_call(border_kernel, in_specs=[pl.BlockSpec(memory_space=SMEM),...]
  transfers between devices with their start and end apart: 6 -> 6, of which waited for: 3 -> 3; matrix products, arithmetic and copies ran while one was open for 1% -> 1% of each run, Pallas kernels for 12% -> 10%
where the time goes in v5:
time: 133 us
  waiting for transfers between devices  47 us (35%)
  blocking collectives  36.3 us (27%)
  Pallas kernels  21.6 us (16%)
  between operations  13.5 us (10%)
  starting transfers between devices  12.4 us (9%)
  local copies, waits for them, and re-layouts  1.86 us (1%)
    reduce_scatter x1, waiting for transfers between devices, on_device(): lax.psum_scatter(tiles.reshape(SHARDS * MADE * ROWS, BLK), 'shot', scatte...  42.9 us
    all_gather x1, blocking collectives, on_device(): lax.all_gather(stats.reshape(2 * OWN, BLK), 'shot').reshape(-1, 2, OWN, BLK)  36.3 us
    pallas_call x1, Pallas kernels, early(): pl.pallas_call(early_kernel, in_specs=[smem, smem, anywhere], out_specs=[...  9.44 us
    ppermute x3, starting transfers between devices, swap(): return lax.ppermute(x, 'det', ends + [(b, a) for a, b in ends])  8.11 us
    pallas_call x1, Pallas kernels, near(): pl.pallas_call(near_kernel, in_specs=[smem, smem, vmem, vmem, anywhere],...  4.74 us
    pallas_call x2, Pallas kernels, border(): pl.pallas_call(border_kernel, in_specs=[pl.BlockSpec(memory_space=SMEM),...  4.46 us
    ppermute x3, waiting for transfers between devices, swap(): return lax.ppermute(x, 'det', ends + [(b, a) for a, b in ends])  4.08 us
  transfers between devices with their start and end apart: 6, of which 3 were waited for; matrix products, arithmetic and copies ran while one was open for 1% of the time, Pallas kernels for 10%

profile of v5, /device:TPU:24, one launch (start us, length us, event | category | flops | bytes accessed | tf_op | source)
XLA Modules:
  0.0 132.8 jit_solution(13759045377776059569)
XLA Ops:
  6.5 0.0 reduce-scatter.2.cloned.1.call-start
  6.5 2.0 %border_for_a.1 = f32[256,1024]{1,0:T(8,128)} custom-call(s32[1]{0:T(128)} %bitcast.2.start_ref, f32[1024,1024]{1,0:T(8,128)} %x_ref.5), custom_call_target="tpu_custom_call" | custom-call | bytes 2097152 | tf_op jit(solution)/shard_map/border_for_a/pallas_call | solution.py:76
  8.6 0.0 copy-start.1
  8.6 4.3 %collective-permute-start.1 = (f32[256,1024]{1,0:T(8,128)}, f32[256,1024]{1,0:T(8,128)S(1)}, u32[]{:S(2)}, u32[]{:S(2)}) collective-permute-start(f32[256,1024]{1,0:T(8,128)} %border_for_a.1), channel_id=1, source_target_pairs={{16,32},{48,64},{80,96},{112,128},{144,160},{176,192},{208,224},{2... | collective-permute-start | bytes 3145736 | tf_op jit(solution)/shard_map/ppermute | solution.py:310
  12.9 2.4 %border_for_b.1 = f32[512,1024]{1,0:T(8,128)} custom-call(s32[1]{0:T(128)} %bitcast.3.start_ref, f32[1024,1024]{1,0:T(8,128)} %x_ref.5), custom_call_target="tpu_custom_call" | custom-call | bytes 4194304 | tf_op jit(solution)/shard_map/border_for_b/pallas_call | solution.py:76
  15.3 1.9 %collective-permute-start = (f32[512,1024]{1,0:T(8,128)}, f32[512,1024]{1,0:T(8,128)S(1)}, u32[]{:S(2)}, u32[]{:S(2)}) collective-permute-start(f32[512,1024]{1,0:T(8,128)} %border_for_b.1), channel_id=1, source_target_pairs={{0,16},{32,48},{64,80},{96,112},{128,144},{160,176},{192,208},{224... | collective-permute-start | bytes 6291464 | tf_op jit(solution)/shard_map/ppermute | solution.py:310
  17.2 0.0 copy-done.1
  17.3 0.1 copy.7.pairs_ref
  17.3 0.1 pad_add_fusion.place_ref
  17.4 9.4 %early_tiles.1 = (f32[16,16,16,256]{3,2,1,0:T(8,128)}, bf16[3584,1024]{1,0:T(8,128)(2,1)S(1)}, f32[2,4,256]{2,1,0:T(4,128)S(1)}, s32[17]{0:T(128)S(1)}, s32[17]{...) custom-call(s32[16,2]{1,0:T(8,128)S(1)} %copy.7.pairs_ref, s32[2]{0:T(128)S(1)} %pad_add_fusion.place_ref, ...), custom_call_target="tpu_custom_call" | custom-call | flops 4026531840 | bytes 12582912 | tf_op jit(solution)/shard_map/early_tiles/pallas_call | solution.py:162
  26.9 0.2 collective-permute-done.1.halo_ref
  27.0 0.2 split_a.1._
  27.3 0.0 collective-permute-done.halo_ref
  27.3 4.7 %near_tiles.1 = (f32[16,16,16,256]{3,2,1,0:T(8,128)}, bf16[3584,1024]{1,0:T(8,128)(2,1)S(1)}) custom-call(s32[17]{0:T(128)S(1)} %get-tuple-element.20.left_ref, s32[17]{0:T(128)S(1)} %get-tuple-element.21.right_ref, f32[512,1024]{1,0:T(8,128)S(1)} %collective-permute-done.halo_ref, ...), custom_call_target="tpu_custom_call", output_to_operand_aliasing={{1}: (3, {}), {0}: (4, {})} | custom-call | flops 2415919104 | bytes 5242880 | tf_op jit(solution)/shard_map/near_tiles/pallas_call | solution.py:215
  32.0 0.0 reduce-scatter.2.cloned.1.call-update
  32.1 36.3 %all_gather.3 = f32[16,8,256]{2,1,0:T(8,128)S(1)} all-gather(f32[1,8,256]{2,1,0:T(8,128)S(1)} %all_gather_reshape.3), channel_id=1, replica_groups=mesh['det'=32,'shot'=16] {'shot'}, dimensions={0}, use_global_device_ids=true | all-gather | bytes 139264 | tf_op jit(solution)/shard_map/all_gather | solution.py:324
  68.4 0.1 fusion
  68.4 1.9 %collective-permute-start.4 = (f32[16,2,2,256]{3,2,1,0:T(2,128)S(1)}, f32[16,2,2,256]{3,2,1,0:T(2,128)S(1)}, u32[]{:S(2)}, u32[]{:S(2)}) collective-permute-start(f32[16,2,2,256]{3,2,1,0:T(2,128)S(1)} %get-tuple-element.33), channel_id=1, source_target_pairs={{16,0},{32,16},{48,32},{64,48},{80,64},{96,80},{112,96},{128,112},... | collective-permute-start | bytes 196616 | tf_op jit(solution)/shard_map/ppermute | solution.py:327
  70.4 2.4 %collective-permute-start.3 = (f32[16,2,2,256]{3,2,1,0:T(2,128)S(1)}, f32[16,2,2,256]{3,2,1,0:T(2,128)S(1)}, u32[]{:S(2)}, u32[]{:S(2)}) collective-permute-start(f32[16,2,2,256]{3,2,1,0:T(2,128)S(1)} %get-tuple-element.34), channel_id=1, source_target_pairs={{0,16},{16,32},{32,48},{48,64},{64,80},{80,96},{96,112},{112,128},... | collective-permute-start | bytes 196616 | tf_op jit(solution)/shard_map/ppermute | solution.py:326
  72.8 42.9 %reduce-scatter.2.cloned.1.call-done = f32[256,256]{1,0:T(8,128)} async-done(((f32[4096,256]{1,0:T(8,128)}), f32[256,256]{1,0:T(8,128)}) %reduce-scatter.2.cloned.1.call-update) | async-done | bytes 262160 | tf_op jit(solution)/shard_map/reduce_scatter | solution.py:319
  115.7 0.7 slice.13
  116.4 1.9 %collective-permute-start.2 = (f32[16,256]{1,0:T(8,128)S(1)}, f32[16,256]{1,0:T(8,128)S(1)}, u32[]{:S(2)}, u32[]{:S(2)}) collective-permute-start(f32[16,256]{1,0:T(8,128)S(1)} %slice.13), channel_id=1, source_target_pairs={{16,32},{48,64},{80,96},{112,128},{144,160},{176,192},{208,224},{2... | collective-permute-start | bytes 49160 | tf_op jit(solution)/shard_map/ppermute | solution.py:310
  118.4 0.0 collective-permute-done.4.above_ref
  118.4 0.0 collective-permute-done.3.below_ref
  118.4 1.3 factors.1
  119.7 3.9 %collective-permute-done.2.home_ref = f32[16,256]{1,0:T(8,128)S(1)} collective-permute-done((f32[16,256]{1,0:T(8,128)S(1)}, f32[16,256]{1,0:T(8,128)S(1)}, u32[]{:S(2)}, u32[]{:S(2)}) %collective-permute-start.2) | collective-permute-done | bytes 16416 | tf_op jit(solution)/shard_map/ppermute | solution.py:310
  123.6 0.0 copy-start
  123.6 0.9 copy-done
  124.5 1.4 %finish.1 = f32[16,16,256]{2,1,0:T(8,128)} custom-call(s32[16]{0:T(128)S(1)} %get-tuple-element.19.slot_ref, f32[16,16,256]{2,1,0:T(8,128)S(1)} %bitcast.7, f32[16,256]{1,0:T(8,128)S(1)} %collective-permute-done.2.home_ref, f32[17,16,256]{2,1,0:T(8,128)S(1)} %get-tuple-element.31.shift_ref, f32[17,16,256]{2,1,0:T(8,128)S(1)} %get-tuple-element.32.scale_ref), custom_call_target="tpu_custom_call" | custom-call | flops 262144 | bytes 1048576 | tf_op jit(solution)/shard_map/finish/pallas_call | solution.py:288
  (2 shorter events, 0.0 us)
Async XLA Ops:
  6.5 109.2 %reduce-scatter.2.cloned.1.call-start = ((), (), s32[]{:S(2)}) async-start(), calls=%async_computation.1 | async-start | bytes 4456448 | tf_op jit(solution)/shard_map/reduce_scatter | solution.py:319
  8.6 8.7 %copy-start.1 = (s32[16,2]{0,1:T(2,128)S(1)}, s32[16,2]{0,1:T(2,128)}, u32[]{:S(2)}) copy-start(s32[16,2]{0,1:T(2,128)} %param.3) | copy-start | bytes 388
  8.6 18.4 %collective-permute-start.1 = (f32[256,1024]{1,0:T(8,128)}, f32[256,1024]{1,0:T(8,128)S(1)}, u32[]{:S(2)}, u32[]{:S(2)}) collective-permute-start(f32[256,1024]{1,0:T(8,128)} %border_for_a.1), channel_id=1, source_target_pairs={{16,32},{48,64},{80,96},{112,128},{144,160},{176,192},{208,224},{2... | collective-permute-start | bytes 3145736 | tf_op jit(solution)/shard_map/ppermute | solution.py:310
  15.3 12.0 %collective-permute-start = (f32[512,1024]{1,0:T(8,128)}, f32[512,1024]{1,0:T(8,128)S(1)}, u32[]{:S(2)}, u32[]{:S(2)}) collective-permute-start(f32[512,1024]{1,0:T(8,128)} %border_for_b.1), channel_id=1, source_target_pairs={{0,16},{32,48},{64,80},{96,112},{128,144},{160,176},{192,208},{224... | collective-permute-start | bytes 6291464 | tf_op jit(solution)/shard_map/ppermute | solution.py:310
  68.4 49.9 %collective-permute-start.4 = (f32[16,2,2,256]{3,2,1,0:T(2,128)S(1)}, f32[16,2,2,256]{3,2,1,0:T(2,128)S(1)}, u32[]{:S(2)}, u32[]{:S(2)}) collective-permute-start(f32[16,2,2,256]{3,2,1,0:T(2,128)S(1)} %get-tuple-element.33), channel_id=1, source_target_pairs={{16,0},{32,16},{48,32},{64,48},{80,64},{96,80},{112,96},{128,112},... | collective-permute-start | bytes 196616 | tf_op jit(solution)/shard_map/ppermute | solution.py:327
  70.4 48.0 %collective-permute-start.3 = (f32[16,2,2,256]{3,2,1,0:T(2,128)S(1)}, f32[16,2,2,256]{3,2,1,0:T(2,128)S(1)}, u32[]{:S(2)}, u32[]{:S(2)}) collective-permute-start(f32[16,2,2,256]{3,2,1,0:T(2,128)S(1)} %get-tuple-element.34), channel_id=1, source_target_pairs={{0,16},{16,32},{32,48},{48,64},{64,80},{80,96},{96,112},{112,128},... | collective-permute-start | bytes 196616 | tf_op jit(solution)/shard_map/ppermute | solution.py:326
  116.4 7.2 %collective-permute-start.2 = (f32[16,256]{1,0:T(8,128)S(1)}, f32[16,256]{1,0:T(8,128)S(1)}, u32[]{:S(2)}, u32[]{:S(2)}) collective-permute-start(f32[16,256]{1,0:T(8,128)S(1)} %slice.13), channel_id=1, source_target_pairs={{16,32},{48,64},{80,96},{112,128},{144,160},{176,192},{208,224},{2... | collective-permute-start | bytes 49160 | tf_op jit(solution)/shard_map/ppermute | solution.py:310
  123.6 1.0 copy-start
Sparse Core Ops, SparseCore 0:
  32.2 83.5 reduce-scatter.1

commit v6 on v5

--- a/solution.py
+++ b/solution.py
@@ -228,8 +228,11 @@
 
 
 def factors_kernel(
-    count, first_ref, second_ref, me_ref, own_ref, below_ref, above_ref, shift_ref, scale_ref, turned, dev, inv
+    count, first_ref, second_ref, me_ref, own_ref, below_ref, above_ref, main_ref, done_ref, shift_ref, scale_ref,
+    turned, dev, inv, tiles, sem,
 ):
+    fetch = pltpu.make_async_copy(main_ref, tiles, sem)
+    fetch.start()
     shards = own_ref.shape[0]
     total = shards * count
     stats = jnp.concatenate([below_ref[...], own_ref[...], above_ref[...]], axis=2)
@@ -251,50 +254,60 @@
         a = jnp.clip(first_ref[slot], 0, OWN - 1)
         b = second_ref[slot] + 2
         left = turned[a, mine, :]
-        shift_ref[slot] = count * jnp.dot(
+        shift = count * jnp.dot(
             left[:, :shards], dev[b], precision=lax.Precision.HIGHEST, preferred_element_type=F32
         )
-        scale_ref[slot] = left[:, shards : shards + 1] * inv[pl.ds(b, 1), :] * (1.0 / total**0.5)
-
-
-def factors(count, first, second, me, *stats):
+        scale = left[:, shards : shards + 1] * inv[pl.ds(b, 1), :] * (1.0 / total**0.5)
+        if slot == 0:
+            fetch.wait()
+        if slot == HOME:
+            shift_ref[...] = shift
+            scale_ref[...] = scale
+        else:
+            done_ref[slot] = (tiles[slot] + shift) * scale
+
+
+def factors(count, first, second, me, own, below, above, main):
     vmem = pl.BlockSpec(memory_space=VMEM)
     smem = pl.BlockSpec(memory_space=SMEM)
     return pl.pallas_call(
         functools.partial(factors_kernel, count),
-        in_specs=[smem] * 3 + [vmem] * 3,
-        out_specs=[vmem] * 2,
-        out_shape=[jax.ShapeDtypeStruct((SLOTS, ROWS, BLK), F32)] * 2,
+        in_specs=[smem] * 3 + [vmem] * 3 + [pl.BlockSpec(memory_space=pl.ANY)],
+        out_specs=[vmem] * 3,
+        out_shape=[jax.ShapeDtypeStruct((MADE, ROWS, BLK), F32)] + [jax.ShapeDtypeStruct((ROWS, BLK), F32)] * 2,
         scratch_shapes=[
             VMEM((OWN, BLK, 128), F32),
             VMEM((8, SHARDS, BLK), F32),
             VMEM((8, BLK), F32),
+            VMEM((MADE, ROWS, BLK), F32),
+            pltpu.SemaphoreType.DMA,
         ],
         compiler_params=pltpu.CompilerParams(vmem_limit_bytes=8 << 20),
         cost_estimate=pl.CostEstimate(flops=1 << 26, bytes_accessed=2 << 20, transcendentals=2048),
         name="factors",
-    )(first, second, me, *stats)
-
-
-def finish_kernel(slot_ref, main_ref, home_ref, shift_ref, scale_ref, out_ref, all_ref):
-    all_ref[:MADE] = (main_ref[...] + shift_ref[:MADE]) * scale_ref[:MADE]
-    all_ref[HOME] = (home_ref[...] + shift_ref[HOME]) * scale_ref[HOME]
+    )(first, second, me, own, below, above, pltpu.with_memory_space_constraint(main, pltpu.HBM))
+
+
+def finish_kernel(slot_ref, done_ref, home_ref, shift_ref, scale_ref, out_ref, home):
+    home[...] = (home_ref[...] + shift_ref[...]) * scale_ref[...]
     for p in range(PAIRS):
-        out_ref[:, p, :] = all_ref[slot_ref[p]]
-
-
-def finish(slot, main, home, shift, scale):
+        slot = slot_ref[p]
+        made = done_ref[jnp.minimum(slot, MADE - 1)]
+        out_ref[:, p, :] = jnp.where(slot == HOME, home[...], made)
+
+
+def finish(slot, done, home, shift, scale):
     vmem = pl.BlockSpec(memory_space=VMEM)
     return pl.pallas_call(
         finish_kernel,
         in_specs=[pl.BlockSpec(memory_space=SMEM)] + [vmem] * 4,
         out_specs=vmem,
         out_shape=jax.ShapeDtypeStruct((ROWS, PAIRS, BLK), F32),
-        scratch_shapes=[VMEM((SLOTS, ROWS, BLK), F32)],
+        scratch_shapes=[VMEM((ROWS, BLK), F32)],
         compiler_params=pltpu.CompilerParams(vmem_limit_bytes=8 << 20),
         cost_estimate=pl.CostEstimate(flops=1 << 18, bytes_accessed=1 << 20, transcendentals=0),
         name="finish",
-    )(slot, main, home, shift, scale)
+    )(slot, done, home, shift, scale)
 
 
 def on_device(features, pairs):
@@ -325,8 +338,9 @@
     up = [(i, i + 1) for i in range(owners - 1)]
     below = lax.ppermute(stats[:, :, 2:], "det", up)
     above = lax.ppermute(stats[:, :, :2], "det", [(b, a) for a, b in up])
-    shift, scale = factors(float(shots), first, second, me, stats, below, above)
-    return finish(slot, main, swap(main[15], 1), shift, scale)
+    home = swap(main[15], 1)
+    done, shift, scale = factors(float(shots), first, second, me, stats, below, above, main)
+    return finish(slot, done, home, shift, scale)
 
 
 def solution(mesh):

time: 133 us -> 132 us (level)
  transfers between devices with their start and end apart: 6 -> 6, of which waited for: 3 -> 3; matrix products, arithmetic and copies ran while one was open for 1% -> 1% of each run, Pallas kernels for 10% -> 11%
where the time goes in v6:
time: 132 us; the launch traced here: 131 us
  waiting for transfers between devices  46 us (35%)
  blocking collectives  36.2 us (27%)
  Pallas kernels  22.2 us (17%)
  between operations  13.5 us (10%)
  starting transfers between devices  12.4 us (9%)
    reduce_scatter x1, waiting for transfers between devices, on_device(): lax.psum_scatter(tiles.reshape(SHARDS * MADE * ROWS, BLK), 'shot', scatte...  42.6 us
    all_gather x1, blocking collectives, on_device(): lax.all_gather(stats.reshape(2 * OWN, BLK), 'shot').reshape(-1, 2, OWN, BLK)  36.2 us
    pallas_call x1, Pallas kernels, early(): pl.pallas_call(early_kernel, in_specs=[smem, smem, anywhere], out_specs=[...  9.44 us
    ppermute x3, starting transfers between devices, swap(): return lax.ppermute(x, 'det', ends + [(b, a) for a, b in ends])  8.11 us
    pallas_call x1, Pallas kernels, near(): pl.pallas_call(near_kernel, in_specs=[smem, smem, vmem, vmem, anywhere],...  4.77 us
    pallas_call x2, Pallas kernels, border(): pl.pallas_call(border_kernel, in_specs=[pl.BlockSpec(memory_space=SMEM),...  4.46 us
    ppermute x3, waiting for transfers between devices, swap(): return lax.ppermute(x, 'det', ends + [(b, a) for a, b in ends])  3.41 us
  transfers between devices with their start and end apart: 6, of which 3 were waited for; matrix products, arithmetic and copies ran while one was open for 1% of the time, Pallas kernels for 11%

profile of v6, /device:TPU:24, one launch (start us, length us, event | category | flops | bytes accessed | tf_op | source)
XLA Modules:
  0.0 131.4 jit_solution(13340451126843226592)
XLA Ops:
  6.5 0.0 reduce-scatter.2.cloned.1.call-start
  6.5 2.0 %border_for_a.1 = f32[256,1024]{1,0:T(8,128)} custom-call(s32[1]{0:T(128)} %bitcast.3.start_ref, f32[1024,1024]{1,0:T(8,128)} %x_ref.5), custom_call_target="tpu_custom_call" | custom-call | bytes 2097152 | tf_op jit(solution)/shard_map/border_for_a/pallas_call | solution.py:76
  8.6 0.0 copy-start
  8.6 4.3 %collective-permute-start.1 = (f32[256,1024]{1,0:T(8,128)}, f32[256,1024]{1,0:T(8,128)S(1)}, u32[]{:S(2)}, u32[]{:S(2)}) collective-permute-start(f32[256,1024]{1,0:T(8,128)} %border_for_a.1), channel_id=1, source_target_pairs={{16,32},{48,64},{80,96},{112,128},{144,160},{176,192},{208,224},{2... | collective-permute-start | bytes 3145736 | tf_op jit(solution)/shard_map/ppermute | solution.py:323
  12.9 2.4 %border_for_b.1 = f32[512,1024]{1,0:T(8,128)} custom-call(s32[1]{0:T(128)} %bitcast.4.start_ref, f32[1024,1024]{1,0:T(8,128)} %x_ref.5), custom_call_target="tpu_custom_call" | custom-call | bytes 4194304 | tf_op jit(solution)/shard_map/border_for_b/pallas_call | solution.py:76
  15.3 1.9 %collective-permute-start = (f32[512,1024]{1,0:T(8,128)}, f32[512,1024]{1,0:T(8,128)S(1)}, u32[]{:S(2)}, u32[]{:S(2)}) collective-permute-start(f32[512,1024]{1,0:T(8,128)} %border_for_b.1), channel_id=1, source_target_pairs={{0,16},{32,48},{64,80},{96,112},{128,144},{160,176},{192,208},{224... | collective-permute-start | bytes 6291464 | tf_op jit(solution)/shard_map/ppermute | solution.py:323
  17.2 0.0 copy-done
  17.3 0.1 copy.7.pairs_ref
  17.3 0.1 pad_add_fusion.place_ref
  17.4 9.4 %early_tiles.1 = (f32[16,16,16,256]{3,2,1,0:T(8,128)}, bf16[3584,1024]{1,0:T(8,128)(2,1)S(1)}, f32[2,4,256]{2,1,0:T(4,128)S(1)}, s32[17]{0:T(128)S(1)}, s32[17]{...) custom-call(s32[16,2]{1,0:T(8,128)S(1)} %copy.7.pairs_ref, s32[2]{0:T(128)S(1)} %pad_add_fusion.place_ref, ...), custom_call_target="tpu_custom_call" | custom-call | flops 4026531840 | bytes 12582912 | tf_op jit(solution)/shard_map/early_tiles/pallas_call | solution.py:162
  26.9 0.1 collective-permute-done.1.halo_ref
  27.0 0.2 split_a.1._
  27.3 0.0 collective-permute-done.halo_ref
  27.3 4.8 %near_tiles.1 = (f32[16,16,16,256]{3,2,1,0:T(8,128)}, bf16[3584,1024]{1,0:T(8,128)(2,1)S(1)}) custom-call(s32[17]{0:T(128)S(1)} %get-tuple-element.24.left_ref, s32[17]{0:T(128)S(1)} %get-tuple-element.25.right_ref, f32[512,1024]{1,0:T(8,128)S(1)} %collective-permute-done.halo_ref, ...), custom_call_target="tpu_custom_call", output_to_operand_aliasing={{1}: (3, {}), {0}: (4, {})} | custom-call | flops 2415919104 | bytes 5242880 | tf_op jit(solution)/shard_map/near_tiles/pallas_call | solution.py:215
  32.1 0.0 reduce-scatter.2.cloned.1.call-update
  32.1 36.2 %all_gather.3 = f32[16,8,256]{2,1,0:T(8,128)S(1)} all-gather(f32[1,8,256]{2,1,0:T(8,128)S(1)} %all_gather_reshape.3), channel_id=1, replica_groups=mesh['det'=32,'shot'=16] {'shot'}, dimensions={0}, use_global_device_ids=true | all-gather | bytes 139264 | tf_op jit(solution)/shard_map/all_gather | solution.py:337
  68.3 0.1 fusion
  68.4 1.9 %collective-permute-start.3 = (f32[16,2,2,256]{3,2,1,0:T(2,128)S(1)}, f32[16,2,2,256]{3,2,1,0:T(2,128)S(1)}, u32[]{:S(2)}, u32[]{:S(2)}) collective-permute-start(f32[16,2,2,256]{3,2,1,0:T(2,128)S(1)} %get-tuple-element.35), channel_id=1, source_target_pairs={{16,0},{32,16},{48,32},{64,48},{80,64},{96,80},{112,96},{128,112},... | collective-permute-start | bytes 196616 | tf_op jit(solution)/shard_map/ppermute | solution.py:340
  70.3 2.4 %collective-permute-start.2 = (f32[16,2,2,256]{3,2,1,0:T(2,128)S(1)}, f32[16,2,2,256]{3,2,1,0:T(2,128)S(1)}, u32[]{:S(2)}, u32[]{:S(2)}) collective-permute-start(f32[16,2,2,256]{3,2,1,0:T(2,128)S(1)} %get-tuple-element.36), channel_id=1, source_target_pairs={{0,16},{16,32},{32,48},{48,64},{64,80},{80,96},{96,112},{112,128},... | collective-permute-start | bytes 196616 | tf_op jit(solution)/shard_map/ppermute | solution.py:339
  72.7 42.6 %reduce-scatter.2.cloned.1.call-done = f32[256,256]{1,0:T(8,128)} async-done(((f32[4096,256]{1,0:T(8,128)}), f32[256,256]{1,0:T(8,128)}) %reduce-scatter.2.cloned.1.call-update) | async-done | bytes 262160 | tf_op jit(solution)/shard_map/reduce_scatter | solution.py:332
  115.3 0.7 slice.15
  116.0 1.9 %collective-permute-start.4 = (f32[16,256]{1,0:T(8,128)S(1)}, f32[16,256]{1,0:T(8,128)S(1)}, u32[]{:S(2)}, u32[]{:S(2)}) collective-permute-start(f32[16,256]{1,0:T(8,128)S(1)} %slice.15), channel_id=1, source_target_pairs={{16,32},{48,64},{80,96},{112,128},{144,160},{176,192},{208,224},{2... | collective-permute-start | bytes 49160 | tf_op jit(solution)/shard_map/ppermute | solution.py:323
  117.9 0.0 collective-permute-done.3.above_ref
  118.0 0.0 collective-permute-done.2.below_ref
  118.0 1.9 %factors.1 = (f32[16,16,256]{2,1,0:T(8,128)S(1)}, f32[16,256]{1,0:T(8,128)S(1)}, f32[16,256]{1,0:T(8,128)S(1)}) custom-call(s32[17]{0:T(128)S(1)} %get-tuple-element.21.first_ref, s32[17]{0:T(128)S(1)} %get-tuple-element.22.second_ref, s32[1]{0:T(128)} %bitcast.2.me_ref, f32[16,2,4,256]{3,2,1,0:T(4,128)S(1)} %reshape.23.own_ref, ...), custom_call_target="tpu_custom_call" | custom-call | flops 67108864 | bytes 2097152 | tf_op jit(solution)/shard_map/factors/pallas_call | solution.py:273
  119.9 3.3 %collective-permute-done.4.home_ref = f32[16,256]{1,0:T(8,128)S(1)} collective-permute-done((f32[16,256]{1,0:T(8,128)S(1)}, f32[16,256]{1,0:T(8,128)S(1)}, u32[]{:S(2)}, u32[]{:S(2)}) %collective-permute-start.4) | collective-permute-done | bytes 16416 | tf_op jit(solution)/shard_map/ppermute | solution.py:323
  123.2 1.4 %finish.1 = f32[16,16,256]{2,1,0:T(8,128)} custom-call(s32[16]{0:T(128)S(1)} %get-tuple-element.20.slot_ref, f32[16,16,256]{2,1,0:T(8,128)S(1)} %get-tuple-element.32.done_ref, f32[16,256]{1,0:T(8,128)S(1)} %collective-permute-done.4.home_ref, f32[16,256]{1,0:T(8,128)S(1)} %get-tuple-element.33.shift_ref, f32[16,256]{1,0:T(8,128)S(1)} %get-tuple-element.34.scale_ref), custom_call_target="tpu_custom_call" | custom-call | flops 262144 | bytes 1048576 | tf_op jit(solution)/shard_map/finish/pallas_call | solution.py:301
  (2 shorter events, 0.0 us)
Async XLA Ops:
  6.5 108.8 %reduce-scatter.2.cloned.1.call-start = ((), (), s32[]{:S(2)}) async-start(), calls=%async_computation.1 | async-start | bytes 4456448 | tf_op jit(solution)/shard_map/reduce_scatter | solution.py:332
  8.6 8.7 %copy-start = (s32[16,2]{0,1:T(2,128)S(1)}, s32[16,2]{0,1:T(2,128)}, u32[]{:S(2)}) copy-start(s32[16,2]{0,1:T(2,128)} %param.3) | copy-start | bytes 388
  8.6 18.4 %collective-permute-start.1 = (f32[256,1024]{1,0:T(8,128)}, f32[256,1024]{1,0:T(8,128)S(1)}, u32[]{:S(2)}, u32[]{:S(2)}) collective-permute-start(f32[256,1024]{1,0:T(8,128)} %border_for_a.1), channel_id=1, source_target_pairs={{16,32},{48,64},{80,96},{112,128},{144,160},{176,192},{208,224},{2... | collective-permute-start | bytes 3145736 | tf_op jit(solution)/shard_map/ppermute | solution.py:323
  15.3 11.9 %collective-permute-start = (f32[512,1024]{1,0:T(8,128)}, f32[512,1024]{1,0:T(8,128)S(1)}, u32[]{:S(2)}, u32[]{:S(2)}) collective-permute-start(f32[512,1024]{1,0:T(8,128)} %border_for_b.1), channel_id=1, source_target_pairs={{0,16},{32,48},{64,80},{96,112},{128,144},{160,176},{192,208},{224... | collective-permute-start | bytes 6291464 | tf_op jit(solution)/shard_map/ppermute | solution.py:323
  68.4 49.6 %collective-permute-start.3 = (f32[16,2,2,256]{3,2,1,0:T(2,128)S(1)}, f32[16,2,2,256]{3,2,1,0:T(2,128)S(1)}, u32[]{:S(2)}, u32[]{:S(2)}) collective-permute-start(f32[16,2,2,256]{3,2,1,0:T(2,128)S(1)} %get-tuple-element.35), channel_id=1, source_target_pairs={{16,0},{32,16},{48,32},{64,48},{80,64},{96,80},{112,96},{128,112},... | collective-permute-start | bytes 196616 | tf_op jit(solution)/shard_map/ppermute | solution.py:340
  70.3 47.7 %collective-permute-start.2 = (f32[16,2,2,256]{3,2,1,0:T(2,128)S(1)}, f32[16,2,2,256]{3,2,1,0:T(2,128)S(1)}, u32[]{:S(2)}, u32[]{:S(2)}) collective-permute-start(f32[16,2,2,256]{3,2,1,0:T(2,128)S(1)} %get-tuple-element.36), channel_id=1, source_target_pairs={{0,16},{16,32},{32,48},{48,64},{64,80},{80,96},{96,112},{112,128},... | collective-permute-start | bytes 196616 | tf_op jit(solution)/shard_map/ppermute | solution.py:339
  116.0 7.2 %collective-permute-start.4 = (f32[16,256]{1,0:T(8,128)S(1)}, f32[16,256]{1,0:T(8,128)S(1)}, u32[]{:S(2)}, u32[]{:S(2)}) collective-permute-start(f32[16,256]{1,0:T(8,128)S(1)} %slice.15), channel_id=1, source_target_pairs={{16,32},{48,64},{80,96},{112,128},{144,160},{176,192},{208,224},{2... | collective-permute-start | bytes 49160 | tf_op jit(solution)/shard_map/ppermute | solution.py:323
Sparse Core Ops, SparseCore 0:
  32.2 83.0 reduce-scatter.1

commit v7 on v6

--- a/solution.py
+++ b/solution.py
@@ -68,6 +68,26 @@
         store.start()
     for store in stores:
         store.wait()
+
+
+def border_held_kernel(start_ref, x_ref, out_ref, sem):
+    copy = pltpu.make_async_copy(x_ref.at[pl.ds(start_ref[0] * BLK, BLK), :], out_ref, sem)
+    copy.start()
+    copy.wait()
+
+
+def border_held(start, features):
+    shots = features.shape[1]
+    return pl.pallas_call(
+        border_held_kernel,
+        in_specs=[pl.BlockSpec(memory_space=SMEM), pl.BlockSpec(memory_space=pl.ANY)],
+        out_specs=pl.BlockSpec(memory_space=VMEM),
+        out_shape=jax.ShapeDtypeStruct((BLK, shots), F32),
+        scratch_shapes=[pltpu.SemaphoreType.DMA],
+        compiler_params=pltpu.CompilerParams(vmem_limit_bytes=8 << 20),
+        cost_estimate=pl.CostEstimate(flops=0, bytes_accessed=2 << 20, transcendentals=0),
+        name="border_for_a",
+    )(start.reshape(1), pltpu.with_memory_space_constraint(features, pltpu.HBM))
 
 
 def border(start, blocks, features, name):
@@ -203,10 +223,21 @@
     )(halo, parts)
 
 
-def near_kernel(left_ref, right_ref, halo_ref, _, __, tiles_ref, parts_ref, buffers, sems):
+def near_kernel(left_ref, right_ref, halo_ref, before_ref, _, tiles_ref, parts_ref, buffers, sems):
+
+    def copy(k):
+        return pltpu.make_async_copy(buffers.at[k], tiles_ref.at[:, EARLY + k], sems.at[k])
+
+    with_b = MADE - EARLY - 3
+    ahead = [product(before_ref, left_ref[EARLY + k], right_ref[EARLY + k]) for k in range(with_b, MADE - EARLY)]
+    for k, tile in enumerate(ahead):
+        buffers[with_b + k] = tile.reshape(SHARDS, ROWS, BLK)
+        copy(with_b + k).start()
     for k in range(2):
         split_block(halo_ref[k * BLK : (k + 1) * BLK, :], parts_ref, OWN + k, None, None)
-    fill(EARLY, NEAR_GROUPS, parts_ref, left_ref, right_ref, tiles_ref, buffers, sems)
+    fill(EARLY, (with_b,), parts_ref, left_ref, right_ref, tiles_ref, buffers, sems)
+    for k in range(with_b, MADE - EARLY):
+        copy(k).wait()
 
 
 def near(left, right, halo, parts, tiles):
@@ -322,7 +353,7 @@
         ends = [(i, i + 1) for i in range(start, owners - 1, 2)]
         return lax.ppermute(x, "det", ends + [(b, a) for a, b in ends])
 
-    to_a = border(3 * core, 1, features, "border_for_a")
+    to_a = border_held(3 * core, features)
     later, to_a = lax.optimization_barrier((2 - 2 * core, to_a))
     from_a = swap(to_a, 1)
     from_b = swap(border(later, 2, features, "border_for_b"), 0)

time: 132 us -> 133 us (level)
    pallas_call x2 -> x1, Pallas kernels: 4.46 us -> 2.45 us  [border(): pl.pallas_call(border_kernel, in_specs=[pl.BlockSpec(memory_space=SMEM),...]
  transfers between devices with their start and end apart: 6 -> 6, of which waited for: 3 -> 2; matrix products, arithmetic and copies ran while one was open for 1% -> 1% of each run, Pallas kernels for 11% -> 12%
where the time goes in v7:
time: 133 us; the launch traced here: 132 us
  waiting for transfers between devices  46.3 us (35%)
  blocking collectives  36.2 us (27%)
  Pallas kernels  22.7 us (17%)
  between operations  13.5 us (10%)
  starting transfers between devices  12.4 us (9%)
    reduce_scatter x1, waiting for transfers between devices, on_device(): lax.psum_scatter(tiles.reshape(SHARDS * MADE * ROWS, BLK), 'shot', scatte...  43 us
    all_gather x1, blocking collectives, on_device(): lax.all_gather(stats.reshape(2 * OWN, BLK), 'shot').reshape(-1, 2, OWN, BLK)  36.2 us
    pallas_call x1, Pallas kernels, early(): pl.pallas_call(early_kernel, in_specs=[smem, smem, anywhere], out_specs=[...  9.44 us
    ppermute x3, starting transfers between devices, swap(): return lax.ppermute(x, 'det', ends + [(b, a) for a, b in ends])  8.12 us
    pallas_call x1, Pallas kernels, near(): pl.pallas_call(near_kernel, in_specs=[smem, smem, vmem, vmem, anywhere],...  4.76 us
    ppermute x3, waiting for transfers between devices, swap(): return lax.ppermute(x, 'det', ends + [(b, a) for a, b in ends])  3.3 us
  transfers between devices with their start and end apart: 6, of which 2 were waited for; matrix products, arithmetic and copies ran while one was open for 1% of the time, Pallas kernels for 12%

profile of v7, /device:TPU:24, one launch (start us, length us, event | category | flops | bytes accessed | tf_op | source)
XLA Modules:
  0.0 132.1 jit_solution(6951592407379980918)
XLA Ops:
  6.5 0.0 reduce-scatter.2.cloned.1.call-start
  6.5 1.2 border_for_a.1
  7.8 0.0 copy-start
  7.8 4.3 %collective-permute-start.1 = (f32[256,1024]{1,0:T(8,128)S(1)}, f32[256,1024]{1,0:T(8,128)}, u32[]{:S(2)}, u32[]{:S(2)}) collective-permute-start(f32[256,1024]{1,0:T(8,128)S(1)} %border_for_a.1), channel_id=1, source_target_pairs={{16,32},{48,64},{80,96},{112,128},{144,160},{176,192},{208,224},{2... | collective-permute-start | bytes 3145736 | tf_op jit(solution)/shard_map/ppermute | solution.py:354
  12.1 2.4 %border_for_b.1 = f32[512,1024]{1,0:T(8,128)} custom-call(s32[1]{0:T(128)} %bitcast.4.start_ref, f32[1024,1024]{1,0:T(8,128)} %x_ref.5), custom_call_target="tpu_custom_call" | custom-call | bytes 4194304 | tf_op jit(solution)/shard_map/border_for_b/pallas_call | solution.py:96
  14.5 1.9 %collective-permute-start = (f32[512,1024]{1,0:T(8,128)}, f32[512,1024]{1,0:T(8,128)S(1)}, u32[]{:S(2)}, u32[]{:S(2)}) collective-permute-start(f32[512,1024]{1,0:T(8,128)} %border_for_b.1), channel_id=1, source_target_pairs={{0,16},{32,48},{64,80},{96,112},{128,144},{160,176},{192,208},{224... | collective-permute-start | bytes 6291464 | tf_op jit(solution)/shard_map/ppermute | solution.py:354
  16.5 0.0 copy-done
  16.5 0.1 copy.7.pairs_ref
  16.6 0.1 pad_add_fusion.place_ref
  16.6 9.4 %early_tiles.1 = (f32[16,16,16,256]{3,2,1,0:T(8,128)}, bf16[3584,1024]{1,0:T(8,128)(2,1)S(1)}, f32[2,4,256]{2,1,0:T(4,128)S(1)}, s32[17]{0:T(128)S(1)}, s32[17]{...) custom-call(s32[16,2]{1,0:T(8,128)S(1)} %copy.7.pairs_ref, s32[2]{0:T(128)S(1)} %pad_add_fusion.place_ref, ...), custom_call_target="tpu_custom_call" | custom-call | flops 4026531840 | bytes 12582912 | tf_op jit(solution)/shard_map/early_tiles/pallas_call | solution.py:182
  26.1 0.0 collective-permute-done.1.halo_ref
  26.1 1.5 %split_a.1.before_ref = bf16[3584,1024]{1,0:T(8,128)(2,1)S(1)} custom-call(f32[256,1024]{1,0:T(8,128)} %collective-permute-done.1.halo_ref, bf16[3584,1024]{1,0:T(8,128)(2,1)S(1)} %get-tuple-element.28._), custom_call_target="tpu_custom_call", output_to_operand_aliasing={{}: (1, {})} | custom-call | flops 17179869184 | bytes 1048576 | tf_op jit(solution)/shard_map/split_a/pallas_call | solution.py:214
  27.6 0.0 collective-permute-done.halo_ref
  27.6 4.8 %near_tiles.1 = (f32[16,16,16,256]{3,2,1,0:T(8,128)}, bf16[3584,1024]{1,0:T(8,128)(2,1)S(1)}) custom-call(s32[17]{0:T(128)S(1)} %get-tuple-element.24.left_ref, s32[17]{0:T(128)S(1)} %get-tuple-element.25.right_ref, f32[512,1024]{1,0:T(8,128)S(1)} %collective-permute-done.halo_ref, ...), custom_call_target="tpu_custom_call", output_to_operand_aliasing={{1}: (3, {}), {0}: (4, {})} | custom-call | flops 2415919104 | bytes 5242880 | tf_op jit(solution)/shard_map/near_tiles/pallas_call | solution.py:246
  32.4 0.0 reduce-scatter.2.cloned.1.call-update
  32.4 36.2 %all_gather.3 = f32[16,8,256]{2,1,0:T(8,128)S(1)} all-gather(f32[1,8,256]{2,1,0:T(8,128)S(1)} %all_gather_reshape.3), channel_id=1, replica_groups=mesh['det'=32,'shot'=16] {'shot'}, dimensions={0}, use_global_device_ids=true | all-gather | bytes 139264 | tf_op jit(solution)/shard_map/all_gather | solution.py:368
  68.6 0.1 fusion
  68.7 1.9 %collective-permute-start.3 = (f32[16,2,2,256]{3,2,1,0:T(2,128)S(1)}, f32[16,2,2,256]{3,2,1,0:T(2,128)S(1)}, u32[]{:S(2)}, u32[]{:S(2)}) collective-permute-start(f32[16,2,2,256]{3,2,1,0:T(2,128)S(1)} %get-tuple-element.35), channel_id=1, source_target_pairs={{16,0},{32,16},{48,32},{64,48},{80,64},{96,80},{112,96},{128,112},... | collective-permute-start | bytes 196616 | tf_op jit(solution)/shard_map/ppermute | solution.py:371
  70.6 2.4 %collective-permute-start.2 = (f32[16,2,2,256]{3,2,1,0:T(2,128)S(1)}, f32[16,2,2,256]{3,2,1,0:T(2,128)S(1)}, u32[]{:S(2)}, u32[]{:S(2)}) collective-permute-start(f32[16,2,2,256]{3,2,1,0:T(2,128)S(1)} %get-tuple-element.36), channel_id=1, source_target_pairs={{0,16},{16,32},{32,48},{48,64},{64,80},{80,96},{96,112},{112,128},... | collective-permute-start | bytes 196616 | tf_op jit(solution)/shard_map/ppermute | solution.py:370
  73.0 43.0 %reduce-scatter.2.cloned.1.call-done = f32[256,256]{1,0:T(8,128)} async-done(((f32[4096,256]{1,0:T(8,128)}), f32[256,256]{1,0:T(8,128)}) %reduce-scatter.2.cloned.1.call-update) | async-done | bytes 262160 | tf_op jit(solution)/shard_map/reduce_scatter | solution.py:363
  116.0 0.7 slice.15
  116.7 1.9 %collective-permute-start.4 = (f32[16,256]{1,0:T(8,128)S(1)}, f32[16,256]{1,0:T(8,128)S(1)}, u32[]{:S(2)}, u32[]{:S(2)}) collective-permute-start(f32[16,256]{1,0:T(8,128)S(1)} %slice.15), channel_id=1, source_target_pairs={{16,32},{48,64},{80,96},{112,128},{144,160},{176,192},{208,224},{2... | collective-permute-start | bytes 49160 | tf_op jit(solution)/shard_map/ppermute | solution.py:354
  118.6 0.0 collective-permute-done.3.above_ref
  118.6 0.0 collective-permute-done.2.below_ref
  118.7 1.9 %factors.1 = (f32[16,16,256]{2,1,0:T(8,128)S(1)}, f32[16,256]{1,0:T(8,128)S(1)}, f32[16,256]{1,0:T(8,128)S(1)}) custom-call(s32[17]{0:T(128)S(1)} %get-tuple-element.21.first_ref, s32[17]{0:T(128)S(1)} %get-tuple-element.22.second_ref, s32[1]{0:T(128)} %bitcast.2.me_ref, f32[16,2,4,256]{3,2,1,0:T(4,128)S(1)} %reshape.23.own_ref, ...), custom_call_target="tpu_custom_call" | custom-call | flops 67108864 | bytes 2097152 | tf_op jit(solution)/shard_map/factors/pallas_call | solution.py:304
  120.6 3.3 %collective-permute-done.4.home_ref = f32[16,256]{1,0:T(8,128)S(1)} collective-permute-done((f32[16,256]{1,0:T(8,128)S(1)}, f32[16,256]{1,0:T(8,128)S(1)}, u32[]{:S(2)}, u32[]{:S(2)}) %collective-permute-start.4) | collective-permute-done | bytes 16416 | tf_op jit(solution)/shard_map/ppermute | solution.py:354
  123.9 1.4 %finish.1 = f32[16,16,256]{2,1,0:T(8,128)} custom-call(s32[16]{0:T(128)S(1)} %get-tuple-element.20.slot_ref, f32[16,16,256]{2,1,0:T(8,128)S(1)} %get-tuple-element.32.done_ref, f32[16,256]{1,0:T(8,128)S(1)} %collective-permute-done.4.home_ref, f32[16,256]{1,0:T(8,128)S(1)} %get-tuple-element.33.shift_ref, f32[16,256]{1,0:T(8,128)S(1)} %get-tuple-element.34.scale_ref), custom_call_target="tpu_custom_call" | custom-call | flops 262144 | bytes 1048576 | tf_op jit(solution)/shard_map/finish/pallas_call | solution.py:332
  (2 shorter events, 0.0 us)
Async XLA Ops:
  6.5 109.5 %reduce-scatter.2.cloned.1.call-start = ((), (), s32[]{:S(2)}) async-start(), calls=%async_computation.1 | async-start | bytes 4456448 | tf_op jit(solution)/shard_map/reduce_scatter | solution.py:363
  7.8 8.7 %copy-start = (s32[16,2]{0,1:T(2,128)S(1)}, s32[16,2]{0,1:T(2,128)}, u32[]{:S(2)}) copy-start(s32[16,2]{0,1:T(2,128)} %param.3) | copy-start | bytes 388
  7.8 18.3 %collective-permute-start.1 = (f32[256,1024]{1,0:T(8,128)S(1)}, f32[256,1024]{1,0:T(8,128)}, u32[]{:S(2)}, u32[]{:S(2)}) collective-permute-start(f32[256,1024]{1,0:T(8,128)S(1)} %border_for_a.1), channel_id=1, source_target_pairs={{16,32},{48,64},{80,96},{112,128},{144,160},{176,192},{208,224},{2... | collective-permute-start | bytes 3145736 | tf_op jit(solution)/shard_map/ppermute | solution.py:354
  14.5 13.1 %collective-permute-start = (f32[512,1024]{1,0:T(8,128)}, f32[512,1024]{1,0:T(8,128)S(1)}, u32[]{:S(2)}, u32[]{:S(2)}) collective-permute-start(f32[512,1024]{1,0:T(8,128)} %border_for_b.1), channel_id=1, source_target_pairs={{0,16},{32,48},{64,80},{96,112},{128,144},{160,176},{192,208},{224... | collective-permute-start | bytes 6291464 | tf_op jit(solution)/shard_map/ppermute | solution.py:354
  68.7 50.0 %collective-permute-start.3 = (f32[16,2,2,256]{3,2,1,0:T(2,128)S(1)}, f32[16,2,2,256]{3,2,1,0:T(2,128)S(1)}, u32[]{:S(2)}, u32[]{:S(2)}) collective-permute-start(f32[16,2,2,256]{3,2,1,0:T(2,128)S(1)} %get-tuple-element.35), channel_id=1, source_target_pairs={{16,0},{32,16},{48,32},{64,48},{80,64},{96,80},{112,96},{128,112},... | collective-permute-start | bytes 196616 | tf_op jit(solution)/shard_map/ppermute | solution.py:371
  70.6 48.0 %collective-permute-start.2 = (f32[16,2,2,256]{3,2,1,0:T(2,128)S(1)}, f32[16,2,2,256]{3,2,1,0:T(2,128)S(1)}, u32[]{:S(2)}, u32[]{:S(2)}) collective-permute-start(f32[16,2,2,256]{3,2,1,0:T(2,128)S(1)} %get-tuple-element.36), channel_id=1, source_target_pairs={{0,16},{16,32},{32,48},{48,64},{64,80},{80,96},{96,112},{112,128},... | collective-permute-start | bytes 196616 | tf_op jit(solution)/shard_map/ppermute | solution.py:370
  116.7 7.2 %collective-permute-start.4 = (f32[16,256]{1,0:T(8,128)S(1)}, f32[16,256]{1,0:T(8,128)S(1)}, u32[]{:S(2)}, u32[]{:S(2)}) collective-permute-start(f32[16,256]{1,0:T(8,128)S(1)} %slice.15), channel_id=1, source_target_pairs={{16,32},{48,64},{80,96},{112,128},{144,160},{176,192},{208,224},{2... | collective-permute-start | bytes 49160 | tf_op jit(solution)/shard_map/ppermute | solution.py:354
Sparse Core Ops, SparseCore 0:
  32.5 83.4 reduce-scatter.1

commit v8 on v6

--- a/solution.py
+++ b/solution.py
@@ -203,10 +203,21 @@
     )(halo, parts)
 
 
-def near_kernel(left_ref, right_ref, halo_ref, _, __, tiles_ref, parts_ref, buffers, sems):
+def near_kernel(left_ref, right_ref, halo_ref, before_ref, _, tiles_ref, parts_ref, buffers, sems):
+
+    def copy(k):
+        return pltpu.make_async_copy(buffers.at[k], tiles_ref.at[:, EARLY + k], sems.at[k])
+
+    with_b = MADE - EARLY - 3
+    ahead = [product(before_ref, left_ref[EARLY + k], right_ref[EARLY + k]) for k in range(with_b, MADE - EARLY)]
+    for k, tile in enumerate(ahead):
+        buffers[with_b + k] = tile.reshape(SHARDS, ROWS, BLK)
+        copy(with_b + k).start()
     for k in range(2):
         split_block(halo_ref[k * BLK : (k + 1) * BLK, :], parts_ref, OWN + k, None, None)
-    fill(EARLY, NEAR_GROUPS, parts_ref, left_ref, right_ref, tiles_ref, buffers, sems)
+    fill(EARLY, (with_b,), parts_ref, left_ref, right_ref, tiles_ref, buffers, sems)
+    for k in range(with_b, MADE - EARLY):
+        copy(k).wait()
 
 
 def near(left, right, halo, parts, tiles):

time: 132 us -> 132 us (level)
  no operation moved by 1% of the time
where the time goes in v8:
time: 132 us
  waiting for transfers between devices  46.2 us (35%)
  blocking collectives  36.2 us (27%)
  Pallas kernels  22.2 us (17%)
  between operations  13.5 us (10%)
  starting transfers between devices  12.4 us (9%)
    reduce_scatter x1, waiting for transfers between devices, on_device(): lax.psum_scatter(tiles.reshape(SHARDS * MADE * ROWS, BLK), 'shot', scatte...  42.7 us
    all_gather x1, blocking collectives, on_device(): lax.all_gather(stats.reshape(2 * OWN, BLK), 'shot').reshape(-1, 2, OWN, BLK)  36.2 us
    pallas_call x1, Pallas kernels, early(): pl.pallas_call(early_kernel, in_specs=[smem, smem, anywhere], out_specs=[...  9.44 us
    ppermute x3, starting transfers between devices, swap(): return lax.ppermute(x, 'det', ends + [(b, a) for a, b in ends])  8.11 us
    pallas_call x1, Pallas kernels, near(): pl.pallas_call(near_kernel, in_specs=[smem, smem, vmem, vmem, anywhere],...  4.75 us
    pallas_call x2, Pallas kernels, border(): pl.pallas_call(border_kernel, in_specs=[pl.BlockSpec(memory_space=SMEM),...  4.46 us
    ppermute x3, waiting for transfers between devices, swap(): return lax.ppermute(x, 'det', ends + [(b, a) for a, b in ends])  3.41 us
  transfers between devices with their start and end apart: 6, of which 3 were waited for; matrix products, arithmetic and copies ran while one was open for 1% of the time, Pallas kernels for 11%

profile of v8, /device:TPU:24, one launch (start us, length us, event | category | flops | bytes accessed | tf_op | source)
XLA Modules:
  0.0 131.5 jit_solution(17251381463431698674)
XLA Ops:
  6.5 0.0 reduce-scatter.2.cloned.1.call-start
  6.5 2.0 %border_for_a.1 = f32[256,1024]{1,0:T(8,128)} custom-call(s32[1]{0:T(128)} %bitcast.3.start_ref, f32[1024,1024]{1,0:T(8,128)} %x_ref.5), custom_call_target="tpu_custom_call" | custom-call | bytes 2097152 | tf_op jit(solution)/shard_map/border_for_a/pallas_call | solution.py:76
  8.6 0.0 copy-start
  8.6 4.3 %collective-permute-start.1 = (f32[256,1024]{1,0:T(8,128)}, f32[256,1024]{1,0:T(8,128)S(1)}, u32[]{:S(2)}, u32[]{:S(2)}) collective-permute-start(f32[256,1024]{1,0:T(8,128)} %border_for_a.1), channel_id=1, source_target_pairs={{16,32},{48,64},{80,96},{112,128},{144,160},{176,192},{208,224},{2... | collective-permute-start | bytes 3145736 | tf_op jit(solution)/shard_map/ppermute | solution.py:334
  12.9 2.4 %border_for_b.1 = f32[512,1024]{1,0:T(8,128)} custom-call(s32[1]{0:T(128)} %bitcast.4.start_ref, f32[1024,1024]{1,0:T(8,128)} %x_ref.5), custom_call_target="tpu_custom_call" | custom-call | bytes 4194304 | tf_op jit(solution)/shard_map/border_for_b/pallas_call | solution.py:76
  15.3 1.9 %collective-permute-start = (f32[512,1024]{1,0:T(8,128)}, f32[512,1024]{1,0:T(8,128)S(1)}, u32[]{:S(2)}, u32[]{:S(2)}) collective-permute-start(f32[512,1024]{1,0:T(8,128)} %border_for_b.1), channel_id=1, source_target_pairs={{0,16},{32,48},{64,80},{96,112},{128,144},{160,176},{192,208},{224... | collective-permute-start | bytes 6291464 | tf_op jit(solution)/shard_map/ppermute | solution.py:334
  17.2 0.0 copy-done
  17.3 0.1 copy.7.pairs_ref
  17.3 0.1 pad_add_fusion.place_ref
  17.4 9.4 %early_tiles.1 = (f32[16,16,16,256]{3,2,1,0:T(8,128)}, bf16[3584,1024]{1,0:T(8,128)(2,1)S(1)}, f32[2,4,256]{2,1,0:T(4,128)S(1)}, s32[17]{0:T(128)S(1)}, s32[17]{...) custom-call(s32[16,2]{1,0:T(8,128)S(1)} %copy.7.pairs_ref, s32[2]{0:T(128)S(1)} %pad_add_fusion.place_ref, ...), custom_call_target="tpu_custom_call" | custom-call | flops 4026531840 | bytes 12582912 | tf_op jit(solution)/shard_map/early_tiles/pallas_call | solution.py:162
  26.9 0.1 collective-permute-done.1.halo_ref
  27.0 0.2 split_a.1.before_ref
  27.3 0.0 collective-permute-done.halo_ref
  27.3 4.8 %near_tiles.1 = (f32[16,16,16,256]{3,2,1,0:T(8,128)}, bf16[3584,1024]{1,0:T(8,128)(2,1)S(1)}) custom-call(s32[17]{0:T(128)S(1)} %get-tuple-element.24.left_ref, s32[17]{0:T(128)S(1)} %get-tuple-element.25.right_ref, f32[512,1024]{1,0:T(8,128)S(1)} %collective-permute-done.halo_ref, ...), custom_call_target="tpu_custom_call", output_to_operand_aliasing={{1}: (3, {}), {0}: (4, {})} | custom-call | flops 2415919104 | bytes 5242880 | tf_op jit(solution)/shard_map/near_tiles/pallas_call | solution.py:226
  32.0 0.0 reduce-scatter.2.cloned.1.call-update
  32.1 36.2 %all_gather.3 = f32[16,8,256]{2,1,0:T(8,128)S(1)} all-gather(f32[1,8,256]{2,1,0:T(8,128)S(1)} %all_gather_reshape.3), channel_id=1, replica_groups=mesh['det'=32,'shot'=16] {'shot'}, dimensions={0}, use_global_device_ids=true | all-gather | bytes 139264 | tf_op jit(solution)/shard_map/all_gather | solution.py:348
  68.3 0.1 fusion
  68.4 1.9 %collective-permute-start.3 = (f32[16,2,2,256]{3,2,1,0:T(2,128)S(1)}, f32[16,2,2,256]{3,2,1,0:T(2,128)S(1)}, u32[]{:S(2)}, u32[]{:S(2)}) collective-permute-start(f32[16,2,2,256]{3,2,1,0:T(2,128)S(1)} %get-tuple-element.35), channel_id=1, source_target_pairs={{16,0},{32,16},{48,32},{64,48},{80,64},{96,80},{112,96},{128,112},... | collective-permute-start | bytes 196616 | tf_op jit(solution)/shard_map/ppermute | solution.py:351
  70.3 2.4 %collective-permute-start.2 = (f32[16,2,2,256]{3,2,1,0:T(2,128)S(1)}, f32[16,2,2,256]{3,2,1,0:T(2,128)S(1)}, u32[]{:S(2)}, u32[]{:S(2)}) collective-permute-start(f32[16,2,2,256]{3,2,1,0:T(2,128)S(1)} %get-tuple-element.36), channel_id=1, source_target_pairs={{0,16},{16,32},{32,48},{48,64},{64,80},{80,96},{96,112},{112,128},... | collective-permute-start | bytes 196616 | tf_op jit(solution)/shard_map/ppermute | solution.py:350
  72.7 42.7 %reduce-scatter.2.cloned.1.call-done = f32[256,256]{1,0:T(8,128)} async-done(((f32[4096,256]{1,0:T(8,128)}), f32[256,256]{1,0:T(8,128)}) %reduce-scatter.2.cloned.1.call-update) | async-done | bytes 262160 | tf_op jit(solution)/shard_map/reduce_scatter | solution.py:343
  115.4 0.7 slice.15
  116.1 1.9 %collective-permute-start.4 = (f32[16,256]{1,0:T(8,128)S(1)}, f32[16,256]{1,0:T(8,128)S(1)}, u32[]{:S(2)}, u32[]{:S(2)}) collective-permute-start(f32[16,256]{1,0:T(8,128)S(1)} %slice.15), channel_id=1, source_target_pairs={{16,32},{48,64},{80,96},{112,128},{144,160},{176,192},{208,224},{2... | collective-permute-start | bytes 49160 | tf_op jit(solution)/shard_map/ppermute | solution.py:334
  118.1 0.0 collective-permute-done.3.above_ref
  118.1 0.0 collective-permute-done.2.below_ref
  118.1 1.9 %factors.1 = (f32[16,16,256]{2,1,0:T(8,128)S(1)}, f32[16,256]{1,0:T(8,128)S(1)}, f32[16,256]{1,0:T(8,128)S(1)}) custom-call(s32[17]{0:T(128)S(1)} %get-tuple-element.21.first_ref, s32[17]{0:T(128)S(1)} %get-tuple-element.22.second_ref, s32[1]{0:T(128)} %bitcast.2.me_ref, f32[16,2,4,256]{3,2,1,0:T(4,128)S(1)} %reshape.23.own_ref, ...), custom_call_target="tpu_custom_call" | custom-call | flops 67108864 | bytes 2097152 | tf_op jit(solution)/shard_map/factors/pallas_call | solution.py:284
  120.0 3.3 %collective-permute-done.4.home_ref = f32[16,256]{1,0:T(8,128)S(1)} collective-permute-done((f32[16,256]{1,0:T(8,128)S(1)}, f32[16,256]{1,0:T(8,128)S(1)}, u32[]{:S(2)}, u32[]{:S(2)}) %collective-permute-start.4) | collective-permute-done | bytes 16416 | tf_op jit(solution)/shard_map/ppermute | solution.py:334
  123.3 1.4 %finish.1 = f32[16,16,256]{2,1,0:T(8,128)} custom-call(s32[16]{0:T(128)S(1)} %get-tuple-element.20.slot_ref, f32[16,16,256]{2,1,0:T(8,128)S(1)} %get-tuple-element.32.done_ref, f32[16,256]{1,0:T(8,128)S(1)} %collective-permute-done.4.home_ref, f32[16,256]{1,0:T(8,128)S(1)} %get-tuple-element.33.shift_ref, f32[16,256]{1,0:T(8,128)S(1)} %get-tuple-element.34.scale_ref), custom_call_target="tpu_custom_call" | custom-call | flops 262144 | bytes 1048576 | tf_op jit(solution)/shard_map/finish/pallas_call | solution.py:312
  (2 shorter events, 0.0 us)
Async XLA Ops:
  6.5 108.9 %reduce-scatter.2.cloned.1.call-start = ((), (), s32[]{:S(2)}) async-start(), calls=%async_computation.1 | async-start | bytes 4456448 | tf_op jit(solution)/shard_map/reduce_scatter | solution.py:343
  8.6 8.7 %copy-start = (s32[16,2]{0,1:T(2,128)S(1)}, s32[16,2]{0,1:T(2,128)}, u32[]{:S(2)}) copy-start(s32[16,2]{0,1:T(2,128)} %param.3) | copy-start | bytes 388
  8.6 18.4 %collective-permute-start.1 = (f32[256,1024]{1,0:T(8,128)}, f32[256,1024]{1,0:T(8,128)S(1)}, u32[]{:S(2)}, u32[]{:S(2)}) collective-permute-start(f32[256,1024]{1,0:T(8,128)} %border_for_a.1), channel_id=1, source_target_pairs={{16,32},{48,64},{80,96},{112,128},{144,160},{176,192},{208,224},{2... | collective-permute-start | bytes 3145736 | tf_op jit(solution)/shard_map/ppermute | solution.py:334
  15.3 11.9 %collective-permute-start = (f32[512,1024]{1,0:T(8,128)}, f32[512,1024]{1,0:T(8,128)S(1)}, u32[]{:S(2)}, u32[]{:S(2)}) collective-permute-start(f32[512,1024]{1,0:T(8,128)} %border_for_b.1), channel_id=1, source_target_pairs={{0,16},{32,48},{64,80},{96,112},{128,144},{160,176},{192,208},{224... | collective-permute-start | bytes 6291464 | tf_op jit(solution)/shard_map/ppermute | solution.py:334
  68.4 49.7 %collective-permute-start.3 = (f32[16,2,2,256]{3,2,1,0:T(2,128)S(1)}, f32[16,2,2,256]{3,2,1,0:T(2,128)S(1)}, u32[]{:S(2)}, u32[]{:S(2)}) collective-permute-start(f32[16,2,2,256]{3,2,1,0:T(2,128)S(1)} %get-tuple-element.35), channel_id=1, source_target_pairs={{16,0},{32,16},{48,32},{64,48},{80,64},{96,80},{112,96},{128,112},... | collective-permute-start | bytes 196616 | tf_op jit(solution)/shard_map/ppermute | solution.py:351
  70.3 47.8 %collective-permute-start.2 = (f32[16,2,2,256]{3,2,1,0:T(2,128)S(1)}, f32[16,2,2,256]{3,2,1,0:T(2,128)S(1)}, u32[]{:S(2)}, u32[]{:S(2)}) collective-permute-start(f32[16,2,2,256]{3,2,1,0:T(2,128)S(1)} %get-tuple-element.36), channel_id=1, source_target_pairs={{0,16},{16,32},{32,48},{48,64},{64,80},{80,96},{96,112},{112,128},... | collective-permute-start | bytes 196616 | tf_op jit(solution)/shard_map/ppermute | solution.py:350
  116.1 7.2 %collective-permute-start.4 = (f32[16,256]{1,0:T(8,128)S(1)}, f32[16,256]{1,0:T(8,128)S(1)}, u32[]{:S(2)}, u32[]{:S(2)}) collective-permute-start(f32[16,256]{1,0:T(8,128)S(1)} %slice.15), channel_id=1, source_target_pairs={{16,32},{48,64},{80,96},{112,128},{144,160},{176,192},{208,224},{2... | collective-permute-start | bytes 49160 | tf_op jit(solution)/shard_map/ppermute | solution.py:334
Sparse Core Ops, SparseCore 0:
  32.2 83.2 reduce-scatter.1
